TPU v7x, 128 devices: a whole 4x4x4 slice. The times are simulated.
128 devices in a mesh: ctx: 16 (over y, x), head: 8 (over z, core).
Axes of the slice: x: 4, y: 4, z: 4, core: 2. Of those that a mesh axis runs over, the one named last changes fastest.
Arguments:
- signal: bfloat16 [32768, 8192], P('ctx', 'head'), may hold values from -6 to 6
- log_decay: float32 [128, 32768], P('head', 'ctx'), may hold values from -0.61 to 0, as said below
- state_in: bfloat16 [32768, 1024], P(('ctx', 'head')), may hold values from -0.14941406 to 0.14941406
- state_out: bfloat16 [32768, 1024], P(('ctx', 'head')), may hold values from -0.14941406 to 0.14941406
- cotangent: bfloat16 [32768, 8192], P('ctx', 'head'), may hold values from -0.59765625 to 0.59765625
Outputs:
- output: bfloat16 [32768, 8192], P('ctx', 'head')
- grad_signal: bfloat16 [32768, 8192], P('ctx', 'head')
- grad_state_in: bfloat16 [32768, 1024], P(('ctx', 'head'))
- grad_state_out: bfloat16 [32768, 1024], P(('ctx', 'head'))
- grad_decay: float32 [128, 32768], P('head', 'ctx')
Inputs may be any that keep to these rules, and one draw needn't show every extreme that they name: `log_decay`: negative everywhere.
All inputs are finite; a program needn't handle non-finite values.
Results may differ from a plain program's by a relative error of at most 0.0064.
Values may be sent and summed in bfloat16 or wider, within the bound.
No kernel may reach another device: no remote copies, remote signals or barrier semaphores. Data moves between devices by JAX's collectives and lax.ppermute only.
A program may use at most 128 MiB of HBM per device.

v0:
```python
import jax
import jax.numpy as jnp
from jax import lax
from jax.sharding import PartitionSpec as P

HEAD_COUNT = 128
P_SIZE = 64
N = 128
G = 8
Q = 256


def entering(part, axis, combine, identity, reverse):
    count = lax.axis_size(axis)
    place = lax.axis_index(axis)
    ahead = count - 1 - place if reverse else place
    gathered = jax.tree.map(lambda a: lax.all_gather(a, axis), part)
    state = jax.tree.map(lambda a, e: jnp.zeros_like(a) + jnp.asarray(e, a.dtype), part, identity)

    def one(hop, state):
        source = count - 1 - hop if reverse else hop
        return combine(
            state, jax.tree.map(lambda a: lax.dynamic_index_in_dim(a, source, 0, False), gathered)
        )

    return lax.fori_loop(0, ahead, one, state)


def multiply(pattern, first_op, second_op):
    return jnp.einsum(pattern, first_op, second_op, preferred_element_type=jnp.float32)


def masked_exp(chosen, exponent):
    return jnp.where(chosen, jnp.exp(jnp.where(chosen, exponent, 0.0)), 0.0)


def block_mixing(in_rows, out_rows, cumulated):
    positions = jnp.arange(cumulated.shape[0], dtype=jnp.int32)
    below_mask = positions[:, None] >= positions[None, :]
    spread = jnp.transpose(cumulated, (1, 2, 0))
    damping = masked_exp(below_mask, spread[:, :, :, None] - spread[:, :, None, :])
    scores = multiply("tgn,sgn->gts", out_rows, in_rows)
    mixing = (scores[:, None] * damping).astype(jnp.bfloat16)
    return (below_mask, damping, mixing)


def first_pass(blocks):
    values, grads, in_rows, out_rows, cumulated, block_sum = blocks
    weights_end = jnp.exp(block_sum - cumulated)[..., None]
    weighted = (values.astype(jnp.float32) * weights_end).astype(jnp.bfloat16)
    end_states = multiply("sgjp,sgn->gjpn", weighted, in_rows)
    scaled = (grads.astype(jnp.float32) * jnp.exp(cumulated)[..., None]).astype(jnp.bfloat16)
    direct_adjoint = multiply("tgjp,tgn->gjpn", scaled, out_rows)
    return (end_states, direct_adjoint)


def finish(
    values,
    grads,
    in_rows,
    out_rows,
    cumulated,
    block_sum,
    intra_part,
    below_mask,
    damping,
    mixing,
    start_state,
    after_adjoint,
):
    starts_low = start_state.astype(jnp.bfloat16)
    after_low = after_adjoint.astype(jnp.bfloat16)
    weights_start = jnp.exp(cumulated)[..., None]
    weights_end = jnp.exp(block_sum - cumulated)[..., None]
    inter_part = weights_start * multiply("gjpn,tgn->tgjp", starts_low, out_rows)
    output = (intra_part + inter_part).astype(jnp.bfloat16)
    grad_mix = jnp.where(below_mask, multiply("tgjp,sgjp->gjts", grads, values), 0.0)
    grad_scores = jnp.sum(grad_mix * damping, axis=1).astype(jnp.bfloat16)
    back_term = multiply("gjpn,sgn->sgjp", after_low, in_rows)
    grad_values = (multiply("gjts,tgjp->sgjp", mixing, grads) + weights_end * back_term).astype(
        jnp.bfloat16
    )
    scaled = (grads.astype(jnp.float32) * weights_start).astype(jnp.bfloat16)
    weighted = (values.astype(jnp.float32) * weights_end).astype(jnp.bfloat16)
    grad_out_rows = (
        multiply("gts,sgn->tgn", grad_scores, in_rows)
        + multiply("tgjp,gjpn->tgn", scaled, starts_low)
    ).astype(jnp.bfloat16)
    grad_in_rows = (
        multiply("gts,tgn->sgn", grad_scores, out_rows)
        + multiply("sgjp,gjpn->sgn", weighted, after_low)
    ).astype(jnp.bfloat16)
    pair_terms = grad_mix * mixing.astype(jnp.float32)
    weight_grad = jnp.sum(values.astype(jnp.float32) * back_term, axis=-1) * weights_end[..., 0]
    cum_grad = jnp.transpose(jnp.sum(pair_terms, axis=3) - jnp.sum(pair_terms, axis=2), (2, 0, 1))
    cum_grad = cum_grad + jnp.sum(grads.astype(jnp.float32) * inter_part, axis=-1) - weight_grad
    total_grad = jnp.exp(block_sum) * jnp.sum(after_adjoint * start_state, axis=(2, 3)) + jnp.sum(
        weight_grad, axis=0
    )
    grad_decay = jnp.flip(jnp.cumsum(jnp.flip(cum_grad, 0), axis=0), 0) + total_grad
    return (output, grad_values, grad_in_rows, grad_out_rows, grad_decay)


def second_pass(blocks):
    values, grads, in_rows, out_rows, cumulated, block_sum, start_state, after_adjoint = blocks
    below_mask, damping, mixing = block_mixing(in_rows, out_rows, cumulated)
    intra_part = multiply("gjts,sgjp->tgjp", mixing, values)
    return finish(
        values,
        grads,
        in_rows,
        out_rows,
        cumulated,
        block_sum,
        intra_part,
        below_mask,
        damping,
        mixing,
        start_state,
        after_adjoint,
    )


def forward_step(current, element):
    end_state, decay_sum = element
    return (jnp.exp(decay_sum)[:, :, None, None] * current + end_state, current)


def backward_step(current, element):
    direct_state, decay_sum = element
    return (direct_state + jnp.exp(decay_sum)[:, :, None, None] * current, current)


def join_maps(earlier, later):
    return (earlier[0] + later[0], jnp.exp(later[0])[..., None, None] * earlier[1] + later[1])


def body(signal, log_decay, state_in, state_out, cotangent):
    in_local, out_local = (
        lax.all_to_all(state_in, "head", split_axis=1, concat_axis=0, tiled=True),
        lax.all_to_all(state_out, "head", split_axis=1, concat_axis=0, tiled=True),
    )
    tokens = signal.shape[0]
    block_count = tokens // Q
    per_group = HEAD_COUNT // G
    groups = in_local.shape[1] // N
    signal_blocks = signal.reshape(block_count, Q, groups, per_group, P_SIZE)
    grad_blocks = cotangent.reshape(block_count, Q, groups, per_group, P_SIZE)
    in_blocks = in_local.reshape(block_count, Q, groups, N)
    out_blocks = out_local.reshape(block_count, Q, groups, N)
    cum_decay = jnp.cumsum(log_decay.reshape(groups, per_group, block_count, Q), axis=-1)
    cum_decay = jnp.transpose(cum_decay, (2, 3, 0, 1))
    block_decay = cum_decay[:, -1]
    end_states, direct_adjoint = lax.map(
        first_pass, (signal_blocks, grad_blocks, in_blocks, out_blocks, cum_decay, block_decay)
    )
    zero_state = jnp.zeros((groups, per_group, P_SIZE, N), jnp.float32)
    local_end, local_starts = lax.scan(forward_step, zero_state, (end_states, block_decay))
    local_first, after_local = lax.scan(
        backward_step, zero_state, (direct_adjoint, block_decay), reverse=True
    )
    device_decay = jnp.sum(block_decay, axis=0)
    identity = (jnp.zeros_like(device_decay), zero_state)
    incoming = entering((device_decay, local_end), "ctx", join_maps, identity, False)[1]
    outgoing = entering((device_decay, local_first), "ctx", join_maps, identity, True)[1]
    running_sum = jnp.cumsum(block_decay, axis=0)
    prior_sum = running_sum - block_decay
    later_sum = device_decay - running_sum
    start_states = local_starts + jnp.exp(prior_sum)[..., None, None] * incoming
    after_adjoint = after_local + jnp.exp(later_sum)[..., None, None] * outgoing
    results = lax.map(
        second_pass,
        (
            signal_blocks,
            grad_blocks,
            in_blocks,
            out_blocks,
            cum_decay,
            block_decay,
            start_states,
            after_adjoint,
        ),
    )
    output, grad_values, grad_in_rows, grad_out_rows, grad_decay = results
    grad_in_rows = grad_in_rows.reshape(tokens, groups * N)
    grad_out_rows = grad_out_rows.reshape(tokens, groups * N)
    grad_in_rows, grad_out_rows = (
        lax.all_to_all(grad_in_rows, "head", split_axis=0, concat_axis=1, tiled=True),
        lax.all_to_all(grad_out_rows, "head", split_axis=0, concat_axis=1, tiled=True),
    )
    grad_decay = jnp.transpose(grad_decay, (2, 3, 0, 1)).reshape(groups * per_group, tokens)
    return (
        output.reshape(tokens, groups * per_group * P_SIZE),
        grad_values.reshape(tokens, groups * per_group * P_SIZE),
        grad_in_rows,
        grad_out_rows,
        grad_decay,
    )


def solution(mesh):
    in_specs = (
        P("ctx", "head"),
        P("head", "ctx"),
        P(("ctx", "head"), None),
        P(("ctx", "head"), None),
        P("ctx", "head"),
    )
    out_specs = (
        P("ctx", "head"),
        P("ctx", "head"),
        P(("ctx", "head"), None),
        P(("ctx", "head"), None),
        P("head", "ctx"),
    )
    return jax.shard_map(body, mesh=mesh, in_specs=in_specs, out_specs=out_specs, check_vma=False)
```

profile of v0, /device:TPU:31, one launch (start us, length us, event | category | flops | bytes accessed | tf_op | source)
XLA Modules:
  0.0 719.1 jit_solution(1070538983863243115)
XLA Ops:
  9.2 6.0 all-to-all-start
  16.2 9.0 %reduce-window.14 = f32[1,16,8,2,128]{4,2,3,1,0:T(8,128)S(1)} reduce-window(f32[1,16,8,2,128]{4,2,3,1,0:T(8,128)S(1)} %copy.67, f32[]{:T(128)} %constant.157.clone.1), window={size=1x1x1x1x128 pad=0_0x0_0x0_0x0_0x127_0}, to_apply=%region_0.0 | reduce-window | flops 4161536 | bytes 262148 | tf_op jit(solution)/shard_map/reduce-window.2
  27.7 4.8 all-to-all-start.1
  35.1 11.6 %reshape.589 = bf16[8,256,1,16,64]{4,3,1,0,2:T(8,128)(2,1)} reshape(bf16[2048,1024]{1,0:T(8,128)(2,1)} %param.21) | data formatting | bytes 8388608 | tf_op jit(solution)/shard_map/reshape | solution.py:148
  46.7 10.3 %copy.76 = bf16[8,256,1,16,64]{1,4,3,2,0:T(8,128)(2,1)} copy(bf16[8,256,1,16,64]{4,3,1,0,2:T(8,128)(2,1)} %reshape.589) | data formatting | bytes 8388608 | tf_op jit(solution)/shard_map/while | solution.py:154
  57.0 11.6 %reshape.588 = bf16[8,256,1,16,64]{4,3,1,0,2:T(8,128)(2,1)} reshape(bf16[2048,1024]{1,0:T(8,128)(2,1)} %param.17) | data formatting | bytes 8388608 | tf_op jit(solution)/shard_map/reshape | solution.py:147
  68.6 10.3 %copy.83 = bf16[8,256,1,16,64]{1,4,3,2,0:T(8,128)(2,1)} copy(bf16[8,256,1,16,64]{4,3,1,0,2:T(8,128)(2,1)} %reshape.588) | data formatting | bytes 8388608 | tf_op jit(solution)/shard_map/while | solution.py:171
  79.5 2.5 broadcast.167.clone.1
  84.6 47.4 %while.86 = (s32[]{:T(128)}, f32[8,1,16,64,128]{4,3,2,1,0:T(8,128)}, f32[8,1,16,64,128]{4,3,2,1,0:T(8,128)}, bf16[8,256,1,16,64]{1,4,3,2,0:T(8,128)(2,1)}, f32[8...) while((s32[]{:T(128)}, ...), condition=%wide.region_3.4_spmd, body=%wide.region_2.3_spmd.sunk | while | flops 135794688 | bytes 2346285 | solution.py:154
  134.5 21.4 %while.91 = (s32[]{:T(128)}, f32[1,16,64,128]{3,2,1,0:T(8,128)S(1)}, f32[8,1,16,64,128]{4,3,2,1,0:T(8,128)}, f32[8,1,16,64,128]{4,3,2,1,0:T(8,128)}, f32[8,1,16]...) while((s32[]{:T(128)}, f32[1,16,64,128]{3,2,1,0:T(8,128)S(1)}, ...), condition=%wide.region_11.12_spmd.clone, body=%wide.region_10.11_spmd.clone.sunk | while | flops 524292 | bytes 2621752 | solution.py:159
  156.7 2.5 broadcast.167.clone.3
  159.3 21.3 %while.90 = (s32[]{:T(128)}, f32[1,16,64,128]{3,2,1,0:T(8,128)S(1)}, f32[8,1,16,64,128]{4,3,2,1,0:T(8,128)}, f32[8,1,16]{2,1,0:T(1,128)}, f32[8,1,16,64,128]{4,3,2,1,0:T(8,128)}, /*index=5*/s32[]{:T(128)}, s32[]{:T(128)}) while((s32[]{:T(128)}, f32[1,16,64,128]{3,2,1,0:T(8,128)S(1)}, f32[8,1,16,64,128]{4,3,2,1,0:T(8,128)}, ...), condition=%wide.region_5.6_spmd.clone, body=%wide.region_4.5_spmd.clone.sunk | while | flops 524291 | bytes 2622240 | solution.py:158
  183.0 28.8 %all-reduce = f32[256]{0:T(256)S(1)} all-reduce(f32[256]{0:T(256)S(1)} %dynamic-update-slice), channel_id=2, replica_groups=mesh['ctx'=16,'head'=8] {'ctx'}, use_global_device_ids=true, to_apply=%add | all-reduce | flops 256 | bytes 2048
  213.3 13.7 %all-gather.8.cloned.1.call-done = f32[16,16,64,128]{3,2,1,0:T(8,128)} async-done(((f32[1,16,64,128]{3,2,1,0:T(8,128)}), f32[16,16,64,128]{3,2,1,0:T(8,128)}) %all-gather.8.cloned.1.call-update) | async-done | bytes 8388624 | tf_op jit(solution)/shard_map/all_gather | solution.py:17
  227.0 72.3 %all-gather.6.cloned.1.call-done = f32[16,16,64,128]{3,2,1,0:T(8,128)} async-done(((f32[1,16,64,128]{3,2,1,0:T(8,128)}), f32[16,16,64,128]{3,2,1,0:T(8,128)}) %all-gather.6.cloned.1.call-update) | async-done | bytes 8388624 | tf_op jit(solution)/shard_map/all_gather | solution.py:17
  299.4 18.7 %while.87 = (s32[]{:T(128)}, f32[1,16,64,128]{3,2,1,0:T(8,128)S(1)}, s32[]{:T(128)}, f32[16,1,16]{2,1,0:T(1,128)S(1)}, f32[16,1,16,64,128]{4,3,2,1,0:T(8,128)}, /*index=5*/s32[]{:T(128)}, s32[]{:T(128)}, s32[]{:T(128)}) while((s32[]{:T(128)}, f32[1,16,64,128]{3,2,1,0:T(8,128)S(1)}, s32[]{:T(128)}, f32[16,1,16]{2,1,0:T(1,128)S(1)}, ...), condition=%wide.region_9.10_spmd, body=%wide.region_8.9_spmd.sunk | while | flops 262149 | bytes 1573183 | solution.py:26
  318.1 7.7 %multiply_add_fusion = (f32[8,1,16,64,128]{4,3,2,1,0:T(8,128)}, f32[8,1,16,64,128]{4,3,2,1,0:T(8,128)}) fusion(f32[8,1,16,64,128]{4,3,2,1,0:T(8,128)} %get-tuple-element.394, f32[16,64,128]{2,1,0:T(8,128)S(1)} %bitcast.404, f32[8,16]{1,0:T(8,128)S(1)} %get-tuple-element.679, f32[8,1,16,64,128]{4,3,2,1,0:T(8,128)} %get-tuple-element.390, ...), kind=kLoop, calls=%fused_computation.142 | loop fusion | flops 4194304 | bytes 17826816 | tf_op jit(solution)/shard_map/add | solution.py:170
  325.8 319.3 %while.89 = (s32[]{:T(128)}, bf16[8,256,1,16,64]{1,4,3,2,0:T(8,128)(2,1)}, bf16[8,256,1,16,64]{1,4,3,2,0:T(8,128)(2,1)}, bf16[8,256,1,128]{1,3,2,0:T(8,128)(2,1)...) while((s32[]{:T(128)}, ...), condition=%wide.region_24.25_spmd, body=%wide.region_14.24_spmd.sunk | while | flops 750145664 | bytes 15791805 | solution.py:171
  332.0 3.6 fusion.164
  354.4 3.3 fusion.163
  357.7 3.4 fusion.162
  371.9 3.6 fusion.164
  394.4 3.3 fusion.163
  397.7 3.4 fusion.162
  411.9 3.6 fusion.164
  434.3 3.2 fusion.163
  437.5 3.4 fusion.162
  451.7 3.6 fusion.164
  474.1 3.2 fusion.163
  477.4 3.4 fusion.162
  491.6 3.6 fusion.164
  514.0 3.3 fusion.163
  517.3 3.4 fusion.162
  531.5 3.6 fusion.164
  554.0 3.2 fusion.163
  557.2 3.4 fusion.162
  571.5 3.6 fusion.164
  593.9 3.2 fusion.163
  597.1 3.4 fusion.162
  611.4 3.6 fusion.164
  633.8 3.2 fusion.163
  637.1 3.4 fusion.162
  645.0 14.5 %all_to_all.70 = bf16[8,256,128]{1,2,0:T(8,128)(2,1)S(1)} all-to-all(bf16[8,256,128]{1,2,0:T(8,128)(2,1)} %bitcast.415), channel_id=1, replica_groups=mesh['ctx'=16,'head'=8] {'head'}, dimensions={0} | all-to-all | bytes 1048576 | tf_op jit(solution)/shard_map/all_to_all | solution.py:188
  659.5 4.4 all-to-all-start.3
  663.9 10.9 %copy.96 = bf16[8,256,1,16,64]{4,3,1,0,2:T(8,128)(2,1)} copy(bf16[8,256,1,16,64]{1,4,3,2,0:T(8,128)(2,1)} %get-tuple-element.397) | data formatting | bytes 8388608
  674.8 11.9 %reshape.586 = bf16[2048,1024]{1,0:T(8,128)(2,1)} reshape(bf16[8,256,1,16,64]{4,3,1,0,2:T(8,128)(2,1)} %copy.96) | data formatting | bytes 8388608
  686.7 10.9 %copy.97 = bf16[8,256,1,16,64]{4,3,1,0,2:T(8,128)(2,1)} copy(bf16[8,256,1,16,64]{1,4,3,2,0:T(8,128)(2,1)} %get-tuple-element.398) | data formatting | bytes 8388608
  697.5 11.9 %reshape.587 = bf16[2048,1024]{1,0:T(8,128)(2,1)} reshape(bf16[8,256,1,16,64]{4,3,1,0,2:T(8,128)(2,1)} %copy.97) | data formatting | bytes 8388608
  (473 shorter events, 365.0 us)
Async XLA Ops:
  9.2 18.5 %all-to-all-start = ((bf16[256,8,128]{0,2,1:T(8,128)(2,1)}), bf16[256,8,128]{0,2,1:T(8,128)(2,1)S(1)}, u32[]{:S(2)}, u32[]{:S(2)}) async-start(bf16[256,8,128]{0,2,1:T(8,128)(2,1)} %bitcast.54), calls=%async_computation | async-start | bytes 1048576 | tf_op jit(solution)/shard_map/all_to_all | solution.py:141
  27.7 51.5 %all-to-all-start.1 = ((bf16[256,8,128]{0,2,1:T(8,128)(2,1)}), bf16[256,8,128]{0,2,1:T(8,128)(2,1)S(1)}, u32[]{:S(2)}, u32[]{:S(2)}) async-start(bf16[256,8,128]{0,2,1:T(8,128)(2,1)} %bitcast.57), calls=%async_computation.1 | async-start | bytes 1048576 | tf_op jit(solution)/shard_map/all_to_all | solution.py:140
  32.5 194.4 %all-gather.8.cloned.1.call-start = ((), (), s32[]{:S(2)}) async-start(), calls=%async_computation.5 | async-start | bytes 8912896 | tf_op jit(solution)/shard_map/all_gather | solution.py:17
  156.7 142.6 %all-gather.6.cloned.1.call-start = ((), (), s32[]{:S(2)}) async-start(), calls=%async_computation.4 | async-start | bytes 8912896 | tf_op jit(solution)/shard_map/all_gather | solution.py:17
  159.3 22.2 %copy-start.8 = (u32[128]{0:T(128)S(1)}, u32[128]{0:T(128)}, u32[]{:S(2)}) copy-start(u32[128]{0:T(128)} %constant.163) | copy-start | bytes 1540
  180.6 0.8 copy-start.1
  331.9 3.7 copy-start.5
  332.0 3.6 copy-start.3
  354.4 3.3 copy-start.4
  354.4 3.3 copy-start.6
  357.7 3.4 copy-start.2
  371.9 3.7 copy-start.5
  371.9 3.6 copy-start.3
  394.3 3.3 copy-start.4
  394.3 3.3 copy-start.6
  397.6 3.4 copy-start.2
  411.8 3.7 copy-start.5
  411.9 3.6 copy-start.3
  434.3 3.2 copy-start.4
  434.3 3.2 copy-start.6
  437.5 3.4 copy-start.2
  451.7 3.7 copy-start.5
  451.7 3.6 copy-start.3
  474.1 3.2 copy-start.4
  474.1 3.2 copy-start.6
  477.3 3.4 copy-start.2
  491.5 3.7 copy-start.5
  491.6 3.6 copy-start.3
  514.0 3.3 copy-start.4
  514.0 3.3 copy-start.6
  517.2 3.4 copy-start.2
  531.5 3.7 copy-start.5
  531.5 3.6 copy-start.3
  554.0 3.2 copy-start.4
  554.0 3.2 copy-start.6
  557.2 3.4 copy-start.2
  571.4 3.7 copy-start.5
  571.5 3.6 copy-start.3
  593.9 3.2 copy-start.4
  593.9 3.2 copy-start.6
  597.1 3.4 copy-start.2
  611.3 3.7 copy-start.5
  611.4 3.6 copy-start.3
  633.8 3.2 copy-start.4
  633.8 3.2 copy-start.6
  637.0 3.4 copy-start.2
  659.5 51.8 %all-to-all-start.3 = ((bf16[8,256,128]{1,2,0:T(8,128)(2,1)}), bf16[8,256,128]{1,2,0:T(8,128)(2,1)S(1)}, u32[]{:S(2)}, u32[]{:S(2)}) async-start(bf16[8,256,128]{1,2,0:T(8,128)(2,1)} %bitcast.416), calls=%async_computation.3 | async-start | bytes 1048576 | tf_op jit(solution)/shard_map/all_to_all | solution.py:189
  697.5 11.9 %copy-start.7 = (f32[8,256,1,16]{1,2,3,0:T(1,128)S(1)}, f32[8,256,1,16]{1,2,3,0:T(1,128)}, u32[]{:S(2)}) copy-start(f32[8,256,1,16]{1,2,3,0:T(1,128)} %get-tuple-element.401) | copy-start | bytes 393220
  (1 other events, 0.8 us)
Sparse Core Ops, SparseCore 0:
  156.8 70.0 all-gather.7
  229.1 70.1 all-gather.5
where the time goes:
time: 730 us; the launch traced here: 719 us
  local copies, waits for them, and re-layouts  226 us (31%)
  matrix products  178 us (24%)
  other arithmetic  153 us (21%)
  waiting for transfers between devices  86 us (12%)
  blocking collectives  43.3 us (6%)
  starting transfers between devices  15.3 us (2%)
  between operations  14.9 us (2%)
    dot_general x96, matrix products, multiply(): jnp.einsum(pattern, first_op, second_op, preferred_element_type=jnp.float32)  178 us
    all_gather x2, waiting for transfers between devices, entering(): gathered = jax.tree.map(lambda a: lax.all_gather(a, axis), part)  86 us
    unnamed x18, local copies, waits for them, and re-layouts  52.8 us
    another operation x42, local copies, waits for them, and re-layouts  44.5 us
    another operation x30, other arithmetic  39.2 us
    unnamed x1, blocking collectives  28.8 us
    add x15, other arithmetic, join_maps(): jnp.exp(later[0])[..., None, None] * earlier[1] + later[1]  17.8 us
    dynamic_slice x16, local copies, waits for them, and re-layouts, body(): lax.map(first_pass, (signal_blocks, grad_blocks, in_blocks, out_blocks, c...  14.8 us
  transfers between devices with their start and end apart: 5, of which 2 were waited for; matrix products, arithmetic and copies ran while one was open for 18% of the time, Pallas kernels for 0%

commit v1 on v0

v1 whole, which is shorter than its diff:
```python
import jax
import jax.numpy as jnp
from jax import lax
from jax.experimental import pallas as pl
from jax.experimental.pallas import tpu as pltpu
from jax.sharding import PartitionSpec as P

HEADS = 16
P_SIZE = 64
N = 128
C = 128
LANES = HEADS * P_SIZE
TOKENS = 2048
PIECES = TOKENS // C
ROW = 4
SLICE = LANES // ROW
MIB = 1 << 20

F32 = jnp.float32
BF16 = jnp.bfloat16


def dot(a, b):
    return lax.dot_general(a, b, (((1,), (0,)), ((), ())), preferred_element_type=F32)


def dot_nt(a, b):
    return lax.dot_general(a, b, (((1,), (1,)), ((), ())), preferred_element_type=F32)


def dot_tn(a, b):
    return lax.dot_general(a, b, (((0,), (0,)), ((), ())), preferred_element_type=F32)


def split2(a):
    high = a.astype(BF16)
    return high, (a - high.astype(F32)).astype(BF16)


def split3(a):
    high = a.astype(BF16)
    rest = a - high.astype(F32)
    return (high,) + split2(rest)


def iota(shape, dim):
    return lax.broadcasted_iota(jnp.int32, shape, dim)


def lane_heads(rows):
    return (iota((rows, LANES), 1) // P_SIZE) == (iota((rows, LANES), 0) % HEADS)


def one_hot(chosen):
    return jnp.where(chosen, 1.0, 0.0).astype(BF16)


TILES = 4
TILE = LANES // TILES


def tile(i):
    return slice(i * TILE, (i + 1) * TILE)


def piece_rows(j):
    return pl.ds(pl.multiple_of(j * C, C), C)


def scale_kernel(
    sig_hbm, cot_hbm, ld_ref, us_ref, vs_ref, g_ref, u2_ref, v2_ref, half_ref, ind_ref, sbuf, cbuf, ssem, csem
):
    slots = sbuf.shape[0]

    def reads(j):
        slot = lax.rem(j, slots)
        return (
            pltpu.make_async_copy(sig_hbm.at[piece_rows(j)], sbuf.at[slot], ssem.at[slot]),
            pltpu.make_async_copy(cot_hbm.at[piece_rows(j)], cbuf.at[slot], csem.at[slot]),
        )

    for j in range(slots):
        for copy in reads(j):
            copy.start()

    ind_ref[...] = one_hot(lane_heads(2 * HEADS))
    decay = jnp.concatenate([ld_ref[:, j * C : (j + 1) * C] for j in range(PIECES)], axis=0)
    upto = one_hot(iota((C, C), 0) <= iota((C, C), 1))
    cum = sum(dot(part, upto) for part in split3(decay))
    total = cum[:, C - 1 : C]
    u = jnp.exp(cum - 0.5 * total)
    v = jnp.exp(0.5 * total - cum)
    for ref, value in ((u2_ref, u), (v2_ref, v)):
        high, low = split2(value)
        for j in range(PIECES):
            rows = slice(j * HEADS, (j + 1) * HEADS)
            ref[j] = jnp.concatenate([high[rows], low[rows]], axis=0)
    chosen = lane_heads(HEADS)
    for j in range(PIECES):
        rows = slice(j * HEADS, (j + 1) * HEADS)
        spread = jnp.where(chosen, 0.5 * total[rows], 0.0)
        half_ref[j : j + 1, :] = jnp.sum(spread, axis=0, keepdims=True)

    def piece(j, carry):
        slot = lax.rem(j, slots)
        for copy in reads(j):
            copy.wait()
        u_rows, v_rows = u2_ref[j].T, v2_ref[j].T
        grad = jnp.zeros((C, C), F32)
        for i in range(TILES):
            us = (cbuf[slot, :, tile(i)].astype(F32) * dot(u_rows, ind_ref[:, tile(i)])).astype(BF16)
            vs = (sbuf[slot, :, tile(i)].astype(F32) * dot(v_rows, ind_ref[:, tile(i)])).astype(BF16)
            us_ref[piece_rows(j), tile(i)] = us
            vs_ref[piece_rows(j), tile(i)] = vs
            grad = grad + dot_nt(us, vs)
        g_ref[j] = jnp.where(iota((C, C), 0) >= iota((C, C), 1), grad, 0.0).astype(BF16)

        @pl.when(j + slots < PIECES)
        def _():
            for copy in reads(j + slots):
                copy.start()

        return carry

    lax.fori_loop(0, PIECES, piece, 0)


def log_rows(*logs):
    lanes = logs[0].shape[1]
    place = iota((16, lanes), 0)
    out = jnp.zeros((16, lanes), F32)
    for i, log in enumerate(logs):
        for k, part in enumerate(split3(log)):
            out = jnp.where(place == 3 * i + k, part.astype(F32), out)
    return out


def log_of(block, i=0):
    return jnp.sum(block[3 * i : 3 * i + 3, :], axis=0, keepdims=True)


def scaled(a):
    most = jnp.maximum(jnp.max(jnp.abs(a), axis=0, keepdims=True), 1e-30)
    return a * (1.0 / most), jnp.log(most)


def state_kernel(us_ref, vs_ref, r0, r1, r2, r3, other, half_ref, x_ref, local_ref, after_ref, msg_ref, xt_ref):
    z, core, homes = head_places()
    for d, ref in enumerate((r0, r1, r2, r3)):
        x_ref[2 * homes[d] + core] = ref[core]
        x_ref[2 * homes[d] + 1 - core] = other[d]
    for j in range(PIECES):
        rows = slice((j % 2) * C, (j % 2 + 1) * C)
        for i in range(2):
            xt_ref[i, :, j * C : (j + 1) * C] = x_ref[j // 2, i, rows, :].T
    me = lax.rem(lax.axis_index("ctx"), ROW)

    def part(d, carry):
        lanes = pl.ds(pl.multiple_of(lax.rem(me + d, ROW) * SLICE, SLICE), SLICE)
        state = jnp.zeros((N, SLICE), F32)
        adjoint = jnp.zeros((N, SLICE), F32)
        total = jnp.zeros((1, SLICE), F32)
        for i in range(PIECES):
            k = PIECES - 1 - i
            local_ref[i, :, lanes] = state.astype(BF16)
            half = half_ref[i : i + 1, lanes]
            weight = jnp.exp(half)
            end = dot(xt_ref[0, :, i * C : (i + 1) * C], vs_ref[i * C : (i + 1) * C, lanes])
            state = weight * (weight * state + end)
            total = total + 2.0 * half
            after_ref[k, :, lanes] = adjoint.astype(BF16)
            weight = jnp.exp(half_ref[k : k + 1, lanes])
            end = dot(xt_ref[1, :, k * C : (k + 1) * C], us_ref[k * C : (k + 1) * C, lanes])
            adjoint = weight * (weight * adjoint + end)
        local_ref[PIECES, :, lanes] = state.astype(BF16)
        msg_ref[d, 0:N, :], first = scaled(state)
        msg_ref[d, N : 2 * N, :], second = scaled(adjoint)
        msg_ref[d, 2 * N :, :] = log_rows(total, first, second)
        return carry

    lax.fori_loop(0, ROW, part, 0)


def between(logs, places, chosen):
    total = jnp.zeros_like(logs[0])
    for log, place in zip(logs, places):
        total = total + jnp.where(chosen(place), log, 0.0)
    return total


def pick(flag, log):
    return jnp.where(flag, jnp.exp(log), 0.0)


def head_places():
    index = lax.axis_index("head")
    z, core = lax.div(index, 2), lax.rem(index, 2)
    return z, core, [lax.rem(z + ROW - d, ROW) for d in range(ROW)]


def own_places():
    index = lax.axis_index("ctx")
    x, y = lax.rem(index, ROW), lax.div(index, ROW)
    return x, y, [lax.rem(x + ROW - d, ROW) for d in range(ROW)]


def row_kernel(r0, r1, r2, r3, out_ref):
    x, y, places = own_places()
    refs = (r0, r1, r2, r3)
    ends = [r[2 * N :, :] for r in refs]
    logs = [log_of(end) for end in ends]
    state = jnp.zeros((N, SLICE), F32)
    adjoint = jnp.zeros((N, SLICE), F32)
    for ref, end, own in zip(refs, ends, places):
        state += jnp.exp(between(logs, places, lambda p: p > own) + log_of(end, 1)) * ref[0:N, :]
        adjoint += jnp.exp(between(logs, places, lambda p: p < own) + log_of(end, 2)) * ref[N : 2 * N, :]
    for d in range(1, ROW):
        out_ref[d - 1, 0:N, :], most = scaled(jnp.where(y + d < ROW, state, adjoint))
        out_ref[d - 1, N:, :] = log_rows(sum(logs), most)


def enter_kernel(r0, r1, r2, r3, q1, q2, q3, out_ref):
    x, y, places = own_places()
    refs, rows = (r0, r1, r2, r3), (q1, q2, q3)
    ends = [r[2 * N :, :] for r in refs]
    logs = [log_of(end) for end in ends]
    row_ends = [r[N:, :] for r in rows]
    row_logs = [log_of(end) for end in row_ends]
    row_places = [lax.rem(y + ROW - d, ROW) for d in range(1, ROW)]
    state = jnp.zeros((N, SLICE), F32)
    adjoint = jnp.zeros((N, SLICE), F32)
    for ref, end, own in zip(rows, row_ends, row_places):
        block = ref[0:N, :]
        before = between(row_logs, row_places, lambda p: (p > own) & (p < y)) + log_of(end, 1)
        behind = between(row_logs, row_places, lambda p: (p < own) & (p > y)) + log_of(end, 1)
        state += pick(own < y, before) * block
        adjoint += pick(own > y, behind) * block
    for e in range(ROW):
        to = lax.rem(x + e, ROW)
        first = jnp.exp(between(logs, places, lambda p: p < to)) * state
        second = jnp.exp(between(logs, places, lambda p: p > to)) * adjoint
        for ref, end, own in zip(refs, ends, places):
            before = between(logs, places, lambda p: (p > own) & (p < to)) + log_of(end, 1)
            behind = between(logs, places, lambda p: (p < own) & (p > to)) + log_of(end, 2)
            first += pick(own < to, before) * ref[0:N, :]
            second += pick(own > to, behind) * ref[N : 2 * N, :]
        out_ref[e, 0:N, :], first_log = scaled(first)
        out_ref[e, N : 2 * N, :], second_log = scaled(second)
        out_ref[e, 2 * N :, :] = log_rows(first_log, second_log)


def projection_kernel(
    us_ref,
    vs_ref,
    x_ref,
    g_ref,
    half_ref,
    local_ref,
    after_ref,
    s0,
    s1,
    s2,
    s3,
    grad_ref,
    start_ref,
    behind_ref,
    total_ref,
    enter_ref,
    last_ref,
):
    z, core, homes = head_places()
    x, y, places = own_places()
    for ref, place in zip((s0, s1, s2, s3), places):
        lanes = pl.ds(pl.multiple_of(place * SLICE, SLICE), SLICE)
        end = ref[2 * N :, :]
        enter_ref[0, :, lanes] = jnp.exp(log_of(end, 0)) * ref[0:N, :]
        enter_ref[1, :, lanes] = jnp.exp(log_of(end, 1)) * ref[N : 2 * N, :]
    later = jnp.zeros((1, LANES), F32)
    laters = [None] * PIECES
    for j in reversed(range(PIECES)):
        laters[j] = later
        later = later + 2.0 * half_ref[j : j + 1, :]

    prior = jnp.zeros((1, LANES), F32)
    for j in range(PIECES + 1):
        first = local_ref[j].astype(F32) + jnp.exp(prior) * enter_ref[0]
        if j > 0:
            total_ref[j - 1 : j, :] = jnp.sum(first * last_ref[...], axis=0, keepdims=True)
        if j == PIECES:
            break
        rows = slice(j * C, (j + 1) * C)
        half = half_ref[j : j + 1, :]
        prior = prior + 2.0 * half
        weight = jnp.exp(half)
        part = slice((j % 2) * C, (j % 2 + 1) * C)
        start = (weight * first).astype(BF16)
        start_ref[j] = start
        to = (lax.rem(j // 4 + ROW - z, ROW), j // 2 % 2)
        grad_ref[*to, 1, part, :] = (dot(g_ref[j], x_ref[j // 2, 0, part, :]) + dot_nt(us_ref[rows], start)).astype(BF16)
        second = after_ref[j].astype(F32) + jnp.exp(laters[j]) * enter_ref[1]
        last_ref[...] = second
        behind = (weight * second).astype(BF16)
        behind_ref[j] = behind
        grad_ref[*to, 0, part, :] = (dot_tn(g_ref[j], x_ref[j // 2, 1, part, :]) + dot_nt(vs_ref[rows], behind)).astype(BF16)


def result_kernel(
    us_ref,
    vs_ref,
    start_ref,
    behind_ref,
    x_ref,
    u2_ref,
    v2_ref,
    total_ref,
    out_hbm,
    grad_hbm,
    decay_ref,
    obuf,
    gbuf,
    ind_ref,
    of_ref,
    heads_ref,
    osem,
    gsem,
):
    outs = obuf.shape[0]

    def writes(j):
        slot = lax.rem(j, outs)
        return (
            pltpu.make_async_copy(obuf.at[slot], out_hbm.at[piece_rows(j)], osem.at[slot]),
            pltpu.make_async_copy(gbuf.at[slot], grad_hbm.at[piece_rows(j)], gsem.at[slot]),
        )

    ind_ref[...] = one_hot(lane_heads(2 * HEADS))
    own = ind_ref[0:HEADS, :]
    of_ref[...] = one_hot(iota((LANES, C), 0) // P_SIZE == iota((LANES, C), 1))
    heads_ref[...] = sum(dot_nt(own, part) for part in split3(total_ref[...]))
    lower = iota((C, C), 0) >= iota((C, C), 1)
    upper = iota((C, C), 0) <= iota((C, C), 1)
    from_on = one_hot(lower)

    def piece(j, carry):
        place = lax.rem(j, outs)
        part = pl.ds(pl.multiple_of(lax.rem(j, 2) * C, C), C)
        block = lax.div(j, 2)
        x_in, x_out = x_ref[block, 0, part, :], x_ref[block, 1, part, :]
        scores = jnp.where(lower, dot_nt(x_out, x_in), 0.0).astype(BF16)
        turned = jnp.where(upper, dot_nt(x_in, x_out), 0.0).astype(BF16)
        u_rows, v_rows = u2_ref[j].T, v2_ref[j].T
        left_out = jnp.concatenate([scores, x_out], axis=1)
        left_grad = jnp.concatenate([turned, x_in], axis=1)

        @pl.when(j >= outs)
        def _():
            for copy in writes(j - outs):
                copy.wait()

        total = jnp.sum(jnp.where(iota((HEADS, PIECES), 1) == j, heads_ref[...], 0.0), axis=1, keepdims=True)
        cum_grad = jnp.zeros((C, C), F32)
        for i in range(TILES):
            us, vs = us_ref[piece_rows(j), tile(i)], vs_ref[piece_rows(j), tile(i)]
            out = dot(left_out, jnp.concatenate([vs, start_ref[j, :, tile(i)]], axis=0))
            obuf[place, :, tile(i)] = (out * dot(u_rows, ind_ref[:, tile(i)])).astype(BF16)
            grad = dot(left_grad, jnp.concatenate([us, behind_ref[j, :, tile(i)]], axis=0))
            gbuf[place, :, tile(i)] = (grad * dot(v_rows, ind_ref[:, tile(i)])).astype(BF16)
            diff = us.astype(F32) * out - vs.astype(F32) * grad
            cum_grad = cum_grad + dot(diff.astype(BF16), of_ref[tile(i), :])
        for copy in writes(j):
            copy.start()
        cum_grad = cum_grad.T[0:HEADS] + jnp.where(iota((HEADS, C), 1) == C - 1, total, 0.0)
        sums = dot(jnp.concatenate(split3(cum_grad), axis=0), from_on)
        decay_ref[:, piece_rows(j)] = sums[0:HEADS] + sums[HEADS : 2 * HEADS] + sums[2 * HEADS :]
        return carry

    lax.fori_loop(0, PIECES, piece, 0)
    for j in range(PIECES - outs, PIECES):
        for copy in writes(j):
            copy.wait()


def split_kernel(in_ref, out_ref, *sent):
    z, core, homes = head_places()
    for d, ref in enumerate(sent):
        for to in range(2):
            group = 2 * lax.rem(z + d, ROW) + to
            columns = pl.ds(pl.multiple_of(group * N, N), N)
            ref[to, 0] = in_ref[:, columns]
            ref[to, 1] = out_ref[:, columns]


def swap_kernel(r0, r1, r2, r3, after_hbm, other_ref):
    z, core, homes = head_places()
    for d, ref in enumerate((r0, r1, r2, r3)):
        other_ref[d] = ref[1 - core]


def join_kernel(r0, r1, r2, r3, other, in_ref, out_ref):
    z, core, homes = head_places()
    for d, ref in enumerate((r0, r1, r2, r3)):
        columns = pl.ds(pl.multiple_of((2 * homes[d] + core) * N, N), N)
        in_ref[:, columns] = ref[core, 0]
        out_ref[:, columns] = ref[core, 1]
        columns = pl.ds(pl.multiple_of((2 * homes[d] + 1 - core) * N, N), N)
        in_ref[:, columns] = other[d, 0]
        out_ref[:, columns] = other[d, 1]


VMEM = pl.BlockSpec(memory_space=pltpu.VMEM)
HBM = pl.BlockSpec(memory_space=pltpu.HBM)
DMA = pltpu.SemaphoreType.DMA


def call(kernel, args, outs, specs, out_specs, scratch=(), limit=10, flops=0, moved=0):
    return pl.pallas_call(
        kernel,
        out_shape=outs,
        in_specs=specs,
        out_specs=out_specs,
        scratch_shapes=list(scratch),
        compiler_params=pltpu.CompilerParams(vmem_limit_bytes=limit * MIB),
        cost_estimate=pl.CostEstimate(flops=flops, bytes_accessed=moved, transcendentals=0),
    )(*args)


def held(shape, dtype=BF16):
    return pltpu.VMEM(shape, dtype)


def far(a):
    return pltpu.with_memory_space_constraint(a, pltpu.HBM)


def kept(shape, dtype=BF16):
    return pltpu.HBM(shape, dtype)


def plain(shape, dtype=BF16):
    return jax.ShapeDtypeStruct(shape, dtype)


def along_x(d):
    return [(y * ROW + x, y * ROW + (x + d) % ROW) for y in range(ROW) for x in range(ROW)]


def along_y(d):
    return [(y * ROW + x, (y + d) % ROW * ROW + x) for y in range(ROW) for x in range(ROW)]


def along_z(d):
    return [(z * 2 + c, (z + d) % ROW * 2 + c) for z in range(ROW) for c in range(2)]


def send(a, pairs):
    return lax.ppermute(a.astype(jnp.float16), "ctx", pairs).astype(F32)


OTHER_CORE = [(i, i ^ 1) for i in range(2 * ROW)]


def body(signal, log_decay, state_in, state_out, cotangent):
    own = state_in.shape[0]
    chip = (2, 2, own, N)
    blocks = (2 * ROW, 2, own, N)
    wide = (TOKENS, LANES)
    states = (PIECES, N, LANES)
    band = (C, LANES)

    sent = call(split_kernel, (state_in, state_out), [held(chip)] * ROW, [VMEM] * 2, [VMEM] * ROW)
    got = [sent[0]] + [lax.ppermute(sent[d], "head", along_z(d)) for d in (1, 3, 2)]
    got = [got[0], got[1], got[3], got[2]]
    us, vs, g, u2, v2, half = call(
        scale_kernel,
        (far(signal), far(cotangent), log_decay),
        (
            held(wide),
            held(wide),
            held((PIECES, C, C)),
            held((PIECES, 2 * HEADS, C)),
            held((PIECES, 2 * HEADS, C)),
            held((PIECES, LANES), F32),
        ),
        [HBM, HBM, VMEM],
        [VMEM] * 6,
        [pltpu.VMEM((2 * HEADS, LANES), BF16)] + [pltpu.VMEM((4,) + band, BF16)] * 2 + [DMA((4,))] * 2,
        flops=1 << 33,
        moved=1 << 23,
    )
    other = call(swap_kernel, got + [half], held((ROW, 2, own, N)), [VMEM] * 5, VMEM)
    other = lax.ppermute(other, "head", OTHER_CORE)
    x, local, after, msg = call(
        state_kernel,
        [us, vs] + got + [other, half],
        (held(blocks), held((PIECES + 1, N, LANES)), held(states), held((ROW, 2 * N + 16, SLICE), F32)),
        [VMEM] * 8,
        [VMEM] * 4,
        [pltpu.VMEM((2, N, TOKENS), BF16)],
    )
    mates = [msg[0]] + [send(msg[d], along_x(d)) for d in range(1, ROW)]
    totals = call(row_kernel, mates, held((ROW - 1, N + 16, SLICE), F32), [VMEM] * 4, VMEM)
    rows = [send(totals[d - 1], along_y(d)) for d in range(1, ROW)]
    back = call(enter_kernel, mates + rows, held((ROW, 2 * N + 16, SLICE), F32), [VMEM] * 7, VMEM)
    shares = [back[0]] + [send(back[e], along_x(e)) for e in range(1, ROW)]
    grads, start, behind, total = call(
        projection_kernel,
        [us, vs, x, g, half, local, after] + shares,
        (held((ROW,) + chip), held(states), held(states), held((PIECES, LANES), F32)),
        [VMEM] * 11,
        [VMEM] * 4,
        [pltpu.VMEM((2,) + band, F32), pltpu.VMEM(band, F32)],
    )
    returned = [grads[0]] + [lax.ppermute(grads[d], "head", along_z(d)) for d in (1, 3, 2)]
    returned = [returned[0], returned[1], returned[3], returned[2]]
    output, grad_signal, grad_decay = call(
        result_kernel,
        (us, vs, start, behind, x, u2, v2, total),
        (plain(wide), plain(wide), plain((HEADS, TOKENS), F32)),
        [VMEM] * 8,
        [HBM, HBM, VMEM],
        [pltpu.VMEM((2,) + band, BF16)] * 2
        + [pltpu.VMEM((2 * HEADS, LANES), BF16), pltpu.VMEM((LANES, C), BF16), pltpu.VMEM((HEADS, PIECES), F32)]
        + [DMA((2,)), DMA((2,))],
        flops=1 << 34,
        moved=1 << 23,
    )
    other = call(swap_kernel, returned + [far(grad_decay)], held((ROW, 2, own, N)), [VMEM] * ROW + [HBM], VMEM)
    other = lax.ppermute(other, "head", OTHER_CORE)
    narrow = plain(state_in.shape)
    grad_in, grad_out = call(join_kernel, returned + [other], (narrow, narrow), [VMEM] * 5, [VMEM] * 2)
    return output, grad_signal, grad_in, grad_out, grad_decay


def solution(mesh):
    in_specs = (
        P("ctx", "head"),
        P("head", "ctx"),
        P(("ctx", "head"), None),
        P(("ctx", "head"), None),
        P("ctx", "head"),
    )
    out_specs = (
        P("ctx", "head"),
        P("ctx", "head"),
        P(("ctx", "head"), None),
        P(("ctx", "head"), None),
        P("head", "ctx"),
    )
    return jax.shard_map(body, mesh=mesh, in_specs=in_specs, out_specs=out_specs, check_vma=False)
```

time: 730 us -> 91.9 us (0.13)
  the two profiles are of different devices: /device:TPU:31 before, /device:TPU:1 now
where the time goes in v1:
time: 91.9 us; the launch traced here: 91.7 us
  Pallas kernels  40 us (44%)
  waiting for transfers between devices  25.7 us (28%)
  starting transfers between devices  21.4 us (23%)
  local copies, waits for them, and re-layouts  3.32 us (4%)
    pallas_call x10, Pallas kernels, call(): pl.pallas_call(kernel, out_shape=outs, in_specs=specs, out_specs=out_spec...  40 us
    ppermute x9, waiting for transfers between devices, send(): return lax.ppermute(a.astype(jnp.float16), 'ctx', pairs).astype(F32)  22.7 us
    ppermute x9, starting transfers between devices, send(): return lax.ppermute(a.astype(jnp.float16), 'ctx', pairs).astype(F32)  9.02 us
    ppermute x3, starting transfers between devices, body(): lax.ppermute(sent[d], 'head', along_z(d))  6.57 us
    ppermute x2, starting transfers between devices, body(): other = lax.ppermute(other, 'head', OTHER_CORE)  3.22 us
    ppermute x2, waiting for transfers between devices, body(): other = lax.ppermute(other, 'head', OTHER_CORE)  3.07 us
    unnamed x6, local copies, waits for them, and re-layouts  2.98 us
    ppermute x3, starting transfers between devices, body(): lax.ppermute(grads[d], 'head', along_z(d))  2.58 us
  transfers between devices with their start and end apart: 17, of which 11 were waited for; matrix products, arithmetic and copies ran while one was open for 0% of the time, Pallas kernels for 32%

profile of v1, /device:TPU:1, one launch (start us, length us, event | category | flops | bytes accessed | tf_op | source)
XLA Modules:
  0.0 91.7 jit_solution(17013347930477891745)
XLA Ops:
  0.6 1.0 %copy-done = bf16[256,1024]{1,0:T(8,128)(2,1)S(1)} copy-done((bf16[256,1024]{1,0:T(8,128)(2,1)S(1)}, bf16[256,1024]{1,0:T(8,128)(2,1)}, u32[]{:S(2)}) %copy-start) | copy-done | bytes 524312
  1.7 1.0 %copy-done.1 = bf16[256,1024]{1,0:T(8,128)(2,1)S(1)} copy-done((bf16[256,1024]{1,0:T(8,128)(2,1)S(1)}, bf16[256,1024]{1,0:T(8,128)(2,1)}, u32[]{:S(2)}) %copy-start.1) | copy-done | bytes 524312
  2.7 0.3 shard_map.93
  3.0 2.5 %collective-permute-start = (bf16[2,2,256,128]{3,2,1,0:T(8,128)(2,1)S(1)}, bf16[2,2,256,128]{3,2,1,0:T(8,128)(2,1)S(1)}, u32[]{:S(2)}, u32[]{:S(2)}) collective-permute-start(bf16[2,2,256,128]{3,2,1,0:T(8,128)(2,1)S(1)} %get-tuple-element.31), channel_id=1, source_target_pairs={{0,2},{1,3},{2,4},{3,5},{4,6},{5,7},{6,0},{7,1},{8,10},{9,11},{10,... | collective-permute-start | bytes 786440 | tf_op jit(solution)/shard_map/ppermute | solution.py:471
  5.5 3.3 %collective-permute-start.1 = (bf16[2,2,256,128]{3,2,1,0:T(8,128)(2,1)S(1)}, bf16[2,2,256,128]{3,2,1,0:T(8,128)(2,1)S(1)}, u32[]{:S(2)}, u32[]{:S(2)}) collective-permute-start(bf16[2,2,256,128]{3,2,1,0:T(8,128)(2,1)S(1)} %get-tuple-element.32), channel_id=1, source_target_pairs={{0,4},{1,5},{2,6},{3,7},{4,0},{5,1},{6,2},{7,3},{8,12},{9,13},{10,... | collective-permute-start | bytes 786440 | tf_op jit(solution)/shard_map/ppermute | solution.py:471
  8.8 0.7 collective-permute-start.2
  9.6 0.9 copy-done.2
  10.5 12.2 %shard_map.92 = (bf16[2048,1024]{1,0:T(8,128)(2,1)S(1)}, bf16[2048,1024]{1,0:T(8,128)(2,1)S(1)}, bf16[16,128,128]{2,1,0:T(8,128)(2,1)S(1)}, bf16[16,32,128]{2,1,...) custom-call(bf16[2048,1024]{1,0:T(8,128)(2,1)} %sig_hbm.1, bf16[2048,1024]{1,0:T(8,128)(2,1)} %cot_hbm.1, ...), custom_call_target="tpu_custom_call" | custom-call | flops 8589934592 | bytes 8388608 | tf_op jit(solution)/shard_map/pallas_call | solution.py:416
  22.7 0.0 collective-permute-done.r1
  22.7 0.0 collective-permute-done.1.r2
  22.8 1.6 %collective-permute-start.3 = (bf16[4,2,256,128]{3,2,1,0:T(8,128)(2,1)S(1)}, bf16[4,2,256,128]{3,2,1,0:T(8,128)(2,1)S(1)}, u32[]{:S(2)}, u32[]{:S(2)}) collective-permute-start(bf16[4,2,256,128]{3,2,1,0:T(8,128)(2,1)S(1)} %shard_map.94), channel_id=1, source_target_pairs={{0,1},{1,0},{2,3},{3,2},{4,5},{5,4},{6,7},{7,6},{8,9},{9,8},{10,11... | collective-permute-start | bytes 1572872 | tf_op jit(solution)/shard_map/ppermute | solution.py:491
  24.4 1.5 %collective-permute-done.3.other = bf16[4,2,256,128]{3,2,1,0:T(8,128)(2,1)S(1)} collective-permute-done((bf16[4,2,256,128]{3,2,1,0:T(8,128)(2,1)S(1)}, bf16[4,2,256,128]{3,2,1,0:T(8,128)(2,1)S(1)}, u32[]{:S(2)}, u32[]{:S(2)}) %collective-permute-start.3) | collective-permute-done | bytes 524320 | tf_op jit(solution)/shard_map/ppermute | solution.py:491
  25.9 4.1 %shard_map.95 = (bf16[8,2,256,128]{3,2,1,0:T(8,128)(2,1)S(1)}, bf16[17,128,1024]{2,1,0:T(8,128)(2,1)S(1)}, bf16[16,128,1024]{2,1,0:T(8,128)(2,1)S(1)}, f32[4,272,256]{2,1,0:T(8,128)S(1)}) custom-call(bf16[2048,1024]{1,0:T(8,128)(2,1)S(1)} %get-tuple-element.28.us_ref, bf16[2048,1024]{1,0:T(8,128)(2,1)S(1)} %get-tuple-element.29.vs_ref, ...), custom_call_target="tpu_custom_call" | custom-call | tf_op jit(solution)/shard_map/pallas_call | solution.py:416
  30.0 0.1 convert.15
  30.1 0.1 slice_bitcast_fusion.9
  30.2 2.6 %collective-permute-start.6 = (f16[272,256]{1,0:T(8,128)(2,1)S(1)}, f16[272,256]{1,0:T(8,128)(2,1)S(1)}, u32[]{:S(2)}, u32[]{:S(2)}) collective-permute-start(f16[272,256]{1,0:T(8,128)(2,1)S(1)} %get-tuple-element.58), channel_id=1, source_target_pairs={{0,24},{8,0},{16,8},{24,16},{32,56},{40,32},{48,40},{56,48},{64,88... | collective-permute-start | bytes 417800 | tf_op jit(solution)/shard_map/ppermute | solution.py:456
  32.7 0.5 collective-permute-start.5
  33.2 0.6 collective-permute-start.4
  33.9 4.4 %collective-permute-done.6 = f16[272,256]{1,0:T(8,128)(2,1)S(1)} collective-permute-done((f16[272,256]{1,0:T(8,128)(2,1)S(1)}, f16[272,256]{1,0:T(8,128)(2,1)S(1)}, u32[]{:S(2)}, u32[]{:S(2)}) %collective-permute-start.6) | collective-permute-done | bytes 139296 | tf_op jit(solution)/shard_map/ppermute | solution.py:456
  38.3 0.5 collective-permute-done.5
  38.9 4.0 %collective-permute-done.4 = f16[272,256]{1,0:T(8,128)(2,1)S(1)} collective-permute-done((f16[272,256]{1,0:T(8,128)(2,1)S(1)}, f16[272,256]{1,0:T(8,128)(2,1)S(1)}, u32[]{:S(2)}, u32[]{:S(2)}) %collective-permute-start.4) | collective-permute-done | bytes 139296 | tf_op jit(solution)/shard_map/ppermute | solution.py:456
  42.8 0.2 shard_map.96
  43.1 2.8 %collective-permute-start.9 = (f16[144,256]{1,0:T(8,128)(2,1)S(1)}, f16[144,256]{1,0:T(8,128)(2,1)S(1)}, u32[]{:S(2)}, u32[]{:S(2)}) collective-permute-start(f16[144,256]{1,0:T(8,128)(2,1)S(1)} %get-tuple-element.61), channel_id=1, source_target_pairs={{0,96},{8,104},{16,112},{24,120},{32,0},{40,8},{48,16},{56,24},{64... | collective-permute-start | bytes 221192 | tf_op jit(solution)/shard_map/ppermute | solution.py:456
  45.9 0.3 collective-permute-start.8
  46.2 0.7 collective-permute-start.7
  46.9 0.4 collective-permute-done.9
  47.3 3.4 %collective-permute-done.8 = f16[144,256]{1,0:T(8,128)(2,1)S(1)} collective-permute-done((f16[144,256]{1,0:T(8,128)(2,1)S(1)}, f16[144,256]{1,0:T(8,128)(2,1)S(1)}, u32[]{:S(2)}, u32[]{:S(2)}) %collective-permute-start.8) | collective-permute-done | bytes 73760 | tf_op jit(solution)/shard_map/ppermute | solution.py:456
  50.7 1.9 %collective-permute-done.7 = f16[144,256]{1,0:T(8,128)(2,1)S(1)} collective-permute-done((f16[144,256]{1,0:T(8,128)(2,1)S(1)}, f16[144,256]{1,0:T(8,128)(2,1)S(1)}, u32[]{:S(2)}, u32[]{:S(2)}) %collective-permute-start.7) | collective-permute-done | bytes 73760 | tf_op jit(solution)/shard_map/ppermute | solution.py:456
  52.6 0.7 shard_map.97
  53.3 0.1 convert.17
  53.4 0.1 slice_bitcast_fusion.6
  53.5 0.1 collective-permute-start.12
  53.6 0.1 collective-permute-start.11
  53.6 1.4 %collective-permute-start.10 = (f16[272,256]{1,0:T(8,128)(2,1)S(1)}, f16[272,256]{1,0:T(8,128)(2,1)S(1)}, u32[]{:S(2)}, u32[]{:S(2)}) collective-permute-start(f16[272,256]{1,0:T(8,128)(2,1)S(1)} %get-tuple-element.57), channel_id=1, source_target_pairs={{0,8},{8,16},{16,24},{24,0},{32,40},{40,48},{48,56},{56,32},{64,72... | collective-permute-start | bytes 417800 | tf_op jit(solution)/shard_map/ppermute | solution.py:456
  55.0 2.4 %collective-permute-done.12 = f16[272,256]{1,0:T(8,128)(2,1)S(1)} collective-permute-done((f16[272,256]{1,0:T(8,128)(2,1)S(1)}, f16[272,256]{1,0:T(8,128)(2,1)S(1)}, u32[]{:S(2)}, u32[]{:S(2)}) %collective-permute-start.12) | collective-permute-done | bytes 139296 | tf_op jit(solution)/shard_map/ppermute | solution.py:456
  57.5 1.6 %collective-permute-done.11 = f16[272,256]{1,0:T(8,128)(2,1)S(1)} collective-permute-done((f16[272,256]{1,0:T(8,128)(2,1)S(1)}, f16[272,256]{1,0:T(8,128)(2,1)S(1)}, u32[]{:S(2)}, u32[]{:S(2)}) %collective-permute-start.11) | collective-permute-done | bytes 139296 | tf_op jit(solution)/shard_map/ppermute | solution.py:456
  59.1 4.1 %collective-permute-done.10 = f16[272,256]{1,0:T(8,128)(2,1)S(1)} collective-permute-done((f16[272,256]{1,0:T(8,128)(2,1)S(1)}, f16[272,256]{1,0:T(8,128)(2,1)S(1)}, u32[]{:S(2)}, u32[]{:S(2)}) %collective-permute-start.10) | collective-permute-done | bytes 139296 | tf_op jit(solution)/shard_map/ppermute | solution.py:456
  63.3 4.4 %shard_map.98 = (bf16[4,2,2,256,128]{4,3,2,1,0:T(8,128)(2,1)S(1)}, bf16[16,128,1024]{2,1,0:T(8,128)(2,1)S(1)}, bf16[16,128,1024]{2,1,0:T(8,128)(2,1)S(1)}, f32[16,1024]{1,0:T(8,128)S(1)}) custom-call(bf16[2048,1024]{1,0:T(8,128)(2,1)S(1)} %get-tuple-element.28.us_ref, bf16[2048,1024]{1,0:T(8,128)(2,1)S(1)} %get-tuple-element.29.vs_ref, ...), custom_call_target="tpu_custom_call" | custom-call | tf_op jit(solution)/shard_map/pallas_call | solution.py:416
  67.6 0.1 slice_bitcast_fusion.2
  67.7 0.1 collective-permute-start.15
  67.8 2.5 %collective-permute-start.14 = (bf16[2,2,256,128]{3,2,1,0:T(8,128)(2,1)S(1)}, bf16[2,2,256,128]{3,2,1,0:T(8,128)(2,1)S(1)}, u32[]{:S(2)}, u32[]{:S(2)}) collective-permute-start(bf16[2,2,256,128]{3,2,1,0:T(8,128)(2,1)S(1)} %get-tuple-element.52), channel_id=1, source_target_pairs={{0,4},{1,5},{2,6},{3,7},{4,0},{5,1},{6,2},{7,3},{8,12},{9,13},{10,... | collective-permute-start | bytes 786440 | tf_op jit(solution)/shard_map/ppermute | solution.py:513
  70.3 0.0 collective-permute-start.13
  70.3 16.8 %shard_map.99 = (bf16[2048,1024]{1,0:T(8,128)(2,1)}, bf16[2048,1024]{1,0:T(8,128)(2,1)}, f32[16,2048]{1,0:T(8,128)}) custom-call(bf16[2048,1024]{1,0:T(8,128)(2,1)S(1)} %get-tuple-element.28.us_ref, bf16[2048,1024]{1,0:T(8,128)(2,1)S(1)} %get-tuple-element.29.vs_ref, bf16[16,128,1024]{2,1,0:T(8,128)(2,1)S(1)} %get-tuple-element.40.start_ref, ...), custom_call_target="tpu_custom_call" | custom-call | flops 17179869184 | bytes 8388608 | tf_op jit(solution)/shard_map/pallas_call | solution.py:416
  87.2 0.0 collective-permute-done.14.r2
  87.2 0.0 collective-permute-done.13.r1
  87.3 1.6 %collective-permute-start.16 = (bf16[4,2,256,128]{3,2,1,0:T(8,128)(2,1)S(1)}, bf16[4,2,256,128]{3,2,1,0:T(8,128)(2,1)S(1)}, u32[]{:S(2)}, u32[]{:S(2)}) collective-permute-start(bf16[4,2,256,128]{3,2,1,0:T(8,128)(2,1)S(1)} %shard_map.100), channel_id=1, source_target_pairs={{0,1},{1,0},{2,3},{3,2},{4,5},{5,4},{6,7},{7,6},{8,9},{9,8},{10,11... | collective-permute-start | bytes 1572872 | tf_op jit(solution)/shard_map/ppermute | solution.py:528
  88.9 1.5 %collective-permute-done.16.other = bf16[4,2,256,128]{3,2,1,0:T(8,128)(2,1)S(1)} collective-permute-done((bf16[4,2,256,128]{3,2,1,0:T(8,128)(2,1)S(1)}, bf16[4,2,256,128]{3,2,1,0:T(8,128)(2,1)S(1)}, u32[]{:S(2)}, u32[]{:S(2)}) %collective-permute-start.16) | collective-permute-done | bytes 524320 | tf_op jit(solution)/shard_map/ppermute | solution.py:528
  90.4 1.3 %shard_map.101 = (bf16[256,1024]{1,0:T(8,128)(2,1)}, bf16[256,1024]{1,0:T(8,128)(2,1)}) custom-call(bf16[2,2,256,128]{3,2,1,0:T(8,128)(2,1)S(1)} %get-tuple-element.54.r0, bf16[2,2,256,128]{3,2,1,0:T(8,128)(2,1)S(1)} %collective-permute-done.13.r1, bf16[2,2,256,128]{3,2,1,0:T(8,128)(2,1)S(1)} %collective-permute-done.14.r2, ...), custom_call_target="tpu_custom_call" | custom-call | tf_op jit(solution)/shard_map/pallas_call | solution.py:416
  (20 shorter events, 0.4 us)
Async XLA Ops:
  0.6 1.0 %copy-start = (bf16[256,1024]{1,0:T(8,128)(2,1)S(1)}, bf16[256,1024]{1,0:T(8,128)(2,1)}, u32[]{:S(2)}) copy-start(bf16[256,1024]{1,0:T(8,128)(2,1)} %in_ref.1) | copy-start | bytes 1572868
  1.7 1.0 %copy-start.1 = (bf16[256,1024]{1,0:T(8,128)(2,1)S(1)}, bf16[256,1024]{1,0:T(8,128)(2,1)}, u32[]{:S(2)}) copy-start(bf16[256,1024]{1,0:T(8,128)(2,1)} %out_ref.1) | copy-start | bytes 1572868
  3.0 19.7 %collective-permute-start = (bf16[2,2,256,128]{3,2,1,0:T(8,128)(2,1)S(1)}, bf16[2,2,256,128]{3,2,1,0:T(8,128)(2,1)S(1)}, u32[]{:S(2)}, u32[]{:S(2)}) collective-permute-start(bf16[2,2,256,128]{3,2,1,0:T(8,128)(2,1)S(1)} %get-tuple-element.31), channel_id=1, source_target_pairs={{0,2},{1,3},{2,4},{3,5},{4,6},{5,7},{6,0},{7,1},{8,10},{9,11},{10,... | collective-permute-start | bytes 786440 | tf_op jit(solution)/shard_map/ppermute | solution.py:471
  5.5 17.2 %collective-permute-start.1 = (bf16[2,2,256,128]{3,2,1,0:T(8,128)(2,1)S(1)}, bf16[2,2,256,128]{3,2,1,0:T(8,128)(2,1)S(1)}, u32[]{:S(2)}, u32[]{:S(2)}) collective-permute-start(bf16[2,2,256,128]{3,2,1,0:T(8,128)(2,1)S(1)} %get-tuple-element.32), channel_id=1, source_target_pairs={{0,4},{1,5},{2,6},{3,7},{4,0},{5,1},{6,2},{7,3},{8,12},{9,13},{10,... | collective-permute-start | bytes 786440 | tf_op jit(solution)/shard_map/ppermute | solution.py:471
  8.8 13.9 %collective-permute-start.2 = (bf16[2,2,256,128]{3,2,1,0:T(8,128)(2,1)S(1)}, bf16[2,2,256,128]{3,2,1,0:T(8,128)(2,1)S(1)}, u32[]{:S(2)}, u32[]{:S(2)}) collective-permute-start(bf16[2,2,256,128]{3,2,1,0:T(8,128)(2,1)S(1)} %get-tuple-element.33), channel_id=1, source_target_pairs={{0,6},{1,7},{2,0},{3,1},{4,2},{5,3},{6,4},{7,5},{8,14},{9,15},{10,... | collective-permute-start | bytes 786440 | tf_op jit(solution)/shard_map/ppermute | solution.py:471
  9.6 0.9 copy-start.2
  22.8 3.1 %collective-permute-start.3 = (bf16[4,2,256,128]{3,2,1,0:T(8,128)(2,1)S(1)}, bf16[4,2,256,128]{3,2,1,0:T(8,128)(2,1)S(1)}, u32[]{:S(2)}, u32[]{:S(2)}) collective-permute-start(bf16[4,2,256,128]{3,2,1,0:T(8,128)(2,1)S(1)} %shard_map.94), channel_id=1, source_target_pairs={{0,1},{1,0},{2,3},{3,2},{4,5},{5,4},{6,7},{7,6},{8,9},{9,8},{10,11... | collective-permute-start | bytes 1572872 | tf_op jit(solution)/shard_map/ppermute | solution.py:491
  30.2 8.1 %collective-permute-start.6 = (f16[272,256]{1,0:T(8,128)(2,1)S(1)}, f16[272,256]{1,0:T(8,128)(2,1)S(1)}, u32[]{:S(2)}, u32[]{:S(2)}) collective-permute-start(f16[272,256]{1,0:T(8,128)(2,1)S(1)} %get-tuple-element.58), channel_id=1, source_target_pairs={{0,24},{8,0},{16,8},{24,16},{32,56},{40,32},{48,40},{56,48},{64,88... | collective-permute-start | bytes 417800 | tf_op jit(solution)/shard_map/ppermute | solution.py:456
  32.7 6.1 %collective-permute-start.5 = (f16[272,256]{1,0:T(8,128)(2,1)S(1)}, f16[272,256]{1,0:T(8,128)(2,1)S(1)}, u32[]{:S(2)}, u32[]{:S(2)}) collective-permute-start(f16[272,256]{1,0:T(8,128)(2,1)S(1)} %get-tuple-element.59), channel_id=1, source_target_pairs={{0,16},{8,24},{16,0},{24,8},{32,48},{40,56},{48,32},{56,40},{64,80... | collective-permute-start | bytes 417800 | tf_op jit(solution)/shard_map/ppermute | solution.py:456
  33.2 9.6 %collective-permute-start.4 = (f16[272,256]{1,0:T(8,128)(2,1)S(1)}, f16[272,256]{1,0:T(8,128)(2,1)S(1)}, u32[]{:S(2)}, u32[]{:S(2)}) collective-permute-start(f16[272,256]{1,0:T(8,128)(2,1)S(1)} %get-tuple-element.60), channel_id=1, source_target_pairs={{0,8},{8,16},{16,24},{24,0},{32,40},{40,48},{48,56},{56,32},{64,72... | collective-permute-start | bytes 417800 | tf_op jit(solution)/shard_map/ppermute | solution.py:456
  43.1 4.2 %collective-permute-start.9 = (f16[144,256]{1,0:T(8,128)(2,1)S(1)}, f16[144,256]{1,0:T(8,128)(2,1)S(1)}, u32[]{:S(2)}, u32[]{:S(2)}) collective-permute-start(f16[144,256]{1,0:T(8,128)(2,1)S(1)} %get-tuple-element.61), channel_id=1, source_target_pairs={{0,96},{8,104},{16,112},{24,120},{32,0},{40,8},{48,16},{56,24},{64... | collective-permute-start | bytes 221192 | tf_op jit(solution)/shard_map/ppermute | solution.py:456
  45.9 4.8 %collective-permute-start.8 = (f16[144,256]{1,0:T(8,128)(2,1)S(1)}, f16[144,256]{1,0:T(8,128)(2,1)S(1)}, u32[]{:S(2)}, u32[]{:S(2)}) collective-permute-start(f16[144,256]{1,0:T(8,128)(2,1)S(1)} %get-tuple-element.62), channel_id=1, source_target_pairs={{0,64},{8,72},{16,80},{24,88},{32,96},{40,104},{48,112},{56,120},{... | collective-permute-start | bytes 221192 | tf_op jit(solution)/shard_map/ppermute | solution.py:456
  46.2 6.3 %collective-permute-start.7 = (f16[144,256]{1,0:T(8,128)(2,1)S(1)}, f16[144,256]{1,0:T(8,128)(2,1)S(1)}, u32[]{:S(2)}, u32[]{:S(2)}) collective-permute-start(f16[144,256]{1,0:T(8,128)(2,1)S(1)} %get-tuple-element.63), channel_id=1, source_target_pairs={{0,32},{8,40},{16,48},{24,56},{32,64},{40,72},{48,80},{56,88},{64,... | collective-permute-start | bytes 221192 | tf_op jit(solution)/shard_map/ppermute | solution.py:456
  53.5 4.0 %collective-permute-start.12 = (f16[272,256]{1,0:T(8,128)(2,1)S(1)}, f16[272,256]{1,0:T(8,128)(2,1)S(1)}, u32[]{:S(2)}, u32[]{:S(2)}) collective-permute-start(f16[272,256]{1,0:T(8,128)(2,1)S(1)} %get-tuple-element.55), channel_id=1, source_target_pairs={{0,24},{8,0},{16,8},{24,16},{32,56},{40,32},{48,40},{56,48},{64,88... | collective-permute-start | bytes 417800 | tf_op jit(solution)/shard_map/ppermute | solution.py:456
  53.6 5.6 %collective-permute-start.11 = (f16[272,256]{1,0:T(8,128)(2,1)S(1)}, f16[272,256]{1,0:T(8,128)(2,1)S(1)}, u32[]{:S(2)}, u32[]{:S(2)}) collective-permute-start(f16[272,256]{1,0:T(8,128)(2,1)S(1)} %get-tuple-element.56), channel_id=1, source_target_pairs={{0,16},{8,24},{16,0},{24,8},{32,48},{40,56},{48,32},{56,40},{64,80... | collective-permute-start | bytes 417800 | tf_op jit(solution)/shard_map/ppermute | solution.py:456
  53.6 9.6 %collective-permute-start.10 = (f16[272,256]{1,0:T(8,128)(2,1)S(1)}, f16[272,256]{1,0:T(8,128)(2,1)S(1)}, u32[]{:S(2)}, u32[]{:S(2)}) collective-permute-start(f16[272,256]{1,0:T(8,128)(2,1)S(1)} %get-tuple-element.57), channel_id=1, source_target_pairs={{0,8},{8,16},{16,24},{24,0},{32,40},{40,48},{48,56},{56,32},{64,72... | collective-permute-start | bytes 417800 | tf_op jit(solution)/shard_map/ppermute | solution.py:456
  67.7 19.4 %collective-permute-start.15 = (bf16[2,2,256,128]{3,2,1,0:T(8,128)(2,1)S(1)}, bf16[2,2,256,128]{3,2,1,0:T(8,128)(2,1)S(1)}, u32[]{:S(2)}, u32[]{:S(2)}) collective-permute-start(bf16[2,2,256,128]{3,2,1,0:T(8,128)(2,1)S(1)} %get-tuple-element.51), channel_id=1, source_target_pairs={{0,6},{1,7},{2,0},{3,1},{4,2},{5,3},{6,4},{7,5},{8,14},{9,15},{10,... | collective-permute-start | bytes 786440 | tf_op jit(solution)/shard_map/ppermute | solution.py:513
  67.8 19.4 %collective-permute-start.14 = (bf16[2,2,256,128]{3,2,1,0:T(8,128)(2,1)S(1)}, bf16[2,2,256,128]{3,2,1,0:T(8,128)(2,1)S(1)}, u32[]{:S(2)}, u32[]{:S(2)}) collective-permute-start(bf16[2,2,256,128]{3,2,1,0:T(8,128)(2,1)S(1)} %get-tuple-element.52), channel_id=1, source_target_pairs={{0,4},{1,5},{2,6},{3,7},{4,0},{5,1},{6,2},{7,3},{8,12},{9,13},{10,... | collective-permute-start | bytes 786440 | tf_op jit(solution)/shard_map/ppermute | solution.py:513
  70.3 16.9 %collective-permute-start.13 = (bf16[2,2,256,128]{3,2,1,0:T(8,128)(2,1)S(1)}, bf16[2,2,256,128]{3,2,1,0:T(8,128)(2,1)S(1)}, u32[]{:S(2)}, u32[]{:S(2)}) collective-permute-start(bf16[2,2,256,128]{3,2,1,0:T(8,128)(2,1)S(1)} %get-tuple-element.53), channel_id=1, source_target_pairs={{0,2},{1,3},{2,4},{3,5},{4,6},{5,7},{6,0},{7,1},{8,10},{9,11},{10,... | collective-permute-start | bytes 786440 | tf_op jit(solution)/shard_map/ppermute | solution.py:513
  87.3 3.2 %collective-permute-start.16 = (bf16[4,2,256,128]{3,2,1,0:T(8,128)(2,1)S(1)}, bf16[4,2,256,128]{3,2,1,0:T(8,128)(2,1)S(1)}, u32[]{:S(2)}, u32[]{:S(2)}) collective-permute-start(bf16[4,2,256,128]{3,2,1,0:T(8,128)(2,1)S(1)} %shard_map.100), channel_id=1, source_target_pairs={{0,1},{1,0},{2,3},{3,2},{4,5},{5,4},{6,7},{7,6},{8,9},{9,8},{10,11... | collective-permute-start | bytes 1572872 | tf_op jit(solution)/shard_map/ppermute | solution.py:528

commit v2 on v1

--- a/solution.py
+++ b/solution.py
@@ -68,7 +68,7 @@
 
 
 def scale_kernel(
-    sig_hbm, cot_hbm, ld_ref, us_ref, vs_ref, g_ref, u2_ref, v2_ref, half_ref, ind_ref, sbuf, cbuf, ssem, csem
+    sig_hbm, cot_hbm, ld_ref, us_ref, vs_ref, u2_ref, v2_ref, half_ref, ind_ref, sbuf, cbuf, ssem, csem
 ):
     slots = sbuf.shape[0]
 
@@ -106,14 +106,11 @@
         for copy in reads(j):
             copy.wait()
         u_rows, v_rows = u2_ref[j].T, v2_ref[j].T
-        grad = jnp.zeros((C, C), F32)
         for i in range(TILES):
             us = (cbuf[slot, :, tile(i)].astype(F32) * dot(u_rows, ind_ref[:, tile(i)])).astype(BF16)
             vs = (sbuf[slot, :, tile(i)].astype(F32) * dot(v_rows, ind_ref[:, tile(i)])).astype(BF16)
             us_ref[piece_rows(j), tile(i)] = us
             vs_ref[piece_rows(j), tile(i)] = vs
-            grad = grad + dot_nt(us, vs)
-        g_ref[j] = jnp.where(iota((C, C), 0) >= iota((C, C), 1), grad, 0.0).astype(BF16)
 
         @pl.when(j + slots < PIECES)
         def _():
@@ -144,7 +141,31 @@
     return a * (1.0 / most), jnp.log(most)
 
 
-def state_kernel(us_ref, vs_ref, r0, r1, r2, r3, other, half_ref, x_ref, local_ref, after_ref, msg_ref, xt_ref):
+def state_part(d, us_ref, vs_ref, xt_ref, half_ref, local_ref, after_ref, msg_ref):
+    me = lax.rem(lax.axis_index("ctx"), ROW)
+    lanes = pl.ds(pl.multiple_of(lax.rem(me + d, ROW) * SLICE, SLICE), SLICE)
+    state = jnp.zeros((N, SLICE), F32)
+    adjoint = jnp.zeros((N, SLICE), F32)
+    total = jnp.zeros((1, SLICE), F32)
+    for i in range(PIECES):
+        k = PIECES - 1 - i
+        local_ref[i, :, lanes] = state.astype(BF16)
+        half = half_ref[i : i + 1, lanes]
+        weight = jnp.exp(half)
+        end = dot(xt_ref[0, :, i * C : (i + 1) * C], vs_ref[i * C : (i + 1) * C, lanes])
+        state = weight * (weight * state + end)
+        total = total + 2.0 * half
+        after_ref[k, :, lanes] = adjoint.astype(BF16)
+        weight = jnp.exp(half_ref[k : k + 1, lanes])
+        end = dot(xt_ref[1, :, k * C : (k + 1) * C], us_ref[k * C : (k + 1) * C, lanes])
+        adjoint = weight * (weight * adjoint + end)
+    local_ref[PIECES, :, lanes] = state.astype(BF16)
+    msg_ref[0:N, :], first = scaled(state)
+    msg_ref[N : 2 * N, :], second = scaled(adjoint)
+    msg_ref[2 * N :, :] = log_rows(total, first, second)
+
+
+def state_kernel(us_ref, vs_ref, r0, r1, r2, r3, other, half_ref, x_ref, xt_ref, local_ref, after_ref, msg_ref):
     z, core, homes = head_places()
     for d, ref in enumerate((r0, r1, r2, r3)):
         x_ref[2 * homes[d] + core] = ref[core]
@@ -153,32 +174,16 @@
         rows = slice((j % 2) * C, (j % 2 + 1) * C)
         for i in range(2):
             xt_ref[i, :, j * C : (j + 1) * C] = x_ref[j // 2, i, rows, :].T
-    me = lax.rem(lax.axis_index("ctx"), ROW)
 
     def part(d, carry):
-        lanes = pl.ds(pl.multiple_of(lax.rem(me + d, ROW) * SLICE, SLICE), SLICE)
-        state = jnp.zeros((N, SLICE), F32)
-        adjoint = jnp.zeros((N, SLICE), F32)
-        total = jnp.zeros((1, SLICE), F32)
-        for i in range(PIECES):
-            k = PIECES - 1 - i
-            local_ref[i, :, lanes] = state.astype(BF16)
-            half = half_ref[i : i + 1, lanes]
-            weight = jnp.exp(half)
-            end = dot(xt_ref[0, :, i * C : (i + 1) * C], vs_ref[i * C : (i + 1) * C, lanes])
-            state = weight * (weight * state + end)
-            total = total + 2.0 * half
-            after_ref[k, :, lanes] = adjoint.astype(BF16)
-            weight = jnp.exp(half_ref[k : k + 1, lanes])
-            end = dot(xt_ref[1, :, k * C : (k + 1) * C], us_ref[k * C : (k + 1) * C, lanes])
-            adjoint = weight * (weight * adjoint + end)
-        local_ref[PIECES, :, lanes] = state.astype(BF16)
-        msg_ref[d, 0:N, :], first = scaled(state)
-        msg_ref[d, N : 2 * N, :], second = scaled(adjoint)
-        msg_ref[d, 2 * N :, :] = log_rows(total, first, second)
+        state_part(d, us_ref, vs_ref, xt_ref, half_ref, local_ref, after_ref, msg_ref.at[d - 1])
         return carry
 
-    lax.fori_loop(0, ROW, part, 0)
+    lax.fori_loop(1, ROW, part, 0)
+
+
+def own_state_kernel(us_ref, vs_ref, xt_ref, half_ref, local_in, after_in, local_ref, after_ref, msg_ref):
+    state_part(0, us_ref, vs_ref, xt_ref, half_ref, local_ref, after_ref, msg_ref)
 
 
 def between(logs, places, chosen):
@@ -192,6 +197,22 @@
     return jnp.where(flag, jnp.exp(log), 0.0)
 
 
+def intra_kernel(us_ref, vs_ref, x_ref, after_ref, base_ref, of_ref):
+    of_ref[...] = one_hot(iota((LANES, C), 0) // P_SIZE == iota((LANES, C), 1))
+    lower = iota((C, C), 0) >= iota((C, C), 1)
+
+    def piece(j, carry):
+        rows = piece_rows(j)
+        part = pl.ds(pl.multiple_of(lax.rem(j, 2) * C, C), C)
+        block = lax.div(j, 2)
+        grad = jnp.where(lower, dot_nt(us_ref[rows, :], vs_ref[rows, :]), 0.0).astype(BF16)
+        base_ref[j, 0] = dot_tn(grad, x_ref[block, 1, part, :])
+        base_ref[j, 1] = dot(grad, x_ref[block, 0, part, :])
+        return carry
+
+    lax.fori_loop(0, PIECES, piece, 0, unroll=2)
+
+
 def head_places():
     index = lax.axis_index("head")
     z, core = lax.div(index, 2), lax.rem(index, 2)
@@ -204,7 +225,7 @@
     return x, y, [lax.rem(x + ROW - d, ROW) for d in range(ROW)]
 
 
-def row_kernel(r0, r1, r2, r3, out_ref):
+def row_kernel(r0, r1, r2, r3, base_ref, out_ref):
     x, y, places = own_places()
     refs = (r0, r1, r2, r3)
     ends = [r[2 * N :, :] for r in refs]
@@ -252,8 +273,7 @@
 def projection_kernel(
     us_ref,
     vs_ref,
-    x_ref,
-    g_ref,
+    base_ref,
     half_ref,
     local_ref,
     after_ref,
@@ -283,25 +303,33 @@
 
     prior = jnp.zeros((1, LANES), F32)
     for j in range(PIECES + 1):
-        first = local_ref[j].astype(F32) + jnp.exp(prior) * enter_ref[0]
-        if j > 0:
-            total_ref[j - 1 : j, :] = jnp.sum(first * last_ref[...], axis=0, keepdims=True)
-        if j == PIECES:
-            break
-        rows = slice(j * C, (j + 1) * C)
-        half = half_ref[j : j + 1, :]
-        prior = prior + 2.0 * half
-        weight = jnp.exp(half)
-        part = slice((j % 2) * C, (j % 2 + 1) * C)
-        start = (weight * first).astype(BF16)
-        start_ref[j] = start
-        to = (lax.rem(j // 4 + ROW - z, ROW), j // 2 % 2)
-        grad_ref[*to, 1, part, :] = (dot(g_ref[j], x_ref[j // 2, 0, part, :]) + dot_nt(us_ref[rows], start)).astype(BF16)
-        second = after_ref[j].astype(F32) + jnp.exp(laters[j]) * enter_ref[1]
-        last_ref[...] = second
-        behind = (weight * second).astype(BF16)
-        behind_ref[j] = behind
-        grad_ref[*to, 0, part, :] = (dot_tn(g_ref[j], x_ref[j // 2, 1, part, :]) + dot_nt(vs_ref[rows], behind)).astype(BF16)
+        before = jnp.exp(prior)
+        if j < PIECES:
+            rows = slice(j * C, (j + 1) * C)
+            half = half_ref[j : j + 1, :]
+            prior = prior + 2.0 * half
+            weight, later = jnp.exp(half), jnp.exp(laters[j])
+            part = slice((j % 2) * C, (j % 2 + 1) * C)
+            to = (lax.rem(j // 4 + ROW - z, ROW), j // 2 % 2)
+            grad_out, grad_in = base_ref[j, 1], base_ref[j, 0]
+        for i in range(TILES):
+            t = tile(i)
+            first = local_ref[j, :, t].astype(F32) + before[:, t] * enter_ref[0, :, t]
+            if j > 0:
+                total_ref[j - 1 : j, t] = jnp.sum(first * last_ref[:, t], axis=0, keepdims=True)
+            if j == PIECES:
+                continue
+            start = (weight[:, t] * first).astype(BF16)
+            start_ref[j, :, t] = start
+            grad_out = grad_out + dot_nt(us_ref[rows, t], start)
+            second = after_ref[j, :, t].astype(F32) + later[:, t] * enter_ref[1, :, t]
+            last_ref[:, t] = second
+            behind = (weight[:, t] * second).astype(BF16)
+            behind_ref[j, :, t] = behind
+            grad_in = grad_in + dot_nt(vs_ref[rows, t], behind)
+        if j < PIECES:
+            grad_ref[*to, 1, part, :] = grad_out.astype(BF16)
+            grad_ref[*to, 0, part, :] = grad_in.astype(BF16)
 
 
 def result_kernel(
@@ -312,15 +340,12 @@
     x_ref,
     u2_ref,
     v2_ref,
-    total_ref,
     out_hbm,
     grad_hbm,
-    decay_ref,
+    diff_ref,
     obuf,
     gbuf,
     ind_ref,
-    of_ref,
-    heads_ref,
     osem,
     gsem,
 ):
@@ -334,12 +359,8 @@
         )
 
     ind_ref[...] = one_hot(lane_heads(2 * HEADS))
-    own = ind_ref[0:HEADS, :]
-    of_ref[...] = one_hot(iota((LANES, C), 0) // P_SIZE == iota((LANES, C), 1))
-    heads_ref[...] = sum(dot_nt(own, part) for part in split3(total_ref[...]))
     lower = iota((C, C), 0) >= iota((C, C), 1)
     upper = iota((C, C), 0) <= iota((C, C), 1)
-    from_on = one_hot(lower)
 
     def piece(j, carry):
         place = lax.rem(j, outs)
@@ -357,8 +378,6 @@
             for copy in writes(j - outs):
                 copy.wait()
 
-        total = jnp.sum(jnp.where(iota((HEADS, PIECES), 1) == j, heads_ref[...], 0.0), axis=1, keepdims=True)
-        cum_grad = jnp.zeros((C, C), F32)
         for i in range(TILES):
             us, vs = us_ref[piece_rows(j), tile(i)], vs_ref[piece_rows(j), tile(i)]
             out = dot(left_out, jnp.concatenate([vs, start_ref[j, :, tile(i)]], axis=0))
@@ -366,28 +385,56 @@
             grad = dot(left_grad, jnp.concatenate([us, behind_ref[j, :, tile(i)]], axis=0))
             gbuf[place, :, tile(i)] = (grad * dot(v_rows, ind_ref[:, tile(i)])).astype(BF16)
             diff = us.astype(F32) * out - vs.astype(F32) * grad
-            cum_grad = cum_grad + dot(diff.astype(BF16), of_ref[tile(i), :])
+            diff_ref[piece_rows(j), tile(i)] = diff.astype(BF16)
         for copy in writes(j):
             copy.start()
-        cum_grad = cum_grad.T[0:HEADS] + jnp.where(iota((HEADS, C), 1) == C - 1, total, 0.0)
-        sums = dot(jnp.concatenate(split3(cum_grad), axis=0), from_on)
-        decay_ref[:, piece_rows(j)] = sums[0:HEADS] + sums[HEADS : 2 * HEADS] + sums[2 * HEADS :]
         return carry
 
-    lax.fori_loop(0, PIECES, piece, 0)
+    lax.fori_loop(0, PIECES, piece, 0, unroll=2)
     for j in range(PIECES - outs, PIECES):
         for copy in writes(j):
             copy.wait()
 
 
-def split_kernel(in_ref, out_ref, *sent):
+def decay_part(k, diff_ref, total_ref, of_ref, decay_ref):
+    own = one_hot(lane_heads(HEADS))
+    from_on = one_hot(iota((C, C), 0) >= iota((C, C), 1))
+    last = iota((HEADS, C), 1) == C - 1
+    totals = sum(dot_nt(own, part) for part in split3(total_ref[...]))
+    cum_grad = dot(diff_ref[4 * k * C : 4 * (k + 1) * C, :], of_ref[...])
+    parts = []
+    for j in range(4):
+        total = totals[:, 4 * k + j : 4 * k + j + 1]
+        parts.append(cum_grad[j * C : (j + 1) * C].T[0:HEADS] + jnp.where(last, total, 0.0))
+    sums = sum(dot(part, from_on) for part in split3(jnp.concatenate(parts, axis=0)))
+    for j in range(4):
+        decay_ref[:, (4 * k + j) * C : (4 * k + j + 1) * C] = sums[j * HEADS : (j + 1) * HEADS]
+
+
+def first_decay_kernel(diff_ref, total_ref, of_ref, decay_ref):
+    for k in range(2):
+        decay_part(k, diff_ref, total_ref, of_ref, decay_ref)
+
+
+def decay_kernel(diff_ref, total_ref, of_ref, first_ref, decay_ref):
+    decay_ref[:, 0 : TOKENS // 2] = first_ref[...]
+    for k in range(2, 4):
+        decay_part(k, diff_ref, total_ref, of_ref, decay_ref)
+
+
+def split_kernel(in_hbm, out_hbm, s0, s1, s2, s3, sems):
     z, core, homes = head_places()
-    for d, ref in enumerate(sent):
+    copies = []
+    for d, ref in enumerate((s0, s1, s2, s3)):
         for to in range(2):
             group = 2 * lax.rem(z + d, ROW) + to
             columns = pl.ds(pl.multiple_of(group * N, N), N)
-            ref[to, 0] = in_ref[:, columns]
-            ref[to, 1] = out_ref[:, columns]
+            for i, source in enumerate((in_hbm, out_hbm)):
+                copies.append(pltpu.make_async_copy(source.at[:, columns], ref.at[to, i], sems.at[d, to, i]))
+    for copy in copies:
+        copy.start()
+    for copy in copies:
+        copy.wait()
 
 
 def swap_kernel(r0, r1, r2, r3, after_hbm, other_ref):
@@ -396,7 +443,7 @@
         other_ref[d] = ref[1 - core]
 
 
-def join_kernel(r0, r1, r2, r3, other, in_ref, out_ref):
+def join_kernel(r0, r1, r2, r3, other, after_hbm, in_ref, out_ref):
     z, core, homes = head_places()
     for d, ref in enumerate((r0, r1, r2, r3)):
         columns = pl.ds(pl.multiple_of((2 * homes[d] + core) * N, N), N)
@@ -412,13 +459,14 @@
 DMA = pltpu.SemaphoreType.DMA
 
 
-def call(kernel, args, outs, specs, out_specs, scratch=(), limit=10, flops=0, moved=0):
+def call(kernel, args, outs, specs, out_specs, scratch=(), limit=10, flops=0, moved=0, aliases={}):
     return pl.pallas_call(
         kernel,
         out_shape=outs,
         in_specs=specs,
         out_specs=out_specs,
         scratch_shapes=list(scratch),
+        input_output_aliases=aliases,
         compiler_params=pltpu.CompilerParams(vmem_limit_bytes=limit * MIB),
         cost_estimate=pl.CostEstimate(flops=flops, bytes_accessed=moved, transcendentals=0),
     )(*args)
@@ -467,67 +515,97 @@
     states = (PIECES, N, LANES)
     band = (C, LANES)
 
-    sent = call(split_kernel, (state_in, state_out), [held(chip)] * ROW, [VMEM] * 2, [VMEM] * ROW)
+    sent = call(
+        split_kernel, (far(state_in), far(state_out)), [held(chip)] * ROW, [HBM] * 2, [VMEM] * ROW, [DMA((ROW, 2, 2))]
+    )
     got = [sent[0]] + [lax.ppermute(sent[d], "head", along_z(d)) for d in (1, 3, 2)]
     got = [got[0], got[1], got[3], got[2]]
-    us, vs, g, u2, v2, half = call(
+    us, vs, u2, v2, half = call(
         scale_kernel,
         (far(signal), far(cotangent), log_decay),
         (
             held(wide),
             held(wide),
-            held((PIECES, C, C)),
             held((PIECES, 2 * HEADS, C)),
             held((PIECES, 2 * HEADS, C)),
             held((PIECES, LANES), F32),
         ),
         [HBM, HBM, VMEM],
-        [VMEM] * 6,
+        [VMEM] * 5,
         [pltpu.VMEM((2 * HEADS, LANES), BF16)] + [pltpu.VMEM((4,) + band, BF16)] * 2 + [DMA((4,))] * 2,
         flops=1 << 33,
         moved=1 << 23,
     )
     other = call(swap_kernel, got + [half], held((ROW, 2, own, N)), [VMEM] * 5, VMEM)
     other = lax.ppermute(other, "head", OTHER_CORE)
-    x, local, after, msg = call(
+    x, xt, local, after, msg = call(
         state_kernel,
         [us, vs] + got + [other, half],
-        (held(blocks), held((PIECES + 1, N, LANES)), held(states), held((ROW, 2 * N + 16, SLICE), F32)),
+        (
+            held(blocks),
+            held((2, N, TOKENS)),
+            held((PIECES + 1, N, LANES)),
+            held(states),
+            held((ROW - 1, 2 * N + 16, SLICE), F32),
+        ),
         [VMEM] * 8,
+        [VMEM] * 5,
+    )
+    mates = [send(msg[d - 1], along_x(d)) for d in range(1, ROW)]
+    local, after, own_msg = call(
+        own_state_kernel,
+        (us, vs, xt, half, local, after),
+        (held((PIECES + 1, N, LANES)), held(states), held((2 * N + 16, SLICE), F32)),
+        [VMEM] * 6,
+        [VMEM] * 3,
+        aliases={4: 0, 5: 1},
+        flops=1 << 31,
+        moved=1 << 23,
+    )
+    mates = [own_msg] + mates
+    base, of_head = call(
+        intra_kernel,
+        (us, vs, x, local),
+        (held((PIECES, 2, C, N), F32), held((LANES, C))),
         [VMEM] * 4,
-        [pltpu.VMEM((2, N, TOKENS), BF16)],
-    )
-    mates = [msg[0]] + [send(msg[d], along_x(d)) for d in range(1, ROW)]
-    totals = call(row_kernel, mates, held((ROW - 1, N + 16, SLICE), F32), [VMEM] * 4, VMEM)
+        [VMEM] * 2,
+        flops=1 << 33,
+        moved=1 << 23,
+    )
+    totals = call(row_kernel, mates + [base], held((ROW - 1, N + 16, SLICE), F32), [VMEM] * 5, VMEM)
     rows = [send(totals[d - 1], along_y(d)) for d in range(1, ROW)]
     back = call(enter_kernel, mates + rows, held((ROW, 2 * N + 16, SLICE), F32), [VMEM] * 7, VMEM)
     shares = [back[0]] + [send(back[e], along_x(e)) for e in range(1, ROW)]
     grads, start, behind, total = call(
         projection_kernel,
-        [us, vs, x, g, half, local, after] + shares,
+        [us, vs, base, half, local, after] + shares,
         (held((ROW,) + chip), held(states), held(states), held((PIECES, LANES), F32)),
-        [VMEM] * 11,
+        [VMEM] * 10,
         [VMEM] * 4,
         [pltpu.VMEM((2,) + band, F32), pltpu.VMEM(band, F32)],
     )
     returned = [grads[0]] + [lax.ppermute(grads[d], "head", along_z(d)) for d in (1, 3, 2)]
     returned = [returned[0], returned[1], returned[3], returned[2]]
-    output, grad_signal, grad_decay = call(
+    output, grad_signal, diff = call(
         result_kernel,
-        (us, vs, start, behind, x, u2, v2, total),
-        (plain(wide), plain(wide), plain((HEADS, TOKENS), F32)),
-        [VMEM] * 8,
+        (us, vs, start, behind, x, u2, v2),
+        (plain(wide), plain(wide), held(wide)),
+        [VMEM] * 7,
         [HBM, HBM, VMEM],
-        [pltpu.VMEM((2,) + band, BF16)] * 2
-        + [pltpu.VMEM((2 * HEADS, LANES), BF16), pltpu.VMEM((LANES, C), BF16), pltpu.VMEM((HEADS, PIECES), F32)]
-        + [DMA((2,)), DMA((2,))],
+        [pltpu.VMEM((4,) + band, BF16)] * 2 + [pltpu.VMEM((2 * HEADS, LANES), BF16), DMA((4,)), DMA((4,))],
         flops=1 << 34,
         moved=1 << 23,
     )
-    other = call(swap_kernel, returned + [far(grad_decay)], held((ROW, 2, own, N)), [VMEM] * ROW + [HBM], VMEM)
+    decay = call(first_decay_kernel, (diff, total, of_head), held((HEADS, TOKENS // 2), F32), [VMEM] * 3, VMEM)
+    other = call(swap_kernel, returned + [decay], held((ROW, 2, own, N)), [VMEM] * 5, VMEM)
     other = lax.ppermute(other, "head", OTHER_CORE)
+    grad_decay = call(
+        decay_kernel, (diff, total, of_head, decay), plain((HEADS, TOKENS), F32), [VMEM] * 4, VMEM, flops=1 << 31, moved=1 << 22
+    )
     narrow = plain(state_in.shape)
-    grad_in, grad_out = call(join_kernel, returned + [other], (narrow, narrow), [VMEM] * 5, [VMEM] * 2)
+    grad_in, grad_out = call(
+        join_kernel, returned + [other, far(grad_decay)], (narrow, narrow), [VMEM] * 5 + [HBM], [VMEM] * 2
+    )
     return output, grad_signal, grad_in, grad_out, grad_decay
 
 

time: 91.9 us -> 83.7 us (0.911)
  waiting for transfers between devices: 25.7 us -> 18.7 us
  starting transfers between devices: 21.4 us -> 23.6 us
  local copies, waits for them, and re-layouts: 3.32 us -> 1.22 us
  Pallas kernels: 40 us -> 38.7 us
    ppermute x9, waiting for transfers between devices: 22.7 us -> 12.9 us  [send(): return lax.ppermute(a.astype(jnp.float16), 'ctx', pairs).astype(F32)]
    ppermute x3, waiting for transfers between devices: 0.01 us -> 3.12 us  [body(): lax.ppermute(sent[d], 'head', along_z(d))]
    unnamed x6 -> x2, local copies, waits for them, and re-layouts: 2.98 us -> 0.9 us
    ppermute x2, starting transfers between devices: 3.22 us -> 5.13 us  [body(): other = lax.ppermute(other, 'head', OTHER_CORE)]
    ppermute x2, waiting for transfers between devices: 3.07 us -> 1.54 us  [body(): other = lax.ppermute(other, 'head', OTHER_CORE)]
    pallas_call x10 -> x14, Pallas kernels: 40 us -> 38.7 us  [call(): pl.pallas_call(kernel, out_shape=outs, in_specs=specs, out_specs=out_spec...]
    ppermute x3, waiting for transfers between devices: 0.01 us -> 1.12 us  [body(): lax.ppermute(grads[d], 'head', along_z(d))]
  transfers between devices with their start and end apart: 17 -> 17, of which waited for: 11 -> 10; matrix products, arithmetic and copies ran while one was open for 0% -> 0% of each run, Pallas kernels for 32% -> 33%
where the time goes in v2:
time: 83.7 us; the launch traced here: 83.4 us
  Pallas kernels  38.7 us (46%)
  starting transfers between devices  23.6 us (28%)
  waiting for transfers between devices  18.7 us (22%)
  local copies, waits for them, and re-layouts  1.22 us (1%)
  between operations  0.85 us (1%)
    pallas_call x14, Pallas kernels, call(): pl.pallas_call(kernel, out_shape=outs, in_specs=specs, out_specs=out_spec...  38.7 us
    ppermute x9, waiting for transfers between devices, send(): return lax.ppermute(a.astype(jnp.float16), 'ctx', pairs).astype(F32)  12.9 us
    ppermute x9, starting transfers between devices, send(): return lax.ppermute(a.astype(jnp.float16), 'ctx', pairs).astype(F32)  9 us
    ppermute x3, starting transfers between devices, body(): lax.ppermute(sent[d], 'head', along_z(d))  6.57 us
    ppermute x2, starting transfers between devices, body(): other = lax.ppermute(other, 'head', OTHER_CORE)  5.13 us
    ppermute x3, waiting for transfers between devices, body(): lax.ppermute(sent[d], 'head', along_z(d))  3.12 us
    ppermute x3, starting transfers between devices, body(): lax.ppermute(grads[d], 'head', along_z(d))  2.94 us
  transfers between devices with their start and end apart: 17, of which 10 were waited for; matrix products, arithmetic and copies ran while one was open for 0% of the time, Pallas kernels for 33%

profile of v2, /device:TPU:1, one launch (start us, length us, event | category | flops | bytes accessed | tf_op | source)
XLA Modules:
  0.0 83.4 jit_solution(11405059778180291400)
XLA Ops:
  0.6 1.4 %shard_map.93 = (bf16[2,2,256,128]{3,2,1,0:T(8,128)(2,1)S(1)}, bf16[2,2,256,128]{3,2,1,0:T(8,128)(2,1)S(1)}, bf16[2,2,256,128]{3,2,1,0:T(8,128)(2,1)S(1)}, bf16[2,2,256,128]{3,2,1,0:T(8,128)(2,1)S(1)}) custom-call(bf16[256,1024]{1,0:T(8,128)(2,1)} %in_hbm.1, bf16[256,1024]{1,0:T(8,128)(2,1)} %out_hbm.1), custom_call_target="tpu_custom_call" | custom-call | tf_op jit(solution)/shard_map/pallas_call | solution.py:463
  2.1 2.5 %collective-permute-start = (bf16[2,2,256,128]{3,2,1,0:T(8,128)(2,1)S(1)}, bf16[2,2,256,128]{3,2,1,0:T(8,128)(2,1)S(1)}, u32[]{:S(2)}, u32[]{:S(2)}) collective-permute-start(bf16[2,2,256,128]{3,2,1,0:T(8,128)(2,1)S(1)} %get-tuple-element.36), channel_id=1, source_target_pairs={{0,2},{1,3},{2,4},{3,5},{4,6},{5,7},{6,0},{7,1},{8,10},{9,11},{10,... | collective-permute-start | bytes 786440 | tf_op jit(solution)/shard_map/ppermute | solution.py:521
  4.6 3.3 %collective-permute-start.1 = (bf16[2,2,256,128]{3,2,1,0:T(8,128)(2,1)S(1)}, bf16[2,2,256,128]{3,2,1,0:T(8,128)(2,1)S(1)}, u32[]{:S(2)}, u32[]{:S(2)}) collective-permute-start(bf16[2,2,256,128]{3,2,1,0:T(8,128)(2,1)S(1)} %get-tuple-element.37), channel_id=1, source_target_pairs={{0,4},{1,5},{2,6},{3,7},{4,0},{5,1},{6,2},{7,3},{8,12},{9,13},{10,... | collective-permute-start | bytes 786440 | tf_op jit(solution)/shard_map/ppermute | solution.py:521
  7.9 0.7 collective-permute-start.2
  8.6 0.9 %copy-done = f32[16,2048]{1,0:T(8,128)S(1)} copy-done((f32[16,2048]{1,0:T(8,128)S(1)}, f32[16,2048]{1,0:T(8,128)}, u32[]{:S(2)}) %copy-start) | copy-done | bytes 131096
  9.5 6.6 %shard_map.92 = (bf16[2048,1024]{1,0:T(8,128)(2,1)S(1)}, bf16[2048,1024]{1,0:T(8,128)(2,1)S(1)}, bf16[16,32,128]{2,1,0:T(8,128)(2,1)S(1)}, bf16[16,32,128]{2,1,0:T(8,128)(2,1)S(1)}, f32[16,1024]{1,0:T(8,128)S(1)}) custom-call(bf16[2048,1024]{1,0:T(8,128)(2,1)} %sig_hbm.1, bf16[2048,1024]{1,0:T(8,128)(2,1)} %cot_hbm.1, f32[16,2048]{1,0:T(8,128)S(1)} %copy-done), custom_call_target="tpu_custom_call" | custom-call | flops 8589934592 | bytes 8388608 | tf_op jit(solution)/shard_map/pallas_call | solution.py:463
  16.1 0.0 collective-permute-done.r1
  16.1 3.1 %collective-permute-done.1.r2 = bf16[2,2,256,128]{3,2,1,0:T(8,128)(2,1)S(1)} collective-permute-done((bf16[2,2,256,128]{3,2,1,0:T(8,128)(2,1)S(1)}, bf16[2,2,256,128]{3,2,1,0:T(8,128)(2,1)S(1)}, u32[]{:S(2)}, u32[]{:S(2)}) %collective-permute-start.1) | collective-permute-done | bytes 262176 | tf_op jit(solution)/shard_map/ppermute | solution.py:521
  19.3 1.6 %collective-permute-start.3 = (bf16[4,2,256,128]{3,2,1,0:T(8,128)(2,1)S(1)}, bf16[4,2,256,128]{3,2,1,0:T(8,128)(2,1)S(1)}, u32[]{:S(2)}, u32[]{:S(2)}) collective-permute-start(bf16[4,2,256,128]{3,2,1,0:T(8,128)(2,1)S(1)} %shard_map.94), channel_id=1, source_target_pairs={{0,1},{1,0},{2,3},{3,2},{4,5},{5,4},{6,7},{7,6},{8,9},{9,8},{10,11... | collective-permute-start | bytes 1572872 | tf_op jit(solution)/shard_map/ppermute | solution.py:540
  20.9 1.5 %collective-permute-done.3.other = bf16[4,2,256,128]{3,2,1,0:T(8,128)(2,1)S(1)} collective-permute-done((bf16[4,2,256,128]{3,2,1,0:T(8,128)(2,1)S(1)}, bf16[4,2,256,128]{3,2,1,0:T(8,128)(2,1)S(1)}, u32[]{:S(2)}, u32[]{:S(2)}) %collective-permute-start.3) | collective-permute-done | bytes 524320 | tf_op jit(solution)/shard_map/ppermute | solution.py:540
  22.4 3.2 %shard_map.95 = (bf16[8,2,256,128]{3,2,1,0:T(8,128)(2,1)S(1)}, bf16[2,128,2048]{2,1,0:T(8,128)(2,1)S(1)}, bf16[17,128,1024]{2,1,0:T(8,128)(2,1)S(1)}, bf16[16,12...) custom-call(bf16[2048,1024]{1,0:T(8,128)(2,1)S(1)} %get-tuple-element.33.us_ref, ...), custom_call_target="tpu_custom_call" | custom-call | tf_op jit(solution)/shard_map/pallas_call | solution.py:463
  25.7 0.1 convert.15
  25.8 0.1 slice_bitcast_fusion.8
  25.9 2.5 %collective-permute-start.6 = (f16[272,256]{1,0:T(8,128)(2,1)S(1)}, f16[272,256]{1,0:T(8,128)(2,1)S(1)}, u32[]{:S(2)}, u32[]{:S(2)}) collective-permute-start(f16[272,256]{1,0:T(8,128)(2,1)S(1)} %get-tuple-element.68), channel_id=1, source_target_pairs={{0,24},{8,0},{16,8},{24,16},{32,56},{40,32},{48,40},{56,48},{64,88... | collective-permute-start | bytes 417800 | tf_op jit(solution)/shard_map/ppermute | solution.py:504
  28.4 0.5 collective-permute-start.5
  28.9 0.6 collective-permute-start.4
  29.5 0.9 %shard_map.96 = (bf16[17,128,1024]{2,1,0:T(8,128)(2,1)S(1)}, bf16[16,128,1024]{2,1,0:T(8,128)(2,1)S(1)}, f32[272,256]{1,0:T(8,128)S(1)}) custom-call(bf16[2048,1024]{1,0:T(8,128)(2,1)S(1)} %get-tuple-element.33.us_ref, bf16[2048,1024]{1,0:T(8,128)(2,1)S(1)} %get-tuple-element.34.vs_ref, ...), custom_call_target="tpu_custom_call", output_to_operand_aliasing={{0}: (4, {}), {1}: (5, {})} | custom-call | flops 2147483648 | bytes 8388608 | tf_op jit(solution)/shard_map/pallas_call | solution.py:463
  30.4 6.6 %shard_map.97 = (f32[16,2,128,128]{3,2,1,0:T(8,128)S(1)}, bf16[1024,128]{1,0:T(8,128)(2,1)S(1)}) custom-call(bf16[2048,1024]{1,0:T(8,128)(2,1)S(1)} %get-tuple-element.33.us_ref, bf16[2048,1024]{1,0:T(8,128)(2,1)S(1)} %get-tuple-element.34.vs_ref, bf16[8,2,256,128]{3,2,1,0:T(8,128)(2,1)S(1)} %get-tuple-element.40.x_ref, ...), custom_call_target="tpu_custom_call" | custom-call | flops 8589934592 | bytes 8388608 | tf_op jit(solution)/shard_map/pallas_call | solution.py:463
  37.0 0.0 collective-permute-done.6
  37.1 1.4 %collective-permute-done.4 = f16[272,256]{1,0:T(8,128)(2,1)S(1)} collective-permute-done((f16[272,256]{1,0:T(8,128)(2,1)S(1)}, f16[272,256]{1,0:T(8,128)(2,1)S(1)}, u32[]{:S(2)}, u32[]{:S(2)}) %collective-permute-start.4) | collective-permute-done | bytes 139296 | tf_op jit(solution)/shard_map/ppermute | solution.py:504
  38.5 0.2 shard_map.98
  38.7 2.8 %collective-permute-start.9 = (f16[144,256]{1,0:T(8,128)(2,1)S(1)}, f16[144,256]{1,0:T(8,128)(2,1)S(1)}, u32[]{:S(2)}, u32[]{:S(2)}) collective-permute-start(f16[144,256]{1,0:T(8,128)(2,1)S(1)} %get-tuple-element.71), channel_id=1, source_target_pairs={{0,96},{8,104},{16,112},{24,120},{32,0},{40,8},{48,16},{56,24},{64... | collective-permute-start | bytes 221192 | tf_op jit(solution)/shard_map/ppermute | solution.py:504
  41.5 0.4 collective-permute-start.8
  41.9 0.7 collective-permute-start.7
  42.6 0.4 collective-permute-done.9
  43.0 3.4 %collective-permute-done.8 = f16[144,256]{1,0:T(8,128)(2,1)S(1)} collective-permute-done((f16[144,256]{1,0:T(8,128)(2,1)S(1)}, f16[144,256]{1,0:T(8,128)(2,1)S(1)}, u32[]{:S(2)}, u32[]{:S(2)}) %collective-permute-start.8) | collective-permute-done | bytes 73760 | tf_op jit(solution)/shard_map/ppermute | solution.py:504
  46.3 1.9 %collective-permute-done.7 = f16[144,256]{1,0:T(8,128)(2,1)S(1)} collective-permute-done((f16[144,256]{1,0:T(8,128)(2,1)S(1)}, f16[144,256]{1,0:T(8,128)(2,1)S(1)}, u32[]{:S(2)}, u32[]{:S(2)}) %collective-permute-start.7) | collective-permute-done | bytes 73760 | tf_op jit(solution)/shard_map/ppermute | solution.py:504
  48.2 0.7 shard_map.99
  48.9 0.1 convert.17
  49.0 0.1 slice_bitcast_fusion.5
  49.1 0.1 collective-permute-start.12
  49.2 0.8 collective-permute-start.11
  50.0 0.6 collective-permute-start.10
  50.6 2.4 %collective-permute-done.12 = f16[272,256]{1,0:T(8,128)(2,1)S(1)} collective-permute-done((f16[272,256]{1,0:T(8,128)(2,1)S(1)}, f16[272,256]{1,0:T(8,128)(2,1)S(1)}, u32[]{:S(2)}, u32[]{:S(2)}) %collective-permute-start.12) | collective-permute-done | bytes 139296 | tf_op jit(solution)/shard_map/ppermute | solution.py:504
  53.1 1.6 %collective-permute-done.11 = f16[272,256]{1,0:T(8,128)(2,1)S(1)} collective-permute-done((f16[272,256]{1,0:T(8,128)(2,1)S(1)}, f16[272,256]{1,0:T(8,128)(2,1)S(1)}, u32[]{:S(2)}, u32[]{:S(2)}) %collective-permute-start.11) | collective-permute-done | bytes 139296 | tf_op jit(solution)/shard_map/ppermute | solution.py:504
  54.8 1.8 %collective-permute-done.10 = f16[272,256]{1,0:T(8,128)(2,1)S(1)} collective-permute-done((f16[272,256]{1,0:T(8,128)(2,1)S(1)}, f16[272,256]{1,0:T(8,128)(2,1)S(1)}, u32[]{:S(2)}, u32[]{:S(2)}) %collective-permute-start.10) | collective-permute-done | bytes 139296 | tf_op jit(solution)/shard_map/ppermute | solution.py:504
  56.6 4.3 %shard_map.100 = (bf16[4,2,2,256,128]{4,3,2,1,0:T(8,128)(2,1)S(1)}, bf16[16,128,1024]{2,1,0:T(8,128)(2,1)S(1)}, bf16[16,128,1024]{2,1,0:T(8,128)(2,1)S(1)}, f32[16,1024]{1,0:T(8,128)S(1)}) custom-call(bf16[2048,1024]{1,0:T(8,128)(2,1)S(1)} %get-tuple-element.33.us_ref, bf16[2048,1024]{1,0:T(8,128)(2,1)S(1)} %get-tuple-element.34.vs_ref, ...), custom_call_target="tpu_custom_call" | custom-call | tf_op jit(solution)/shard_map/pallas_call | solution.py:463
  60.9 0.1 slice_bitcast_fusion.1
  61.0 2.0 %collective-permute-start.15 = (bf16[2,2,256,128]{3,2,1,0:T(8,128)(2,1)S(1)}, bf16[2,2,256,128]{3,2,1,0:T(8,128)(2,1)S(1)}, u32[]{:S(2)}, u32[]{:S(2)}) collective-permute-start(bf16[2,2,256,128]{3,2,1,0:T(8,128)(2,1)S(1)} %get-tuple-element.61), channel_id=1, source_target_pairs={{0,6},{1,7},{2,0},{3,1},{4,2},{5,3},{6,4},{7,5},{8,14},{9,15},{10,... | collective-permute-start | bytes 786440 | tf_op jit(solution)/shard_map/ppermute | solution.py:587
  63.0 0.9 %collective-permute-start.14 = (bf16[2,2,256,128]{3,2,1,0:T(8,128)(2,1)S(1)}, bf16[2,2,256,128]{3,2,1,0:T(8,128)(2,1)S(1)}, u32[]{:S(2)}, u32[]{:S(2)}) collective-permute-start(bf16[2,2,256,128]{3,2,1,0:T(8,128)(2,1)S(1)} %get-tuple-element.62), channel_id=1, source_target_pairs={{0,4},{1,5},{2,6},{3,7},{4,0},{5,1},{6,2},{7,3},{8,12},{9,13},{10,... | collective-permute-start | bytes 786440 | tf_op jit(solution)/shard_map/ppermute | solution.py:587
  63.8 0.1 collective-permute-start.13
  64.0 9.5 %shard_map.101 = (bf16[2048,1024]{1,0:T(8,128)(2,1)}, bf16[2048,1024]{1,0:T(8,128)(2,1)}, bf16[2048,1024]{1,0:T(8,128)(2,1)S(1)}) custom-call(bf16[2048,1024]{1,0:T(8,128)(2,1)S(1)} %get-tuple-element.33.us_ref, bf16[2048,1024]{1,0:T(8,128)(2,1)S(1)} %get-tuple-element.34.vs_ref, bf16[16,128,1024]{2,1,0:T(8,128)(2,1)S(1)} %get-tuple-element.49.start_ref, ...), custom_call_target="tpu_custom_call" | custom-call | flops 17179869184 | bytes 8388608 | tf_op jit(solution)/shard_map/pallas_call | solution.py:463
  73.5 1.6 %shard_map.102.after_hbm.first_ref = f32[16,1024]{1,0:T(8,128)S(1)} custom-call(bf16[2048,1024]{1,0:T(8,128)(2,1)S(1)} %get-tuple-element.56.diff_ref, f32[16,1024]{1,0:T(8,128)S(1)} %get-tuple-element.57.total_ref, bf16[1024,128]{1,0:T(8,128)(2,1)S(1)} %get-tuple-element.58.of_ref), custom_call_target="tpu_custom_call" | custom-call | tf_op jit(solution)/shard_map/pallas_call | solution.py:463
  75.1 0.0 collective-permute-done.14.r2
  75.2 1.1 %collective-permute-done.13.r1 = bf16[2,2,256,128]{3,2,1,0:T(8,128)(2,1)S(1)} collective-permute-done((bf16[2,2,256,128]{3,2,1,0:T(8,128)(2,1)S(1)}, bf16[2,2,256,128]{3,2,1,0:T(8,128)(2,1)S(1)}, u32[]{:S(2)}, u32[]{:S(2)}) %collective-permute-start.13) | collective-permute-done | bytes 262176 | tf_op jit(solution)/shard_map/ppermute | solution.py:587
  76.3 3.5 %collective-permute-start.16 = (bf16[4,2,256,128]{3,2,1,0:T(8,128)(2,1)S(1)}, bf16[4,2,256,128]{3,2,1,0:T(8,128)(2,1)S(1)}, u32[]{:S(2)}, u32[]{:S(2)}) collective-permute-start(bf16[4,2,256,128]{3,2,1,0:T(8,128)(2,1)S(1)} %shard_map.103), channel_id=1, source_target_pairs={{0,1},{1,0},{2,3},{3,2},{4,5},{5,4},{6,7},{7,6},{8,9},{9,8},{10,11... | collective-permute-start | bytes 1572872 | tf_op jit(solution)/shard_map/ppermute | solution.py:601
  79.8 2.3 %shard_map.104.after_hbm = f32[16,2048]{1,0:T(8,128)} custom-call(bf16[2048,1024]{1,0:T(8,128)(2,1)S(1)} %get-tuple-element.56.diff_ref, f32[16,1024]{1,0:T(8,128)S(1)} %get-tuple-element.57.total_ref, bf16[1024,128]{1,0:T(8,128)(2,1)S(1)} %get-tuple-element.58.of_ref, f32[16,1024]{1,0:T(8,128)S(1)} %shard_map.102.after_hbm.first_ref), custom_call_target="tpu_custom_call" | custom-call | flops 2147483648 | bytes 4194304 | tf_op jit(solution)/shard_map/pallas_call | solution.py:463
  82.1 1.3 %shard_map.105 = (bf16[256,1024]{1,0:T(8,128)(2,1)}, bf16[256,1024]{1,0:T(8,128)(2,1)}) custom-call(bf16[2,2,256,128]{3,2,1,0:T(8,128)(2,1)S(1)} %get-tuple-element.64.r0, bf16[2,2,256,128]{3,2,1,0:T(8,128)(2,1)S(1)} %collective-permute-done.13.r1, bf16[2,2,256,128]{3,2,1,0:T(8,128)(2,1)S(1)} %collective-permute-done.14.r2, ...), custom_call_target="tpu_custom_call" | custom-call | tf_op jit(solution)/shard_map/pallas_call | solution.py:463
  (19 shorter events, 0.3 us)
Async XLA Ops:
  2.1 14.0 %collective-permute-start = (bf16[2,2,256,128]{3,2,1,0:T(8,128)(2,1)S(1)}, bf16[2,2,256,128]{3,2,1,0:T(8,128)(2,1)S(1)}, u32[]{:S(2)}, u32[]{:S(2)}) collective-permute-start(bf16[2,2,256,128]{3,2,1,0:T(8,128)(2,1)S(1)} %get-tuple-element.36), channel_id=1, source_target_pairs={{0,2},{1,3},{2,4},{3,5},{4,6},{5,7},{6,0},{7,1},{8,10},{9,11},{10,... | collective-permute-start | bytes 786440 | tf_op jit(solution)/shard_map/ppermute | solution.py:521
  4.6 14.6 %collective-permute-start.1 = (bf16[2,2,256,128]{3,2,1,0:T(8,128)(2,1)S(1)}, bf16[2,2,256,128]{3,2,1,0:T(8,128)(2,1)S(1)}, u32[]{:S(2)}, u32[]{:S(2)}) collective-permute-start(bf16[2,2,256,128]{3,2,1,0:T(8,128)(2,1)S(1)} %get-tuple-element.37), channel_id=1, source_target_pairs={{0,4},{1,5},{2,6},{3,7},{4,0},{5,1},{6,2},{7,3},{8,12},{9,13},{10,... | collective-permute-start | bytes 786440 | tf_op jit(solution)/shard_map/ppermute | solution.py:521
  7.9 11.3 %collective-permute-start.2 = (bf16[2,2,256,128]{3,2,1,0:T(8,128)(2,1)S(1)}, bf16[2,2,256,128]{3,2,1,0:T(8,128)(2,1)S(1)}, u32[]{:S(2)}, u32[]{:S(2)}) collective-permute-start(bf16[2,2,256,128]{3,2,1,0:T(8,128)(2,1)S(1)} %get-tuple-element.38), channel_id=1, source_target_pairs={{0,6},{1,7},{2,0},{3,1},{4,2},{5,3},{6,4},{7,5},{8,14},{9,15},{10,... | collective-permute-start | bytes 786440 | tf_op jit(solution)/shard_map/ppermute | solution.py:521
  8.6 0.9 %copy-start = (f32[16,2048]{1,0:T(8,128)S(1)}, f32[16,2048]{1,0:T(8,128)}, u32[]{:S(2)}) copy-start(f32[16,2048]{1,0:T(8,128)} %ld_ref.1) | copy-start | bytes 393220
  19.3 3.2 %collective-permute-start.3 = (bf16[4,2,256,128]{3,2,1,0:T(8,128)(2,1)S(1)}, bf16[4,2,256,128]{3,2,1,0:T(8,128)(2,1)S(1)}, u32[]{:S(2)}, u32[]{:S(2)}) collective-permute-start(bf16[4,2,256,128]{3,2,1,0:T(8,128)(2,1)S(1)} %shard_map.94), channel_id=1, source_target_pairs={{0,1},{1,0},{2,3},{3,2},{4,5},{5,4},{6,7},{7,6},{8,9},{9,8},{10,11... | collective-permute-start | bytes 1572872 | tf_op jit(solution)/shard_map/ppermute | solution.py:540
  25.9 11.1 %collective-permute-start.6 = (f16[272,256]{1,0:T(8,128)(2,1)S(1)}, f16[272,256]{1,0:T(8,128)(2,1)S(1)}, u32[]{:S(2)}, u32[]{:S(2)}) collective-permute-start(f16[272,256]{1,0:T(8,128)(2,1)S(1)} %get-tuple-element.68), channel_id=1, source_target_pairs={{0,24},{8,0},{16,8},{24,16},{32,56},{40,32},{48,40},{56,48},{64,88... | collective-permute-start | bytes 417800 | tf_op jit(solution)/shard_map/ppermute | solution.py:504
  28.4 8.7 %collective-permute-start.5 = (f16[272,256]{1,0:T(8,128)(2,1)S(1)}, f16[272,256]{1,0:T(8,128)(2,1)S(1)}, u32[]{:S(2)}, u32[]{:S(2)}) collective-permute-start(f16[272,256]{1,0:T(8,128)(2,1)S(1)} %get-tuple-element.69), channel_id=1, source_target_pairs={{0,16},{8,24},{16,0},{24,8},{32,48},{40,56},{48,32},{56,40},{64,80... | collective-permute-start | bytes 417800 | tf_op jit(solution)/shard_map/ppermute | solution.py:504
  28.9 9.6 %collective-permute-start.4 = (f16[272,256]{1,0:T(8,128)(2,1)S(1)}, f16[272,256]{1,0:T(8,128)(2,1)S(1)}, u32[]{:S(2)}, u32[]{:S(2)}) collective-permute-start(f16[272,256]{1,0:T(8,128)(2,1)S(1)} %get-tuple-element.70), channel_id=1, source_target_pairs={{0,8},{8,16},{16,24},{24,0},{32,40},{40,48},{48,56},{56,32},{64,72... | collective-permute-start | bytes 417800 | tf_op jit(solution)/shard_map/ppermute | solution.py:504
  38.7 4.2 %collective-permute-start.9 = (f16[144,256]{1,0:T(8,128)(2,1)S(1)}, f16[144,256]{1,0:T(8,128)(2,1)S(1)}, u32[]{:S(2)}, u32[]{:S(2)}) collective-permute-start(f16[144,256]{1,0:T(8,128)(2,1)S(1)} %get-tuple-element.71), channel_id=1, source_target_pairs={{0,96},{8,104},{16,112},{24,120},{32,0},{40,8},{48,16},{56,24},{64... | collective-permute-start | bytes 221192 | tf_op jit(solution)/shard_map/ppermute | solution.py:504
  41.5 4.8 %collective-permute-start.8 = (f16[144,256]{1,0:T(8,128)(2,1)S(1)}, f16[144,256]{1,0:T(8,128)(2,1)S(1)}, u32[]{:S(2)}, u32[]{:S(2)}) collective-permute-start(f16[144,256]{1,0:T(8,128)(2,1)S(1)} %get-tuple-element.72), channel_id=1, source_target_pairs={{0,64},{8,72},{16,80},{24,88},{32,96},{40,104},{48,112},{56,120},{... | collective-permute-start | bytes 221192 | tf_op jit(solution)/shard_map/ppermute | solution.py:504
  41.9 6.3 %collective-permute-start.7 = (f16[144,256]{1,0:T(8,128)(2,1)S(1)}, f16[144,256]{1,0:T(8,128)(2,1)S(1)}, u32[]{:S(2)}, u32[]{:S(2)}) collective-permute-start(f16[144,256]{1,0:T(8,128)(2,1)S(1)} %get-tuple-element.73), channel_id=1, source_target_pairs={{0,32},{8,40},{16,48},{24,56},{32,64},{40,72},{48,80},{56,88},{64,... | collective-permute-start | bytes 221192 | tf_op jit(solution)/shard_map/ppermute | solution.py:504
  49.1 4.0 %collective-permute-start.12 = (f16[272,256]{1,0:T(8,128)(2,1)S(1)}, f16[272,256]{1,0:T(8,128)(2,1)S(1)}, u32[]{:S(2)}, u32[]{:S(2)}) collective-permute-start(f16[272,256]{1,0:T(8,128)(2,1)S(1)} %get-tuple-element.65), channel_id=1, source_target_pairs={{0,24},{8,0},{16,8},{24,16},{32,56},{40,32},{48,40},{56,48},{64,88... | collective-permute-start | bytes 417800 | tf_op jit(solution)/shard_map/ppermute | solution.py:504
  49.2 5.6 %collective-permute-start.11 = (f16[272,256]{1,0:T(8,128)(2,1)S(1)}, f16[272,256]{1,0:T(8,128)(2,1)S(1)}, u32[]{:S(2)}, u32[]{:S(2)}) collective-permute-start(f16[272,256]{1,0:T(8,128)(2,1)S(1)} %get-tuple-element.66), channel_id=1, source_target_pairs={{0,16},{8,24},{16,0},{24,8},{32,48},{40,56},{48,32},{56,40},{64,80... | collective-permute-start | bytes 417800 | tf_op jit(solution)/shard_map/ppermute | solution.py:504
  50.0 6.6 %collective-permute-start.10 = (f16[272,256]{1,0:T(8,128)(2,1)S(1)}, f16[272,256]{1,0:T(8,128)(2,1)S(1)}, u32[]{:S(2)}, u32[]{:S(2)}) collective-permute-start(f16[272,256]{1,0:T(8,128)(2,1)S(1)} %get-tuple-element.67), channel_id=1, source_target_pairs={{0,8},{8,16},{16,24},{24,0},{32,40},{40,48},{48,56},{56,32},{64,72... | collective-permute-start | bytes 417800 | tf_op jit(solution)/shard_map/ppermute | solution.py:504
  61.0 14.1 %collective-permute-start.15 = (bf16[2,2,256,128]{3,2,1,0:T(8,128)(2,1)S(1)}, bf16[2,2,256,128]{3,2,1,0:T(8,128)(2,1)S(1)}, u32[]{:S(2)}, u32[]{:S(2)}) collective-permute-start(bf16[2,2,256,128]{3,2,1,0:T(8,128)(2,1)S(1)} %get-tuple-element.61), channel_id=1, source_target_pairs={{0,6},{1,7},{2,0},{3,1},{4,2},{5,3},{6,4},{7,5},{8,14},{9,15},{10,... | collective-permute-start | bytes 786440 | tf_op jit(solution)/shard_map/ppermute | solution.py:587
  63.0 12.2 %collective-permute-start.14 = (bf16[2,2,256,128]{3,2,1,0:T(8,128)(2,1)S(1)}, bf16[2,2,256,128]{3,2,1,0:T(8,128)(2,1)S(1)}, u32[]{:S(2)}, u32[]{:S(2)}) collective-permute-start(bf16[2,2,256,128]{3,2,1,0:T(8,128)(2,1)S(1)} %get-tuple-element.62), channel_id=1, source_target_pairs={{0,4},{1,5},{2,6},{3,7},{4,0},{5,1},{6,2},{7,3},{8,12},{9,13},{10,... | collective-permute-start | bytes 786440 | tf_op jit(solution)/shard_map/ppermute | solution.py:587
  63.8 12.4 %collective-permute-start.13 = (bf16[2,2,256,128]{3,2,1,0:T(8,128)(2,1)S(1)}, bf16[2,2,256,128]{3,2,1,0:T(8,128)(2,1)S(1)}, u32[]{:S(2)}, u32[]{:S(2)}) collective-permute-start(bf16[2,2,256,128]{3,2,1,0:T(8,128)(2,1)S(1)} %get-tuple-element.63), channel_id=1, source_target_pairs={{0,2},{1,3},{2,4},{3,5},{4,6},{5,7},{6,0},{7,1},{8,10},{9,11},{10,... | collective-permute-start | bytes 786440 | tf_op jit(solution)/shard_map/ppermute | solution.py:587
  76.3 5.8 %collective-permute-start.16 = (bf16[4,2,256,128]{3,2,1,0:T(8,128)(2,1)S(1)}, bf16[4,2,256,128]{3,2,1,0:T(8,128)(2,1)S(1)}, u32[]{:S(2)}, u32[]{:S(2)}) collective-permute-start(bf16[4,2,256,128]{3,2,1,0:T(8,128)(2,1)S(1)} %shard_map.103), channel_id=1, source_target_pairs={{0,1},{1,0},{2,3},{3,2},{4,5},{5,4},{6,7},{7,6},{8,9},{9,8},{10,11... | collective-permute-start | bytes 1572872 | tf_op jit(solution)/shard_map/ppermute | solution.py:601

commit v3 on v2

--- a/solution.py
+++ b/solution.py
@@ -396,62 +396,79 @@
             copy.wait()
 
 
-def decay_part(k, diff_ref, total_ref, of_ref, decay_ref):
-    own = one_hot(lane_heads(HEADS))
+def decay_part(k, diff_ref, heads_ref, of_ref, decay_ref):
     from_on = one_hot(iota((C, C), 0) >= iota((C, C), 1))
     last = iota((HEADS, C), 1) == C - 1
-    totals = sum(dot_nt(own, part) for part in split3(total_ref[...]))
     cum_grad = dot(diff_ref[4 * k * C : 4 * (k + 1) * C, :], of_ref[...])
     parts = []
     for j in range(4):
-        total = totals[:, 4 * k + j : 4 * k + j + 1]
+        total = heads_ref[:, 4 * k + j : 4 * k + j + 1]
         parts.append(cum_grad[j * C : (j + 1) * C].T[0:HEADS] + jnp.where(last, total, 0.0))
     sums = sum(dot(part, from_on) for part in split3(jnp.concatenate(parts, axis=0)))
     for j in range(4):
         decay_ref[:, (4 * k + j) * C : (4 * k + j + 1) * C] = sums[j * HEADS : (j + 1) * HEADS]
 
 
-def first_decay_kernel(diff_ref, total_ref, of_ref, decay_ref):
+def first_decay_kernel(diff_ref, total_ref, of_ref, decay_ref, heads_ref):
+    own = one_hot(lane_heads(HEADS))
+    heads_ref[...] = sum(dot_nt(own, part) for part in split3(total_ref[...]))
     for k in range(2):
-        decay_part(k, diff_ref, total_ref, of_ref, decay_ref)
-
-
-def decay_kernel(diff_ref, total_ref, of_ref, first_ref, decay_ref):
+        decay_part(k, diff_ref, heads_ref, of_ref, decay_ref)
+
+
+def decay_kernel(diff_ref, heads_ref, of_ref, first_ref, decay_ref):
     decay_ref[:, 0 : TOKENS // 2] = first_ref[...]
     for k in range(2, 4):
-        decay_part(k, diff_ref, total_ref, of_ref, decay_ref)
-
-
-def split_kernel(in_hbm, out_hbm, s0, s1, s2, s3, sems):
+        decay_part(k, diff_ref, heads_ref, of_ref, decay_ref)
+
+
+def split_copies(d, in_hbm, out_hbm, ref, sems):
     z, core, homes = head_places()
     copies = []
-    for d, ref in enumerate((s0, s1, s2, s3)):
-        for to in range(2):
-            group = 2 * lax.rem(z + d, ROW) + to
-            columns = pl.ds(pl.multiple_of(group * N, N), N)
-            for i, source in enumerate((in_hbm, out_hbm)):
-                copies.append(pltpu.make_async_copy(source.at[:, columns], ref.at[to, i], sems.at[d, to, i]))
+    for to in range(2):
+        group = 2 * lax.rem(z + d, ROW) + to
+        columns = pl.ds(pl.multiple_of(group * N, N), N)
+        for i, source in enumerate((in_hbm, out_hbm)):
+            copies.append(pltpu.make_async_copy(source.at[:, columns], ref.at[to, i], sems.at[d, to, i]))
+    return copies
+
+
+def far_kernel(in_hbm, out_hbm, ld_hbm, s2, ld_ref, sems, sem):
+    copies = split_copies(2, in_hbm, out_hbm, s2, sems) + [pltpu.make_async_copy(ld_hbm, ld_ref, sem)]
     for copy in copies:
         copy.start()
     for copy in copies:
         copy.wait()
 
 
+def split_kernel(in_hbm, out_hbm, s2, s0, s1, s3, sems):
+    copies = []
+    for d, ref in ((1, s1), (3, s3), (0, s0)):
+        copies += split_copies(d, in_hbm, out_hbm, ref, sems)
+    for copy in copies:
+        copy.start()
+    for copy in copies:
+        copy.wait()
+
+
 def swap_kernel(r0, r1, r2, r3, after_hbm, other_ref):
     z, core, homes = head_places()
     for d, ref in enumerate((r0, r1, r2, r3)):
         other_ref[d] = ref[1 - core]
 
 
-def join_kernel(r0, r1, r2, r3, other, after_hbm, in_ref, out_ref):
+def join_kernel(r0, r1, r2, r3, other, after_hbm, in_hbm, out_hbm, sems):
     z, core, homes = head_places()
+    copies = []
     for d, ref in enumerate((r0, r1, r2, r3)):
-        columns = pl.ds(pl.multiple_of((2 * homes[d] + core) * N, N), N)
-        in_ref[:, columns] = ref[core, 0]
-        out_ref[:, columns] = ref[core, 1]
-        columns = pl.ds(pl.multiple_of((2 * homes[d] + 1 - core) * N, N), N)
-        in_ref[:, columns] = other[d, 0]
-        out_ref[:, columns] = other[d, 1]
+        for k, (source, of_core) in enumerate(((ref.at[core], core), (other.at[d], 1 - core))):
+            columns = pl.ds(pl.multiple_of((2 * homes[d] + of_core) * N, N), N)
+            for i, result in enumerate((in_hbm, out_hbm)):
+                copies.append(pltpu.make_async_copy(source.at[i], result.at[:, columns], sems.at[d, k, i]))
+    for copy in copies:
+        copy.start()
+    for copy in copies:
+        copy.wait()
 
 
 VMEM = pl.BlockSpec(memory_space=pltpu.VMEM)
@@ -515,14 +532,23 @@
     states = (PIECES, N, LANES)
     band = (C, LANES)
 
-    sent = call(
-        split_kernel, (far(state_in), far(state_out)), [held(chip)] * ROW, [HBM] * 2, [VMEM] * ROW, [DMA((ROW, 2, 2))]
-    )
-    got = [sent[0]] + [lax.ppermute(sent[d], "head", along_z(d)) for d in (1, 3, 2)]
-    got = [got[0], got[1], got[3], got[2]]
+    marks = DMA((ROW, 2, 2))
+    s2, decays = call(
+        far_kernel,
+        (far(state_in), far(state_out), far(log_decay)),
+        (held(chip), held(log_decay.shape, F32)),
+        [HBM] * 3,
+        [VMEM] * 2,
+        [marks, DMA],
+    )
+    r2 = lax.ppermute(s2, "head", along_z(2))
+    s0, s1, s3 = call(
+        split_kernel, (far(state_in), far(state_out), s2), [held(chip)] * 3, [HBM] * 2 + [VMEM], [VMEM] * 3, [marks]
+    )
+    got = [s0, lax.ppermute(s1, "head", along_z(1)), r2, lax.ppermute(s3, "head", along_z(3))]
     us, vs, u2, v2, half = call(
         scale_kernel,
-        (far(signal), far(cotangent), log_decay),
+        (far(signal), far(cotangent), decays),
         (
             held(wide),
             held(wide),
@@ -572,8 +598,8 @@
         flops=1 << 33,
         moved=1 << 23,
     )
-    totals = call(row_kernel, mates + [base], held((ROW - 1, N + 16, SLICE), F32), [VMEM] * 5, VMEM)
-    rows = [send(totals[d - 1], along_y(d)) for d in range(1, ROW)]
+    row_totals = call(row_kernel, mates + [base], held((ROW - 1, N + 16, SLICE), F32), [VMEM] * 5, VMEM)
+    rows = [send(row_totals[d - 1], along_y(d)) for d in range(1, ROW)]
     back = call(enter_kernel, mates + rows, held((ROW, 2 * N + 16, SLICE), F32), [VMEM] * 7, VMEM)
     shares = [back[0]] + [send(back[e], along_x(e)) for e in range(1, ROW)]
     grads, start, behind, total = call(
@@ -596,15 +622,21 @@
         flops=1 << 34,
         moved=1 << 23,
     )
-    decay = call(first_decay_kernel, (diff, total, of_head), held((HEADS, TOKENS // 2), F32), [VMEM] * 3, VMEM)
+    decay, totals = call(
+        first_decay_kernel,
+        (diff, total, of_head),
+        (held((HEADS, TOKENS // 2), F32), held((HEADS, PIECES), F32)),
+        [VMEM] * 3,
+        [VMEM] * 2,
+    )
     other = call(swap_kernel, returned + [decay], held((ROW, 2, own, N)), [VMEM] * 5, VMEM)
     other = lax.ppermute(other, "head", OTHER_CORE)
     grad_decay = call(
-        decay_kernel, (diff, total, of_head, decay), plain((HEADS, TOKENS), F32), [VMEM] * 4, VMEM, flops=1 << 31, moved=1 << 22
+        decay_kernel, (diff, totals, of_head, decay), plain((HEADS, TOKENS), F32), [VMEM] * 4, VMEM, flops=1 << 31, moved=1 << 22
     )
     narrow = plain(state_in.shape)
     grad_in, grad_out = call(
-        join_kernel, returned + [other, far(grad_decay)], (narrow, narrow), [VMEM] * 5 + [HBM], [VMEM] * 2
+        join_kernel, returned + [other, far(grad_decay)], (narrow, narrow), [VMEM] * 5 + [HBM], [HBM] * 2, [marks]
     )
     return output, grad_signal, grad_in, grad_out, grad_decay
 

time: 83.7 us -> 83 us (level)
  waiting for transfers between devices: 18.7 us -> 17.4 us
  local copies, waits for them, and re-layouts: 1.22 us -> 0.32 us
    ppermute x3, waiting for transfers between devices: 3.12 us -> 1.5 us  [the longest x1 1.49 us: body(): lax.ppermute(s1, 'head', along_z(1))]
    unnamed x2 -> x0, local copies, waits for them, and re-layouts: 0.9 us -> none
    pallas_call x14 -> x15, Pallas kernels: 38.7 us -> 39.5 us  [call(): pl.pallas_call(kernel, out_shape=outs, in_specs=specs, out_specs=out_spec...]
  transfers between devices with their start and end apart: 17 -> 17, of which waited for: 10 -> 10; matrix products, arithmetic and copies ran while one was open for 0% -> 0% of each run, Pallas kernels for 33% -> 35%
where the time goes in v3:
time: 83 us; the launch traced here: 82.7 us
  Pallas kernels  39.5 us (48%)
  starting transfers between devices  24.1 us (29%)
  waiting for transfers between devices  17.4 us (21%)
  between operations  1.02 us (1%)
    pallas_call x15, Pallas kernels, call(): pl.pallas_call(kernel, out_shape=outs, in_specs=specs, out_specs=out_spec...  39.5 us
    ppermute x9, waiting for transfers between devices, send(): return lax.ppermute(a.astype(jnp.float16), 'ctx', pairs).astype(F32)  12.9 us
    ppermute x9, starting transfers between devices, send(): return lax.ppermute(a.astype(jnp.float16), 'ctx', pairs).astype(F32)  8.98 us
    ppermute x2, starting transfers between devices, body(): other = lax.ppermute(other, 'head', OTHER_CORE)  4.7 us
    ppermute x1, starting transfers between devices, body(): r2 = lax.ppermute(s2, 'head', along_z(2))  4.51 us
    ppermute x3, starting transfers between devices, body(): lax.ppermute(grads[d], 'head', along_z(d))  3.21 us
    ppermute x1, starting transfers between devices, body(): lax.ppermute(s3, 'head', along_z(3))  1.94 us
  transfers between devices with their start and end apart: 17, of which 10 were waited for; matrix products, arithmetic and copies ran while one was open for 0% of the time, Pallas kernels for 35%

profile of v3, /device:TPU:1, one launch (start us, length us, event | category | flops | bytes accessed | tf_op | source)
XLA Modules:
  0.0 82.7 jit_solution(7810534176096451258)
XLA Ops:
  0.6 1.2 %shard_map.92 = (bf16[2,2,256,128]{3,2,1,0:T(8,128)(2,1)S(1)}, f32[16,2048]{1,0:T(8,128)S(1)}) custom-call(bf16[256,1024]{1,0:T(8,128)(2,1)} %in_hbm.3, bf16[256,1024]{1,0:T(8,128)(2,1)} %out_hbm.3, f32[16,2048]{1,0:T(8,128)} %ld_hbm.1), custom_call_target="tpu_custom_call" | custom-call | tf_op jit(solution)/shard_map/pallas_call | solution.py:480
  1.8 4.5 %collective-permute-start.1 = (bf16[2,2,256,128]{3,2,1,0:T(8,128)(2,1)S(1)}, bf16[2,2,256,128]{3,2,1,0:T(8,128)(2,1)S(1)}, u32[]{:S(2)}, u32[]{:S(2)}) collective-permute-start(bf16[2,2,256,128]{3,2,1,0:T(8,128)(2,1)S(1)} %get-tuple-element.39.s2), channel_id=1, source_target_pairs={{0,4},{1,5},{2,6},{3,7},{4,0},{5,1},{6,2},{7,3},{8,12},{9,13},{10,... | collective-permute-start | bytes 786440 | tf_op jit(solution)/shard_map/ppermute | solution.py:544
  6.3 1.3 %shard_map.94 = (bf16[2,2,256,128]{3,2,1,0:T(8,128)(2,1)S(1)}, bf16[2,2,256,128]{3,2,1,0:T(8,128)(2,1)S(1)}, bf16[2,2,256,128]{3,2,1,0:T(8,128)(2,1)S(1)}) custom-call(bf16[256,1024]{1,0:T(8,128)(2,1)} %in_hbm.3, bf16[256,1024]{1,0:T(8,128)(2,1)} %out_hbm.3, bf16[2,2,256,128]{3,2,1,0:T(8,128)(2,1)S(1)} %get-tuple-element.39.s2), custom_call_target="tpu_custom_call" | custom-call | tf_op jit(solution)/shard_map/pallas_call | solution.py:480
  7.6 0.8 collective-permute-start
  8.4 1.9 %collective-permute-start.2 = (bf16[2,2,256,128]{3,2,1,0:T(8,128)(2,1)S(1)}, bf16[2,2,256,128]{3,2,1,0:T(8,128)(2,1)S(1)}, u32[]{:S(2)}, u32[]{:S(2)}) collective-permute-start(bf16[2,2,256,128]{3,2,1,0:T(8,128)(2,1)S(1)} %get-tuple-element.42), channel_id=1, source_target_pairs={{0,6},{1,7},{2,0},{3,1},{4,2},{5,3},{6,4},{7,5},{8,14},{9,15},{10,... | collective-permute-start | bytes 786440 | tf_op jit(solution)/shard_map/ppermute | solution.py:548
  10.4 6.6 %shard_map.93 = (bf16[2048,1024]{1,0:T(8,128)(2,1)S(1)}, bf16[2048,1024]{1,0:T(8,128)(2,1)S(1)}, bf16[16,32,128]{2,1,0:T(8,128)(2,1)S(1)}, bf16[16,32,128]{2,1,0:T(8,128)(2,1)S(1)}, f32[16,1024]{1,0:T(8,128)S(1)}) custom-call(bf16[2048,1024]{1,0:T(8,128)(2,1)} %sig_hbm.1, bf16[2048,1024]{1,0:T(8,128)(2,1)} %cot_hbm.1, f32[16,2048]{1,0:T(8,128)S(1)} %get-tuple-element.36.ld_ref), custom_call_target="tpu_custom_call" | custom-call | flops 8589934592 | bytes 8388608 | tf_op jit(solution)/shard_map/pallas_call | solution.py:480
  16.9 0.0 collective-permute-done.1.r2
  16.9 1.5 %collective-permute-done.r1 = bf16[2,2,256,128]{3,2,1,0:T(8,128)(2,1)S(1)} collective-permute-done((bf16[2,2,256,128]{3,2,1,0:T(8,128)(2,1)S(1)}, bf16[2,2,256,128]{3,2,1,0:T(8,128)(2,1)S(1)}, u32[]{:S(2)}, u32[]{:S(2)}) %collective-permute-start) | collective-permute-done | bytes 262176 | tf_op jit(solution)/shard_map/ppermute | solution.py:548
  18.5 1.5 %collective-permute-start.3 = (bf16[4,2,256,128]{3,2,1,0:T(8,128)(2,1)S(1)}, bf16[4,2,256,128]{3,2,1,0:T(8,128)(2,1)S(1)}, u32[]{:S(2)}, u32[]{:S(2)}) collective-permute-start(bf16[4,2,256,128]{3,2,1,0:T(8,128)(2,1)S(1)} %shard_map.95), channel_id=1, source_target_pairs={{0,1},{1,0},{2,3},{3,2},{4,5},{5,4},{6,7},{7,6},{8,9},{9,8},{10,11... | collective-permute-start | bytes 1572872 | tf_op jit(solution)/shard_map/ppermute | solution.py:566
  20.0 1.5 %collective-permute-done.3.other = bf16[4,2,256,128]{3,2,1,0:T(8,128)(2,1)S(1)} collective-permute-done((bf16[4,2,256,128]{3,2,1,0:T(8,128)(2,1)S(1)}, bf16[4,2,256,128]{3,2,1,0:T(8,128)(2,1)S(1)}, u32[]{:S(2)}, u32[]{:S(2)}) %collective-permute-start.3) | collective-permute-done | bytes 524320 | tf_op jit(solution)/shard_map/ppermute | solution.py:566
  21.6 3.2 %shard_map.96 = (bf16[8,2,256,128]{3,2,1,0:T(8,128)(2,1)S(1)}, bf16[2,128,2048]{2,1,0:T(8,128)(2,1)S(1)}, bf16[17,128,1024]{2,1,0:T(8,128)(2,1)S(1)}, bf16[16,12...) custom-call(bf16[2048,1024]{1,0:T(8,128)(2,1)S(1)} %get-tuple-element.37.us_ref, ...), custom_call_target="tpu_custom_call" | custom-call | tf_op jit(solution)/shard_map/pallas_call | solution.py:480
  24.8 0.1 convert.15
  24.9 0.1 slice_bitcast_fusion.8
  25.0 2.5 %collective-permute-start.6 = (f16[272,256]{1,0:T(8,128)(2,1)S(1)}, f16[272,256]{1,0:T(8,128)(2,1)S(1)}, u32[]{:S(2)}, u32[]{:S(2)}) collective-permute-start(f16[272,256]{1,0:T(8,128)(2,1)S(1)} %get-tuple-element.74), channel_id=1, source_target_pairs={{0,24},{8,0},{16,8},{24,16},{32,56},{40,32},{48,40},{56,48},{64,88... | collective-permute-start | bytes 417800 | tf_op jit(solution)/shard_map/ppermute | solution.py:521
  27.5 0.5 collective-permute-start.5
  28.0 0.6 collective-permute-start.4
  28.6 0.9 %shard_map.97 = (bf16[17,128,1024]{2,1,0:T(8,128)(2,1)S(1)}, bf16[16,128,1024]{2,1,0:T(8,128)(2,1)S(1)}, f32[272,256]{1,0:T(8,128)S(1)}) custom-call(bf16[2048,1024]{1,0:T(8,128)(2,1)S(1)} %get-tuple-element.37.us_ref, bf16[2048,1024]{1,0:T(8,128)(2,1)S(1)} %get-tuple-element.38.vs_ref, ...), custom_call_target="tpu_custom_call", output_to_operand_aliasing={{0}: (4, {}), {1}: (5, {})} | custom-call | flops 2147483648 | bytes 8388608 | tf_op jit(solution)/shard_map/pallas_call | solution.py:480
  29.5 6.6 %shard_map.98 = (f32[16,2,128,128]{3,2,1,0:T(8,128)S(1)}, bf16[1024,128]{1,0:T(8,128)(2,1)S(1)}) custom-call(bf16[2048,1024]{1,0:T(8,128)(2,1)S(1)} %get-tuple-element.37.us_ref, bf16[2048,1024]{1,0:T(8,128)(2,1)S(1)} %get-tuple-element.38.vs_ref, bf16[8,2,256,128]{3,2,1,0:T(8,128)(2,1)S(1)} %get-tuple-element.44.x_ref, ...), custom_call_target="tpu_custom_call" | custom-call | flops 8589934592 | bytes 8388608 | tf_op jit(solution)/shard_map/pallas_call | solution.py:480
  36.1 0.0 collective-permute-done.6
  36.2 1.4 %collective-permute-done.4 = f16[272,256]{1,0:T(8,128)(2,1)S(1)} collective-permute-done((f16[272,256]{1,0:T(8,128)(2,1)S(1)}, f16[272,256]{1,0:T(8,128)(2,1)S(1)}, u32[]{:S(2)}, u32[]{:S(2)}) %collective-permute-start.4) | collective-permute-done | bytes 139296 | tf_op jit(solution)/shard_map/ppermute | solution.py:521
  37.6 0.2 shard_map.99
  37.9 2.8 %collective-permute-start.9 = (f16[144,256]{1,0:T(8,128)(2,1)S(1)}, f16[144,256]{1,0:T(8,128)(2,1)S(1)}, u32[]{:S(2)}, u32[]{:S(2)}) collective-permute-start(f16[144,256]{1,0:T(8,128)(2,1)S(1)} %get-tuple-element.77), channel_id=1, source_target_pairs={{0,96},{8,104},{16,112},{24,120},{32,0},{40,8},{48,16},{56,24},{64... | collective-permute-start | bytes 221192 | tf_op jit(solution)/shard_map/ppermute | solution.py:521
  40.7 0.4 collective-permute-start.8
  41.0 0.7 collective-permute-start.7
  41.7 0.4 collective-permute-done.9
  42.1 3.4 %collective-permute-done.8 = f16[144,256]{1,0:T(8,128)(2,1)S(1)} collective-permute-done((f16[144,256]{1,0:T(8,128)(2,1)S(1)}, f16[144,256]{1,0:T(8,128)(2,1)S(1)}, u32[]{:S(2)}, u32[]{:S(2)}) %collective-permute-start.8) | collective-permute-done | bytes 73760 | tf_op jit(solution)/shard_map/ppermute | solution.py:521
  45.5 1.9 %collective-permute-done.7 = f16[144,256]{1,0:T(8,128)(2,1)S(1)} collective-permute-done((f16[144,256]{1,0:T(8,128)(2,1)S(1)}, f16[144,256]{1,0:T(8,128)(2,1)S(1)}, u32[]{:S(2)}, u32[]{:S(2)}) %collective-permute-start.7) | collective-permute-done | bytes 73760 | tf_op jit(solution)/shard_map/ppermute | solution.py:521
  47.4 0.7 shard_map.100
  48.0 0.1 convert.17
  48.1 0.1 slice_bitcast_fusion.5
  48.2 0.1 collective-permute-start.12
  48.3 0.8 collective-permute-start.11
  49.1 0.6 collective-permute-start.10
  49.8 2.4 %collective-permute-done.12 = f16[272,256]{1,0:T(8,128)(2,1)S(1)} collective-permute-done((f16[272,256]{1,0:T(8,128)(2,1)S(1)}, f16[272,256]{1,0:T(8,128)(2,1)S(1)}, u32[]{:S(2)}, u32[]{:S(2)}) %collective-permute-start.12) | collective-permute-done | bytes 139296 | tf_op jit(solution)/shard_map/ppermute | solution.py:521
  52.2 1.6 %collective-permute-done.11 = f16[272,256]{1,0:T(8,128)(2,1)S(1)} collective-permute-done((f16[272,256]{1,0:T(8,128)(2,1)S(1)}, f16[272,256]{1,0:T(8,128)(2,1)S(1)}, u32[]{:S(2)}, u32[]{:S(2)}) %collective-permute-start.11) | collective-permute-done | bytes 139296 | tf_op jit(solution)/shard_map/ppermute | solution.py:521
  53.9 1.8 %collective-permute-done.10 = f16[272,256]{1,0:T(8,128)(2,1)S(1)} collective-permute-done((f16[272,256]{1,0:T(8,128)(2,1)S(1)}, f16[272,256]{1,0:T(8,128)(2,1)S(1)}, u32[]{:S(2)}, u32[]{:S(2)}) %collective-permute-start.10) | collective-permute-done | bytes 139296 | tf_op jit(solution)/shard_map/ppermute | solution.py:521
  55.7 4.3 %shard_map.101 = (bf16[4,2,2,256,128]{4,3,2,1,0:T(8,128)(2,1)S(1)}, bf16[16,128,1024]{2,1,0:T(8,128)(2,1)S(1)}, bf16[16,128,1024]{2,1,0:T(8,128)(2,1)S(1)}, f32[16,1024]{1,0:T(8,128)S(1)}) custom-call(bf16[2048,1024]{1,0:T(8,128)(2,1)S(1)} %get-tuple-element.37.us_ref, bf16[2048,1024]{1,0:T(8,128)(2,1)S(1)} %get-tuple-element.38.vs_ref, ...), custom_call_target="tpu_custom_call" | custom-call | tf_op jit(solution)/shard_map/pallas_call | solution.py:480
  60.0 0.1 slice_bitcast_fusion.1
  60.1 2.5 %collective-permute-start.15 = (bf16[2,2,256,128]{3,2,1,0:T(8,128)(2,1)S(1)}, bf16[2,2,256,128]{3,2,1,0:T(8,128)(2,1)S(1)}, u32[]{:S(2)}, u32[]{:S(2)}) collective-permute-start(bf16[2,2,256,128]{3,2,1,0:T(8,128)(2,1)S(1)} %get-tuple-element.67), channel_id=1, source_target_pairs={{0,6},{1,7},{2,0},{3,1},{4,2},{5,3},{6,4},{7,5},{8,14},{9,15},{10,... | collective-permute-start | bytes 786440 | tf_op jit(solution)/shard_map/ppermute | solution.py:613
  62.7 0.1 collective-permute-start.14
  62.8 0.6 collective-permute-start.13
  63.3 9.5 %shard_map.102 = (bf16[2048,1024]{1,0:T(8,128)(2,1)}, bf16[2048,1024]{1,0:T(8,128)(2,1)}, bf16[2048,1024]{1,0:T(8,128)(2,1)S(1)}) custom-call(bf16[2048,1024]{1,0:T(8,128)(2,1)S(1)} %get-tuple-element.37.us_ref, bf16[2048,1024]{1,0:T(8,128)(2,1)S(1)} %get-tuple-element.38.vs_ref, bf16[16,128,1024]{2,1,0:T(8,128)(2,1)S(1)} %get-tuple-element.53.start_ref, ...), custom_call_target="tpu_custom_call" | custom-call | flops 17179869184 | bytes 8388608 | tf_op jit(solution)/shard_map/pallas_call | solution.py:480
  72.9 1.6 %shard_map.103 = (f32[16,1024]{1,0:T(8,128)S(1)}, f32[16,16]{1,0:T(8,128)S(1)}) custom-call(bf16[2048,1024]{1,0:T(8,128)(2,1)S(1)} %get-tuple-element.60.diff_ref, f32[16,1024]{1,0:T(8,128)S(1)} %get-tuple-element.61.total_ref, bf16[1024,128]{1,0:T(8,128)(2,1)S(1)} %get-tuple-element.62.of_ref), custom_call_target="tpu_custom_call" | custom-call | tf_op jit(solution)/shard_map/pallas_call | solution.py:480
  74.5 0.0 collective-permute-done.14.r2
  74.5 1.5 %collective-permute-done.13.r1 = bf16[2,2,256,128]{3,2,1,0:T(8,128)(2,1)S(1)} collective-permute-done((bf16[2,2,256,128]{3,2,1,0:T(8,128)(2,1)S(1)}, bf16[2,2,256,128]{3,2,1,0:T(8,128)(2,1)S(1)}, u32[]{:S(2)}, u32[]{:S(2)}) %collective-permute-start.13) | collective-permute-done | bytes 262176 | tf_op jit(solution)/shard_map/ppermute | solution.py:613
  76.0 3.2 %collective-permute-start.16 = (bf16[4,2,256,128]{3,2,1,0:T(8,128)(2,1)S(1)}, bf16[4,2,256,128]{3,2,1,0:T(8,128)(2,1)S(1)}, u32[]{:S(2)}, u32[]{:S(2)}) collective-permute-start(bf16[4,2,256,128]{3,2,1,0:T(8,128)(2,1)S(1)} %shard_map.104), channel_id=1, source_target_pairs={{0,1},{1,0},{2,3},{3,2},{4,5},{5,4},{6,7},{7,6},{8,9},{9,8},{10,11... | collective-permute-start | bytes 1572872 | tf_op jit(solution)/shard_map/ppermute | solution.py:633
  79.2 2.3 %shard_map.105.after_hbm = f32[16,2048]{1,0:T(8,128)} custom-call(bf16[2048,1024]{1,0:T(8,128)(2,1)S(1)} %get-tuple-element.60.diff_ref, f32[16,16]{1,0:T(8,128)S(1)} %get-tuple-element.64.heads_ref, bf16[1024,128]{1,0:T(8,128)(2,1)S(1)} %get-tuple-element.62.of_ref, f32[16,1024]{1,0:T(8,128)S(1)} %get-tuple-element.63.after_hbm.first_ref), custom_call_target="tpu_custom_call" | custom-call | flops 2147483648 | bytes 4194304 | tf_op jit(solution)/shard_map/pallas_call | solution.py:480
  81.4 1.1 %shard_map.106 = (bf16[256,1024]{1,0:T(8,128)(2,1)}, bf16[256,1024]{1,0:T(8,128)(2,1)}) custom-call(bf16[2,2,256,128]{3,2,1,0:T(8,128)(2,1)S(1)} %get-tuple-element.70.r0, bf16[2,2,256,128]{3,2,1,0:T(8,128)(2,1)S(1)} %collective-permute-done.13.r1, bf16[2,2,256,128]{3,2,1,0:T(8,128)(2,1)S(1)} %collective-permute-done.14.r2, ...), custom_call_target="tpu_custom_call" | custom-call | tf_op jit(solution)/shard_map/pallas_call | solution.py:480
  (18 shorter events, 0.3 us)
Async XLA Ops:
  1.8 15.1 %collective-permute-start.1 = (bf16[2,2,256,128]{3,2,1,0:T(8,128)(2,1)S(1)}, bf16[2,2,256,128]{3,2,1,0:T(8,128)(2,1)S(1)}, u32[]{:S(2)}, u32[]{:S(2)}) collective-permute-start(bf16[2,2,256,128]{3,2,1,0:T(8,128)(2,1)S(1)} %get-tuple-element.39.s2), channel_id=1, source_target_pairs={{0,4},{1,5},{2,6},{3,7},{4,0},{5,1},{6,2},{7,3},{8,12},{9,13},{10,... | collective-permute-start | bytes 786440 | tf_op jit(solution)/shard_map/ppermute | solution.py:544
  7.6 10.8 %collective-permute-start = (bf16[2,2,256,128]{3,2,1,0:T(8,128)(2,1)S(1)}, bf16[2,2,256,128]{3,2,1,0:T(8,128)(2,1)S(1)}, u32[]{:S(2)}, u32[]{:S(2)}) collective-permute-start(bf16[2,2,256,128]{3,2,1,0:T(8,128)(2,1)S(1)} %get-tuple-element.41), channel_id=1, source_target_pairs={{0,2},{1,3},{2,4},{3,5},{4,6},{5,7},{6,0},{7,1},{8,10},{9,11},{10,... | collective-permute-start | bytes 786440 | tf_op jit(solution)/shard_map/ppermute | solution.py:548
  8.4 10.0 %collective-permute-start.2 = (bf16[2,2,256,128]{3,2,1,0:T(8,128)(2,1)S(1)}, bf16[2,2,256,128]{3,2,1,0:T(8,128)(2,1)S(1)}, u32[]{:S(2)}, u32[]{:S(2)}) collective-permute-start(bf16[2,2,256,128]{3,2,1,0:T(8,128)(2,1)S(1)} %get-tuple-element.42), channel_id=1, source_target_pairs={{0,6},{1,7},{2,0},{3,1},{4,2},{5,3},{6,4},{7,5},{8,14},{9,15},{10,... | collective-permute-start | bytes 786440 | tf_op jit(solution)/shard_map/ppermute | solution.py:548
  18.5 3.1 %collective-permute-start.3 = (bf16[4,2,256,128]{3,2,1,0:T(8,128)(2,1)S(1)}, bf16[4,2,256,128]{3,2,1,0:T(8,128)(2,1)S(1)}, u32[]{:S(2)}, u32[]{:S(2)}) collective-permute-start(bf16[4,2,256,128]{3,2,1,0:T(8,128)(2,1)S(1)} %shard_map.95), channel_id=1, source_target_pairs={{0,1},{1,0},{2,3},{3,2},{4,5},{5,4},{6,7},{7,6},{8,9},{9,8},{10,11... | collective-permute-start | bytes 1572872 | tf_op jit(solution)/shard_map/ppermute | solution.py:566
  25.0 11.1 %collective-permute-start.6 = (f16[272,256]{1,0:T(8,128)(2,1)S(1)}, f16[272,256]{1,0:T(8,128)(2,1)S(1)}, u32[]{:S(2)}, u32[]{:S(2)}) collective-permute-start(f16[272,256]{1,0:T(8,128)(2,1)S(1)} %get-tuple-element.74), channel_id=1, source_target_pairs={{0,24},{8,0},{16,8},{24,16},{32,56},{40,32},{48,40},{56,48},{64,88... | collective-permute-start | bytes 417800 | tf_op jit(solution)/shard_map/ppermute | solution.py:521
  27.5 8.7 %collective-permute-start.5 = (f16[272,256]{1,0:T(8,128)(2,1)S(1)}, f16[272,256]{1,0:T(8,128)(2,1)S(1)}, u32[]{:S(2)}, u32[]{:S(2)}) collective-permute-start(f16[272,256]{1,0:T(8,128)(2,1)S(1)} %get-tuple-element.75), channel_id=1, source_target_pairs={{0,16},{8,24},{16,0},{24,8},{32,48},{40,56},{48,32},{56,40},{64,80... | collective-permute-start | bytes 417800 | tf_op jit(solution)/shard_map/ppermute | solution.py:521
  28.0 9.6 %collective-permute-start.4 = (f16[272,256]{1,0:T(8,128)(2,1)S(1)}, f16[272,256]{1,0:T(8,128)(2,1)S(1)}, u32[]{:S(2)}, u32[]{:S(2)}) collective-permute-start(f16[272,256]{1,0:T(8,128)(2,1)S(1)} %get-tuple-element.76), channel_id=1, source_target_pairs={{0,8},{8,16},{16,24},{24,0},{32,40},{40,48},{48,56},{56,32},{64,72... | collective-permute-start | bytes 417800 | tf_op jit(solution)/shard_map/ppermute | solution.py:521
  37.9 4.2 %collective-permute-start.9 = (f16[144,256]{1,0:T(8,128)(2,1)S(1)}, f16[144,256]{1,0:T(8,128)(2,1)S(1)}, u32[]{:S(2)}, u32[]{:S(2)}) collective-permute-start(f16[144,256]{1,0:T(8,128)(2,1)S(1)} %get-tuple-element.77), channel_id=1, source_target_pairs={{0,96},{8,104},{16,112},{24,120},{32,0},{40,8},{48,16},{56,24},{64... | collective-permute-start | bytes 221192 | tf_op jit(solution)/shard_map/ppermute | solution.py:521
  40.7 4.8 %collective-permute-start.8 = (f16[144,256]{1,0:T(8,128)(2,1)S(1)}, f16[144,256]{1,0:T(8,128)(2,1)S(1)}, u32[]{:S(2)}, u32[]{:S(2)}) collective-permute-start(f16[144,256]{1,0:T(8,128)(2,1)S(1)} %get-tuple-element.78), channel_id=1, source_target_pairs={{0,64},{8,72},{16,80},{24,88},{32,96},{40,104},{48,112},{56,120},{... | collective-permute-start | bytes 221192 | tf_op jit(solution)/shard_map/ppermute | solution.py:521
  41.0 6.3 %collective-permute-start.7 = (f16[144,256]{1,0:T(8,128)(2,1)S(1)}, f16[144,256]{1,0:T(8,128)(2,1)S(1)}, u32[]{:S(2)}, u32[]{:S(2)}) collective-permute-start(f16[144,256]{1,0:T(8,128)(2,1)S(1)} %get-tuple-element.79), channel_id=1, source_target_pairs={{0,32},{8,40},{16,48},{24,56},{32,64},{40,72},{48,80},{56,88},{64,... | collective-permute-start | bytes 221192 | tf_op jit(solution)/shard_map/ppermute | solution.py:521
  48.2 4.0 %collective-permute-start.12 = (f16[272,256]{1,0:T(8,128)(2,1)S(1)}, f16[272,256]{1,0:T(8,128)(2,1)S(1)}, u32[]{:S(2)}, u32[]{:S(2)}) collective-permute-start(f16[272,256]{1,0:T(8,128)(2,1)S(1)} %get-tuple-element.71), channel_id=1, source_target_pairs={{0,24},{8,0},{16,8},{24,16},{32,56},{40,32},{48,40},{56,48},{64,88... | collective-permute-start | bytes 417800 | tf_op jit(solution)/shard_map/ppermute | solution.py:521
  48.3 5.6 %collective-permute-start.11 = (f16[272,256]{1,0:T(8,128)(2,1)S(1)}, f16[272,256]{1,0:T(8,128)(2,1)S(1)}, u32[]{:S(2)}, u32[]{:S(2)}) collective-permute-start(f16[272,256]{1,0:T(8,128)(2,1)S(1)} %get-tuple-element.72), channel_id=1, source_target_pairs={{0,16},{8,24},{16,0},{24,8},{32,48},{40,56},{48,32},{56,40},{64,80... | collective-permute-start | bytes 417800 | tf_op jit(solution)/shard_map/ppermute | solution.py:521
  49.1 6.6 %collective-permute-start.10 = (f16[272,256]{1,0:T(8,128)(2,1)S(1)}, f16[272,256]{1,0:T(8,128)(2,1)S(1)}, u32[]{:S(2)}, u32[]{:S(2)}) collective-permute-start(f16[272,256]{1,0:T(8,128)(2,1)S(1)} %get-tuple-element.73), channel_id=1, source_target_pairs={{0,8},{8,16},{16,24},{24,0},{32,40},{40,48},{48,56},{56,32},{64,72... | collective-permute-start | bytes 417800 | tf_op jit(solution)/shard_map/ppermute | solution.py:521
  60.1 14.3 %collective-permute-start.15 = (bf16[2,2,256,128]{3,2,1,0:T(8,128)(2,1)S(1)}, bf16[2,2,256,128]{3,2,1,0:T(8,128)(2,1)S(1)}, u32[]{:S(2)}, u32[]{:S(2)}) collective-permute-start(bf16[2,2,256,128]{3,2,1,0:T(8,128)(2,1)S(1)} %get-tuple-element.67), channel_id=1, source_target_pairs={{0,6},{1,7},{2,0},{3,1},{4,2},{5,3},{6,4},{7,5},{8,14},{9,15},{10,... | collective-permute-start | bytes 786440 | tf_op jit(solution)/shard_map/ppermute | solution.py:613
  62.7 11.8 %collective-permute-start.14 = (bf16[2,2,256,128]{3,2,1,0:T(8,128)(2,1)S(1)}, bf16[2,2,256,128]{3,2,1,0:T(8,128)(2,1)S(1)}, u32[]{:S(2)}, u32[]{:S(2)}) collective-permute-start(bf16[2,2,256,128]{3,2,1,0:T(8,128)(2,1)S(1)} %get-tuple-element.68), channel_id=1, source_target_pairs={{0,4},{1,5},{2,6},{3,7},{4,0},{5,1},{6,2},{7,3},{8,12},{9,13},{10,... | collective-permute-start | bytes 786440 | tf_op jit(solution)/shard_map/ppermute | solution.py:613
  62.8 13.2 %collective-permute-start.13 = (bf16[2,2,256,128]{3,2,1,0:T(8,128)(2,1)S(1)}, bf16[2,2,256,128]{3,2,1,0:T(8,128)(2,1)S(1)}, u32[]{:S(2)}, u32[]{:S(2)}) collective-permute-start(bf16[2,2,256,128]{3,2,1,0:T(8,128)(2,1)S(1)} %get-tuple-element.69), channel_id=1, source_target_pairs={{0,2},{1,3},{2,4},{3,5},{4,6},{5,7},{6,0},{7,1},{8,10},{9,11},{10,... | collective-permute-start | bytes 786440 | tf_op jit(solution)/shard_map/ppermute | solution.py:613
  76.0 5.4 %collective-permute-start.16 = (bf16[4,2,256,128]{3,2,1,0:T(8,128)(2,1)S(1)}, bf16[4,2,256,128]{3,2,1,0:T(8,128)(2,1)S(1)}, u32[]{:S(2)}, u32[]{:S(2)}) collective-permute-start(bf16[4,2,256,128]{3,2,1,0:T(8,128)(2,1)S(1)} %shard_map.104), channel_id=1, source_target_pairs={{0,1},{1,0},{2,3},{3,2},{4,5},{5,4},{6,7},{7,6},{8,9},{9,8},{10,11... | collective-permute-start | bytes 1572872 | tf_op jit(solution)/shard_map/ppermute | solution.py:633

commit v4 on v3

--- a/solution.py
+++ b/solution.py
@@ -390,7 +390,7 @@
             copy.start()
         return carry
 
-    lax.fori_loop(0, PIECES, piece, 0, unroll=2)
+    lax.fori_loop(0, PIECES, piece, 0, unroll=4)
     for j in range(PIECES - outs, PIECES):
         for copy in writes(j):
             copy.wait()

time: 83 us -> 82.3 us (level)
  transfers between devices with their start and end apart: 17 -> 17, of which waited for: 10 -> 10; matrix products, arithmetic and copies ran while one was open for 0% -> 0% of each run, Pallas kernels for 35% -> 34%
where the time goes in v4:
time: 82.3 us; the launch traced here: 82 us
  Pallas kernels  38.8 us (47%)
  starting transfers between devices  23.4 us (28%)
  waiting for transfers between devices  18.1 us (22%)
  between operations  1.02 us (1%)
    pallas_call x15, Pallas kernels, call(): pl.pallas_call(kernel, out_shape=outs, in_specs=specs, out_specs=out_spec...  38.8 us
    ppermute x9, waiting for transfers between devices, send(): return lax.ppermute(a.astype(jnp.float16), 'ctx', pairs).astype(F32)  12.9 us
    ppermute x9, starting transfers between devices, send(): return lax.ppermute(a.astype(jnp.float16), 'ctx', pairs).astype(F32)  8.98 us
    ppermute x1, starting transfers between devices, body(): r2 = lax.ppermute(s2, 'head', along_z(2))  4.51 us
    ppermute x2, starting transfers between devices, body(): other = lax.ppermute(other, 'head', OTHER_CORE)  3.99 us
    ppermute x3, starting transfers between devices, body(): lax.ppermute(grads[d], 'head', along_z(d))  3.21 us
    ppermute x3, waiting for transfers between devices, body(): lax.ppermute(grads[d], 'head', along_z(d))  2.21 us
    ppermute x1, starting transfers between devices, body(): lax.ppermute(s3, 'head', along_z(3))  1.94 us
  transfers between devices with their start and end apart: 17, of which 10 were waited for; matrix products, arithmetic and copies ran while one was open for 0% of the time, Pallas kernels for 34%

profile of v4, /device:TPU:1, one launch (start us, length us, event | category | flops | bytes accessed | tf_op | source)
XLA Modules:
  0.0 82.0 jit_solution(18327493779963144485)
XLA Ops:
  0.6 1.2 %shard_map.92 = (bf16[2,2,256,128]{3,2,1,0:T(8,128)(2,1)S(1)}, f32[16,2048]{1,0:T(8,128)S(1)}) custom-call(bf16[256,1024]{1,0:T(8,128)(2,1)} %in_hbm.3, bf16[256,1024]{1,0:T(8,128)(2,1)} %out_hbm.3, f32[16,2048]{1,0:T(8,128)} %ld_hbm.1), custom_call_target="tpu_custom_call" | custom-call | tf_op jit(solution)/shard_map/pallas_call | solution.py:480
  1.8 4.5 %collective-permute-start.1 = (bf16[2,2,256,128]{3,2,1,0:T(8,128)(2,1)S(1)}, bf16[2,2,256,128]{3,2,1,0:T(8,128)(2,1)S(1)}, u32[]{:S(2)}, u32[]{:S(2)}) collective-permute-start(bf16[2,2,256,128]{3,2,1,0:T(8,128)(2,1)S(1)} %get-tuple-element.39.s2), channel_id=1, source_target_pairs={{0,4},{1,5},{2,6},{3,7},{4,0},{5,1},{6,2},{7,3},{8,12},{9,13},{10,... | collective-permute-start | bytes 786440 | tf_op jit(solution)/shard_map/ppermute | solution.py:544
  6.3 1.3 %shard_map.94 = (bf16[2,2,256,128]{3,2,1,0:T(8,128)(2,1)S(1)}, bf16[2,2,256,128]{3,2,1,0:T(8,128)(2,1)S(1)}, bf16[2,2,256,128]{3,2,1,0:T(8,128)(2,1)S(1)}) custom-call(bf16[256,1024]{1,0:T(8,128)(2,1)} %in_hbm.3, bf16[256,1024]{1,0:T(8,128)(2,1)} %out_hbm.3, bf16[2,2,256,128]{3,2,1,0:T(8,128)(2,1)S(1)} %get-tuple-element.39.s2), custom_call_target="tpu_custom_call" | custom-call | tf_op jit(solution)/shard_map/pallas_call | solution.py:480
  7.6 0.8 collective-permute-start
  8.4 1.9 %collective-permute-start.2 = (bf16[2,2,256,128]{3,2,1,0:T(8,128)(2,1)S(1)}, bf16[2,2,256,128]{3,2,1,0:T(8,128)(2,1)S(1)}, u32[]{:S(2)}, u32[]{:S(2)}) collective-permute-start(bf16[2,2,256,128]{3,2,1,0:T(8,128)(2,1)S(1)} %get-tuple-element.42), channel_id=1, source_target_pairs={{0,6},{1,7},{2,0},{3,1},{4,2},{5,3},{6,4},{7,5},{8,14},{9,15},{10,... | collective-permute-start | bytes 786440 | tf_op jit(solution)/shard_map/ppermute | solution.py:548
  10.4 6.6 %shard_map.93 = (bf16[2048,1024]{1,0:T(8,128)(2,1)S(1)}, bf16[2048,1024]{1,0:T(8,128)(2,1)S(1)}, bf16[16,32,128]{2,1,0:T(8,128)(2,1)S(1)}, bf16[16,32,128]{2,1,0:T(8,128)(2,1)S(1)}, f32[16,1024]{1,0:T(8,128)S(1)}) custom-call(bf16[2048,1024]{1,0:T(8,128)(2,1)} %sig_hbm.1, bf16[2048,1024]{1,0:T(8,128)(2,1)} %cot_hbm.1, f32[16,2048]{1,0:T(8,128)S(1)} %get-tuple-element.36.ld_ref), custom_call_target="tpu_custom_call" | custom-call | flops 8589934592 | bytes 8388608 | tf_op jit(solution)/shard_map/pallas_call | solution.py:480
  16.9 0.0 collective-permute-done.1.r2
  16.9 1.5 %collective-permute-done.r1 = bf16[2,2,256,128]{3,2,1,0:T(8,128)(2,1)S(1)} collective-permute-done((bf16[2,2,256,128]{3,2,1,0:T(8,128)(2,1)S(1)}, bf16[2,2,256,128]{3,2,1,0:T(8,128)(2,1)S(1)}, u32[]{:S(2)}, u32[]{:S(2)}) %collective-permute-start) | collective-permute-done | bytes 262176 | tf_op jit(solution)/shard_map/ppermute | solution.py:548
  18.5 1.5 %collective-permute-start.3 = (bf16[4,2,256,128]{3,2,1,0:T(8,128)(2,1)S(1)}, bf16[4,2,256,128]{3,2,1,0:T(8,128)(2,1)S(1)}, u32[]{:S(2)}, u32[]{:S(2)}) collective-permute-start(bf16[4,2,256,128]{3,2,1,0:T(8,128)(2,1)S(1)} %shard_map.95), channel_id=1, source_target_pairs={{0,1},{1,0},{2,3},{3,2},{4,5},{5,4},{6,7},{7,6},{8,9},{9,8},{10,11... | collective-permute-start | bytes 1572872 | tf_op jit(solution)/shard_map/ppermute | solution.py:566
  20.0 1.5 %collective-permute-done.3.other = bf16[4,2,256,128]{3,2,1,0:T(8,128)(2,1)S(1)} collective-permute-done((bf16[4,2,256,128]{3,2,1,0:T(8,128)(2,1)S(1)}, bf16[4,2,256,128]{3,2,1,0:T(8,128)(2,1)S(1)}, u32[]{:S(2)}, u32[]{:S(2)}) %collective-permute-start.3) | collective-permute-done | bytes 524320 | tf_op jit(solution)/shard_map/ppermute | solution.py:566
  21.6 3.2 %shard_map.96 = (bf16[8,2,256,128]{3,2,1,0:T(8,128)(2,1)S(1)}, bf16[2,128,2048]{2,1,0:T(8,128)(2,1)S(1)}, bf16[17,128,1024]{2,1,0:T(8,128)(2,1)S(1)}, bf16[16,12...) custom-call(bf16[2048,1024]{1,0:T(8,128)(2,1)S(1)} %get-tuple-element.37.us_ref, ...), custom_call_target="tpu_custom_call" | custom-call | tf_op jit(solution)/shard_map/pallas_call | solution.py:480
  24.8 0.1 convert.15
  24.9 0.1 slice_bitcast_fusion.8
  25.0 2.5 %collective-permute-start.6 = (f16[272,256]{1,0:T(8,128)(2,1)S(1)}, f16[272,256]{1,0:T(8,128)(2,1)S(1)}, u32[]{:S(2)}, u32[]{:S(2)}) collective-permute-start(f16[272,256]{1,0:T(8,128)(2,1)S(1)} %get-tuple-element.74), channel_id=1, source_target_pairs={{0,24},{8,0},{16,8},{24,16},{32,56},{40,32},{48,40},{56,48},{64,88... | collective-permute-start | bytes 417800 | tf_op jit(solution)/shard_map/ppermute | solution.py:521
  27.5 0.5 collective-permute-start.5
  28.0 0.6 collective-permute-start.4
  28.6 0.9 %shard_map.97 = (bf16[17,128,1024]{2,1,0:T(8,128)(2,1)S(1)}, bf16[16,128,1024]{2,1,0:T(8,128)(2,1)S(1)}, f32[272,256]{1,0:T(8,128)S(1)}) custom-call(bf16[2048,1024]{1,0:T(8,128)(2,1)S(1)} %get-tuple-element.37.us_ref, bf16[2048,1024]{1,0:T(8,128)(2,1)S(1)} %get-tuple-element.38.vs_ref, ...), custom_call_target="tpu_custom_call", output_to_operand_aliasing={{0}: (4, {}), {1}: (5, {})} | custom-call | flops 2147483648 | bytes 8388608 | tf_op jit(solution)/shard_map/pallas_call | solution.py:480
  29.5 6.6 %shard_map.98 = (f32[16,2,128,128]{3,2,1,0:T(8,128)S(1)}, bf16[1024,128]{1,0:T(8,128)(2,1)S(1)}) custom-call(bf16[2048,1024]{1,0:T(8,128)(2,1)S(1)} %get-tuple-element.37.us_ref, bf16[2048,1024]{1,0:T(8,128)(2,1)S(1)} %get-tuple-element.38.vs_ref, bf16[8,2,256,128]{3,2,1,0:T(8,128)(2,1)S(1)} %get-tuple-element.44.x_ref, ...), custom_call_target="tpu_custom_call" | custom-call | flops 8589934592 | bytes 8388608 | tf_op jit(solution)/shard_map/pallas_call | solution.py:480
  36.1 0.0 collective-permute-done.6
  36.2 1.4 %collective-permute-done.4 = f16[272,256]{1,0:T(8,128)(2,1)S(1)} collective-permute-done((f16[272,256]{1,0:T(8,128)(2,1)S(1)}, f16[272,256]{1,0:T(8,128)(2,1)S(1)}, u32[]{:S(2)}, u32[]{:S(2)}) %collective-permute-start.4) | collective-permute-done | bytes 139296 | tf_op jit(solution)/shard_map/ppermute | solution.py:521
  37.6 0.2 shard_map.99
  37.9 2.8 %collective-permute-start.9 = (f16[144,256]{1,0:T(8,128)(2,1)S(1)}, f16[144,256]{1,0:T(8,128)(2,1)S(1)}, u32[]{:S(2)}, u32[]{:S(2)}) collective-permute-start(f16[144,256]{1,0:T(8,128)(2,1)S(1)} %get-tuple-element.77), channel_id=1, source_target_pairs={{0,96},{8,104},{16,112},{24,120},{32,0},{40,8},{48,16},{56,24},{64... | collective-permute-start | bytes 221192 | tf_op jit(solution)/shard_map/ppermute | solution.py:521
  40.7 0.4 collective-permute-start.8
  41.0 0.7 collective-permute-start.7
  41.7 0.4 collective-permute-done.9
  42.1 3.4 %collective-permute-done.8 = f16[144,256]{1,0:T(8,128)(2,1)S(1)} collective-permute-done((f16[144,256]{1,0:T(8,128)(2,1)S(1)}, f16[144,256]{1,0:T(8,128)(2,1)S(1)}, u32[]{:S(2)}, u32[]{:S(2)}) %collective-permute-start.8) | collective-permute-done | bytes 73760 | tf_op jit(solution)/shard_map/ppermute | solution.py:521
  45.5 1.9 %collective-permute-done.7 = f16[144,256]{1,0:T(8,128)(2,1)S(1)} collective-permute-done((f16[144,256]{1,0:T(8,128)(2,1)S(1)}, f16[144,256]{1,0:T(8,128)(2,1)S(1)}, u32[]{:S(2)}, u32[]{:S(2)}) %collective-permute-start.7) | collective-permute-done | bytes 73760 | tf_op jit(solution)/shard_map/ppermute | solution.py:521
  47.4 0.7 shard_map.100
  48.0 0.1 convert.17
  48.1 0.1 slice_bitcast_fusion.5
  48.2 0.1 collective-permute-start.12
  48.3 0.8 %collective-permute-start.11 = (f16[272,256]{1,0:T(8,128)(2,1)S(1)}, f16[272,256]{1,0:T(8,128)(2,1)S(1)}, u32[]{:S(2)}, u32[]{:S(2)}) collective-permute-start(f16[272,256]{1,0:T(8,128)(2,1)S(1)} %get-tuple-element.72), channel_id=1, source_target_pairs={{0,16},{8,24},{16,0},{24,8},{32,48},{40,56},{48,32},{56,40},{64,80... | collective-permute-start | bytes 417800 | tf_op jit(solution)/shard_map/ppermute | solution.py:521
  49.1 0.6 collective-permute-start.10
  49.8 2.4 %collective-permute-done.12 = f16[272,256]{1,0:T(8,128)(2,1)S(1)} collective-permute-done((f16[272,256]{1,0:T(8,128)(2,1)S(1)}, f16[272,256]{1,0:T(8,128)(2,1)S(1)}, u32[]{:S(2)}, u32[]{:S(2)}) %collective-permute-start.12) | collective-permute-done | bytes 139296 | tf_op jit(solution)/shard_map/ppermute | solution.py:521
  52.2 1.6 %collective-permute-done.11 = f16[272,256]{1,0:T(8,128)(2,1)S(1)} collective-permute-done((f16[272,256]{1,0:T(8,128)(2,1)S(1)}, f16[272,256]{1,0:T(8,128)(2,1)S(1)}, u32[]{:S(2)}, u32[]{:S(2)}) %collective-permute-start.11) | collective-permute-done | bytes 139296 | tf_op jit(solution)/shard_map/ppermute | solution.py:521
  53.9 1.8 %collective-permute-done.10 = f16[272,256]{1,0:T(8,128)(2,1)S(1)} collective-permute-done((f16[272,256]{1,0:T(8,128)(2,1)S(1)}, f16[272,256]{1,0:T(8,128)(2,1)S(1)}, u32[]{:S(2)}, u32[]{:S(2)}) %collective-permute-start.10) | collective-permute-done | bytes 139296 | tf_op jit(solution)/shard_map/ppermute | solution.py:521
  55.7 4.3 %shard_map.101 = (bf16[4,2,2,256,128]{4,3,2,1,0:T(8,128)(2,1)S(1)}, bf16[16,128,1024]{2,1,0:T(8,128)(2,1)S(1)}, bf16[16,128,1024]{2,1,0:T(8,128)(2,1)S(1)}, f32[16,1024]{1,0:T(8,128)S(1)}) custom-call(bf16[2048,1024]{1,0:T(8,128)(2,1)S(1)} %get-tuple-element.37.us_ref, bf16[2048,1024]{1,0:T(8,128)(2,1)S(1)} %get-tuple-element.38.vs_ref, ...), custom_call_target="tpu_custom_call" | custom-call | tf_op jit(solution)/shard_map/pallas_call | solution.py:480
  60.0 0.1 slice_bitcast_fusion.1
  60.1 2.5 %collective-permute-start.15 = (bf16[2,2,256,128]{3,2,1,0:T(8,128)(2,1)S(1)}, bf16[2,2,256,128]{3,2,1,0:T(8,128)(2,1)S(1)}, u32[]{:S(2)}, u32[]{:S(2)}) collective-permute-start(bf16[2,2,256,128]{3,2,1,0:T(8,128)(2,1)S(1)} %get-tuple-element.67), channel_id=1, source_target_pairs={{0,6},{1,7},{2,0},{3,1},{4,2},{5,3},{6,4},{7,5},{8,14},{9,15},{10,... | collective-permute-start | bytes 786440 | tf_op jit(solution)/shard_map/ppermute | solution.py:613
  62.7 0.1 collective-permute-start.14
  62.8 0.6 collective-permute-start.13
  63.3 8.8 %shard_map.102 = (bf16[2048,1024]{1,0:T(8,128)(2,1)}, bf16[2048,1024]{1,0:T(8,128)(2,1)}, bf16[2048,1024]{1,0:T(8,128)(2,1)S(1)}) custom-call(bf16[2048,1024]{1,0:T(8,128)(2,1)S(1)} %get-tuple-element.37.us_ref, bf16[2048,1024]{1,0:T(8,128)(2,1)S(1)} %get-tuple-element.38.vs_ref, bf16[16,128,1024]{2,1,0:T(8,128)(2,1)S(1)} %get-tuple-element.53.start_ref, ...), custom_call_target="tpu_custom_call" | custom-call | flops 17179869184 | bytes 8388608 | tf_op jit(solution)/shard_map/pallas_call | solution.py:480
  72.2 1.6 %shard_map.103 = (f32[16,1024]{1,0:T(8,128)S(1)}, f32[16,16]{1,0:T(8,128)S(1)}) custom-call(bf16[2048,1024]{1,0:T(8,128)(2,1)S(1)} %get-tuple-element.60.diff_ref, f32[16,1024]{1,0:T(8,128)S(1)} %get-tuple-element.61.total_ref, bf16[1024,128]{1,0:T(8,128)(2,1)S(1)} %get-tuple-element.62.of_ref), custom_call_target="tpu_custom_call" | custom-call | tf_op jit(solution)/shard_map/pallas_call | solution.py:480
  73.8 0.0 collective-permute-done.14.r2
  73.8 2.2 %collective-permute-done.13.r1 = bf16[2,2,256,128]{3,2,1,0:T(8,128)(2,1)S(1)} collective-permute-done((bf16[2,2,256,128]{3,2,1,0:T(8,128)(2,1)S(1)}, bf16[2,2,256,128]{3,2,1,0:T(8,128)(2,1)S(1)}, u32[]{:S(2)}, u32[]{:S(2)}) %collective-permute-start.13) | collective-permute-done | bytes 262176 | tf_op jit(solution)/shard_map/ppermute | solution.py:613
  76.0 2.4 %collective-permute-start.16 = (bf16[4,2,256,128]{3,2,1,0:T(8,128)(2,1)S(1)}, bf16[4,2,256,128]{3,2,1,0:T(8,128)(2,1)S(1)}, u32[]{:S(2)}, u32[]{:S(2)}) collective-permute-start(bf16[4,2,256,128]{3,2,1,0:T(8,128)(2,1)S(1)} %shard_map.104), channel_id=1, source_target_pairs={{0,1},{1,0},{2,3},{3,2},{4,5},{5,4},{6,7},{7,6},{8,9},{9,8},{10,11... | collective-permute-start | bytes 1572872 | tf_op jit(solution)/shard_map/ppermute | solution.py:633
  78.5 2.3 %shard_map.105.after_hbm = f32[16,2048]{1,0:T(8,128)} custom-call(bf16[2048,1024]{1,0:T(8,128)(2,1)S(1)} %get-tuple-element.60.diff_ref, f32[16,16]{1,0:T(8,128)S(1)} %get-tuple-element.64.heads_ref, bf16[1024,128]{1,0:T(8,128)(2,1)S(1)} %get-tuple-element.62.of_ref, f32[16,1024]{1,0:T(8,128)S(1)} %get-tuple-element.63.after_hbm.first_ref), custom_call_target="tpu_custom_call" | custom-call | flops 2147483648 | bytes 4194304 | tf_op jit(solution)/shard_map/pallas_call | solution.py:480
  80.7 1.1 %shard_map.106 = (bf16[256,1024]{1,0:T(8,128)(2,1)}, bf16[256,1024]{1,0:T(8,128)(2,1)}) custom-call(bf16[2,2,256,128]{3,2,1,0:T(8,128)(2,1)S(1)} %get-tuple-element.70.r0, bf16[2,2,256,128]{3,2,1,0:T(8,128)(2,1)S(1)} %collective-permute-done.13.r1, bf16[2,2,256,128]{3,2,1,0:T(8,128)(2,1)S(1)} %collective-permute-done.14.r2, ...), custom_call_target="tpu_custom_call" | custom-call | tf_op jit(solution)/shard_map/pallas_call | solution.py:480
  (18 shorter events, 0.3 us)
Async XLA Ops:
  1.8 15.1 %collective-permute-start.1 = (bf16[2,2,256,128]{3,2,1,0:T(8,128)(2,1)S(1)}, bf16[2,2,256,128]{3,2,1,0:T(8,128)(2,1)S(1)}, u32[]{:S(2)}, u32[]{:S(2)}) collective-permute-start(bf16[2,2,256,128]{3,2,1,0:T(8,128)(2,1)S(1)} %get-tuple-element.39.s2), channel_id=1, source_target_pairs={{0,4},{1,5},{2,6},{3,7},{4,0},{5,1},{6,2},{7,3},{8,12},{9,13},{10,... | collective-permute-start | bytes 786440 | tf_op jit(solution)/shard_map/ppermute | solution.py:544
  7.6 10.8 %collective-permute-start = (bf16[2,2,256,128]{3,2,1,0:T(8,128)(2,1)S(1)}, bf16[2,2,256,128]{3,2,1,0:T(8,128)(2,1)S(1)}, u32[]{:S(2)}, u32[]{:S(2)}) collective-permute-start(bf16[2,2,256,128]{3,2,1,0:T(8,128)(2,1)S(1)} %get-tuple-element.41), channel_id=1, source_target_pairs={{0,2},{1,3},{2,4},{3,5},{4,6},{5,7},{6,0},{7,1},{8,10},{9,11},{10,... | collective-permute-start | bytes 786440 | tf_op jit(solution)/shard_map/ppermute | solution.py:548
  8.4 10.0 %collective-permute-start.2 = (bf16[2,2,256,128]{3,2,1,0:T(8,128)(2,1)S(1)}, bf16[2,2,256,128]{3,2,1,0:T(8,128)(2,1)S(1)}, u32[]{:S(2)}, u32[]{:S(2)}) collective-permute-start(bf16[2,2,256,128]{3,2,1,0:T(8,128)(2,1)S(1)} %get-tuple-element.42), channel_id=1, source_target_pairs={{0,6},{1,7},{2,0},{3,1},{4,2},{5,3},{6,4},{7,5},{8,14},{9,15},{10,... | collective-permute-start | bytes 786440 | tf_op jit(solution)/shard_map/ppermute | solution.py:548
  18.5 3.1 %collective-permute-start.3 = (bf16[4,2,256,128]{3,2,1,0:T(8,128)(2,1)S(1)}, bf16[4,2,256,128]{3,2,1,0:T(8,128)(2,1)S(1)}, u32[]{:S(2)}, u32[]{:S(2)}) collective-permute-start(bf16[4,2,256,128]{3,2,1,0:T(8,128)(2,1)S(1)} %shard_map.95), channel_id=1, source_target_pairs={{0,1},{1,0},{2,3},{3,2},{4,5},{5,4},{6,7},{7,6},{8,9},{9,8},{10,11... | collective-permute-start | bytes 1572872 | tf_op jit(solution)/shard_map/ppermute | solution.py:566
  25.0 11.1 %collective-permute-start.6 = (f16[272,256]{1,0:T(8,128)(2,1)S(1)}, f16[272,256]{1,0:T(8,128)(2,1)S(1)}, u32[]{:S(2)}, u32[]{:S(2)}) collective-permute-start(f16[272,256]{1,0:T(8,128)(2,1)S(1)} %get-tuple-element.74), channel_id=1, source_target_pairs={{0,24},{8,0},{16,8},{24,16},{32,56},{40,32},{48,40},{56,48},{64,88... | collective-permute-start | bytes 417800 | tf_op jit(solution)/shard_map/ppermute | solution.py:521
  27.5 8.7 %collective-permute-start.5 = (f16[272,256]{1,0:T(8,128)(2,1)S(1)}, f16[272,256]{1,0:T(8,128)(2,1)S(1)}, u32[]{:S(2)}, u32[]{:S(2)}) collective-permute-start(f16[272,256]{1,0:T(8,128)(2,1)S(1)} %get-tuple-element.75), channel_id=1, source_target_pairs={{0,16},{8,24},{16,0},{24,8},{32,48},{40,56},{48,32},{56,40},{64,80... | collective-permute-start | bytes 417800 | tf_op jit(solution)/shard_map/ppermute | solution.py:521
  28.0 9.6 %collective-permute-start.4 = (f16[272,256]{1,0:T(8,128)(2,1)S(1)}, f16[272,256]{1,0:T(8,128)(2,1)S(1)}, u32[]{:S(2)}, u32[]{:S(2)}) collective-permute-start(f16[272,256]{1,0:T(8,128)(2,1)S(1)} %get-tuple-element.76), channel_id=1, source_target_pairs={{0,8},{8,16},{16,24},{24,0},{32,40},{40,48},{48,56},{56,32},{64,72... | collective-permute-start | bytes 417800 | tf_op jit(solution)/shard_map/ppermute | solution.py:521
  37.9 4.2 %collective-permute-start.9 = (f16[144,256]{1,0:T(8,128)(2,1)S(1)}, f16[144,256]{1,0:T(8,128)(2,1)S(1)}, u32[]{:S(2)}, u32[]{:S(2)}) collective-permute-start(f16[144,256]{1,0:T(8,128)(2,1)S(1)} %get-tuple-element.77), channel_id=1, source_target_pairs={{0,96},{8,104},{16,112},{24,120},{32,0},{40,8},{48,16},{56,24},{64... | collective-permute-start | bytes 221192 | tf_op jit(solution)/shard_map/ppermute | solution.py:521
  40.7 4.8 %collective-permute-start.8 = (f16[144,256]{1,0:T(8,128)(2,1)S(1)}, f16[144,256]{1,0:T(8,128)(2,1)S(1)}, u32[]{:S(2)}, u32[]{:S(2)}) collective-permute-start(f16[144,256]{1,0:T(8,128)(2,1)S(1)} %get-tuple-element.78), channel_id=1, source_target_pairs={{0,64},{8,72},{16,80},{24,88},{32,96},{40,104},{48,112},{56,120},{... | collective-permute-start | bytes 221192 | tf_op jit(solution)/shard_map/ppermute | solution.py:521
  41.0 6.3 %collective-permute-start.7 = (f16[144,256]{1,0:T(8,128)(2,1)S(1)}, f16[144,256]{1,0:T(8,128)(2,1)S(1)}, u32[]{:S(2)}, u32[]{:S(2)}) collective-permute-start(f16[144,256]{1,0:T(8,128)(2,1)S(1)} %get-tuple-element.79), channel_id=1, source_target_pairs={{0,32},{8,40},{16,48},{24,56},{32,64},{40,72},{48,80},{56,88},{64,... | collective-permute-start | bytes 221192 | tf_op jit(solution)/shard_map/ppermute | solution.py:521
  48.2 4.0 %collective-permute-start.12 = (f16[272,256]{1,0:T(8,128)(2,1)S(1)}, f16[272,256]{1,0:T(8,128)(2,1)S(1)}, u32[]{:S(2)}, u32[]{:S(2)}) collective-permute-start(f16[272,256]{1,0:T(8,128)(2,1)S(1)} %get-tuple-element.71), channel_id=1, source_target_pairs={{0,24},{8,0},{16,8},{24,16},{32,56},{40,32},{48,40},{56,48},{64,88... | collective-permute-start | bytes 417800 | tf_op jit(solution)/shard_map/ppermute | solution.py:521
  48.3 5.6 %collective-permute-start.11 = (f16[272,256]{1,0:T(8,128)(2,1)S(1)}, f16[272,256]{1,0:T(8,128)(2,1)S(1)}, u32[]{:S(2)}, u32[]{:S(2)}) collective-permute-start(f16[272,256]{1,0:T(8,128)(2,1)S(1)} %get-tuple-element.72), channel_id=1, source_target_pairs={{0,16},{8,24},{16,0},{24,8},{32,48},{40,56},{48,32},{56,40},{64,80... | collective-permute-start | bytes 417800 | tf_op jit(solution)/shard_map/ppermute | solution.py:521
  49.1 6.6 %collective-permute-start.10 = (f16[272,256]{1,0:T(8,128)(2,1)S(1)}, f16[272,256]{1,0:T(8,128)(2,1)S(1)}, u32[]{:S(2)}, u32[]{:S(2)}) collective-permute-start(f16[272,256]{1,0:T(8,128)(2,1)S(1)} %get-tuple-element.73), channel_id=1, source_target_pairs={{0,8},{8,16},{16,24},{24,0},{32,40},{40,48},{48,56},{56,32},{64,72... | collective-permute-start | bytes 417800 | tf_op jit(solution)/shard_map/ppermute | solution.py:521
  60.1 13.6 %collective-permute-start.15 = (bf16[2,2,256,128]{3,2,1,0:T(8,128)(2,1)S(1)}, bf16[2,2,256,128]{3,2,1,0:T(8,128)(2,1)S(1)}, u32[]{:S(2)}, u32[]{:S(2)}) collective-permute-start(bf16[2,2,256,128]{3,2,1,0:T(8,128)(2,1)S(1)} %get-tuple-element.67), channel_id=1, source_target_pairs={{0,6},{1,7},{2,0},{3,1},{4,2},{5,3},{6,4},{7,5},{8,14},{9,15},{10,... | collective-permute-start | bytes 786440 | tf_op jit(solution)/shard_map/ppermute | solution.py:613
  62.7 11.1 %collective-permute-start.14 = (bf16[2,2,256,128]{3,2,1,0:T(8,128)(2,1)S(1)}, bf16[2,2,256,128]{3,2,1,0:T(8,128)(2,1)S(1)}, u32[]{:S(2)}, u32[]{:S(2)}) collective-permute-start(bf16[2,2,256,128]{3,2,1,0:T(8,128)(2,1)S(1)} %get-tuple-element.68), channel_id=1, source_target_pairs={{0,4},{1,5},{2,6},{3,7},{4,0},{5,1},{6,2},{7,3},{8,12},{9,13},{10,... | collective-permute-start | bytes 786440 | tf_op jit(solution)/shard_map/ppermute | solution.py:613
  62.8 13.2 %collective-permute-start.13 = (bf16[2,2,256,128]{3,2,1,0:T(8,128)(2,1)S(1)}, bf16[2,2,256,128]{3,2,1,0:T(8,128)(2,1)S(1)}, u32[]{:S(2)}, u32[]{:S(2)}) collective-permute-start(bf16[2,2,256,128]{3,2,1,0:T(8,128)(2,1)S(1)} %get-tuple-element.69), channel_id=1, source_target_pairs={{0,2},{1,3},{2,4},{3,5},{4,6},{5,7},{6,0},{7,1},{8,10},{9,11},{10,... | collective-permute-start | bytes 786440 | tf_op jit(solution)/shard_map/ppermute | solution.py:613
  76.0 4.7 %collective-permute-start.16 = (bf16[4,2,256,128]{3,2,1,0:T(8,128)(2,1)S(1)}, bf16[4,2,256,128]{3,2,1,0:T(8,128)(2,1)S(1)}, u32[]{:S(2)}, u32[]{:S(2)}) collective-permute-start(bf16[4,2,256,128]{3,2,1,0:T(8,128)(2,1)S(1)} %shard_map.104), channel_id=1, source_target_pairs={{0,1},{1,0},{2,3},{3,2},{4,5},{5,4},{6,7},{7,6},{8,9},{9,8},{10,11... | collective-permute-start | bytes 1572872 | tf_op jit(solution)/shard_map/ppermute | solution.py:633
